TPU v7x, 32 devices: a whole 2x2x4 slice. The times are simulated.
32 devices in a mesh: groups: 2 (over y), gx: 4 (over z), gy: 4 (over x, core).
Axes of the slice: x: 2, y: 2, z: 4, core: 2. Of those that a mesh axis runs over, the one named last changes fastest.
Arguments:
- velocity: float32 [4, 64, 1024], P('groups', 'gx', 'gy'), parts along dimension 0, may hold values from -6 to 6
- kernel_in: bfloat16 [64, 2, 3, 3], replicated, may hold values from -1.5 to 1.5
- bias_in: float32 [64], replicated, may hold values from -3 to 3
- kernel_mid: bfloat16 [64, 64, 3, 3], replicated, may hold values from -0.25 to 0.25
- bias_mid: float32 [64], replicated, may hold values from -3 to 3
- kernel_out: bfloat16 [12, 64, 3, 3], replicated, may hold values from -0.07470703 to 0.07470703
- bias_out: float32 [12], replicated, may hold values from -3 to 3
- cotangent: float32 [4, 64, 1024], P('groups', 'gx', 'gy'), parts along dimension 0, may hold values from -6 to 6
Outputs:
- new_velocity: float32 [4, 64, 1024], P('groups', 'gx', 'gy'), parts along dimension 0
- grad_velocity: float32 [4, 64, 1024], P('groups', 'gx', 'gy'), parts along dimension 0
- grad_kernel_in: float32 [128, 2, 3, 3], P('groups'), parts along dimension 0
- grad_bias_in: float32 [128], P('groups'), parts along dimension 0
- grad_kernel_mid: float32 [128, 64, 3, 3], P('groups'), parts along dimension 0
- grad_bias_mid: float32 [128], P('groups'), parts along dimension 0
- grad_kernel_out: float32 [24, 64, 3, 3], P('groups'), parts along dimension 0
- grad_bias_out: float32 [24], P('groups'), parts along dimension 0
There are 2 independent parts, one for each index of `groups`. A program takes and returns all parts, laid end to end along the dimension named above; an argument that names none is the same for every part. Nothing has to cross between parts.
All inputs are finite; a program needn't handle non-finite values.
Results may differ from a plain program's by a relative error of at most 0.017.
Values may be sent and summed in bfloat16 or wider, within the bound.
No kernel may reach another device: no remote copies, remote signals or barrier semaphores. Data moves between devices by JAX's collectives and lax.ppermute only.
A program may use at most 64 MiB of HBM per device.

v0:
```python
import math

import jax
import jax.numpy as jnp
from jax import lax
from jax.experimental import pallas as pl
from jax.experimental.pallas import tpu as pltpu
from jax.sharding import PartitionSpec as P

advection = 0.2
viscosity = 0.05
forcing_amp = 0.05
forcing_wave = 4
face_base = ((0.0, 0.5, 0.0, 0.0, 0.5, 0.0), (0.0, 0.0, 0.5, 0.5, 0.0, 0.0))
halo = 4
hid = 64
coef = 12
slot = 16
taps_x = [(a, b) for a in (0, 1) for b in (-1, 0, 1)]
taps_y = [(a, b) for a in (-1, 0, 1) for b in (0, 1)]
f32 = jnp.float32
bf16 = jnp.bfloat16


def shift(value, rows, cols):
    if rows:
        value = pltpu.roll(value, (-rows) % value.shape[-2], value.ndim - 2)
    if cols:
        value = pltpu.roll(value, (-cols) % value.shape[-1], value.ndim - 1)
    return value


def mm(lhs, rhs):
    return lax.dot_general(lhs, rhs, (((1,), (0,)), ((), ())), preferred_element_type=f32)


def mm_nt(lhs, rhs):
    return lax.dot_general(lhs, rhs, (((1,), (1,)), ((), ())), preferred_element_type=f32)


def sigma_of(linear):
    return 0.5 * jnp.tanh(0.5 * linear) + 0.5


def store_shifted(refs, at, value):
    rows = value.shape[0]
    for b in range(3):
        refs[b, at : at + rows, :] = shift(value, 0, b - 1).astype(refs.dtype)


def put_plane(planes, k, stride, value):
    for j in range(planes.shape[0]):
        planes[j, pl.ds(k, value.shape[0], stride=stride), :] = value[:, 128 * j : 128 * j + 128]


def take_plane(planes, k, count, stride):
    tiles = [planes[j, pl.ds(k, count, stride=stride), :] for j in range(planes.shape[0])]
    return jnp.concatenate(tiles, axis=1)


def take_rows(planes, at, size):
    return jnp.concatenate([planes[j, at : at + size, :] for j in range(planes.shape[0])], axis=1)


def put_rows(planes, at, value):
    for j in range(planes.shape[0]):
        planes[j, at : at + value.shape[0], :] = value[:, 128 * j : 128 * j + 128]


def faces(w0, w1):
    normal_x = 0.5 * (w0 + shift(w0, 1, 0))
    normal_y = 0.5 * (w1 + shift(w1, 0, 1))
    return normal_x, normal_y


def shifted_fields(w):
    table = {}
    for b in (-1, 0, 1):
        col = shift(w, 0, b)
        for a in (-1, 0, 1):
            table[a, b] = shift(col, a, 0)
    return table


def lane_sums(total):
    lanes = total.shape[1]
    part = total[:, :128]
    for k in range(1, lanes // 128):
        part = part + total[:, 128 * k : 128 * k + 128]
    return jnp.sum(part.T, axis=0, keepdims=True)


def backward_kernel(
    rows,
    cols,
    ext_ref,
    w_in_ref,
    w_mid_ref,
    w_mid_t_ref,
    w_out_t_ref,
    b_in_ref,
    b_mid_ref,
    pay_ref,
    act_two_ref,
    grad_one_ref,
    stage,
    state_in,
    head_in,
    act_one,
    slope_one,
    grad_two,
    acc_mid,
    acc_small,
    bias_acc,
):
    height, width = stage.shape[1], stage.shape[2]
    deep = rows + 2 * halo
    stage[...] = jnp.zeros(stage.shape, f32)
    stage[:, 0:deep, 0 : cols + 2 * halo] = ext_ref[...]
    w0, w1, c0, c1 = stage[0], stage[1], stage[2], stage[3]
    lane = lax.broadcasted_iota(jnp.int32, (1, width), 1)
    own_cols = (lane >= halo) & (lane < halo + cols)

    planes = head_in
    planes[...] = jnp.zeros(planes.shape, f32)
    put_plane(planes, 0, slot, w0)
    put_plane(planes, 1, slot, w1)
    for r in range(0, deep, 2):
        store_shifted(state_in.at[0], r * slot, take_rows(planes, r * slot, 2 * slot))

    normal_x, normal_y = faces(w0, w1)
    t0, t1 = shifted_fields(w0), shifted_fields(w1)
    fx0 = -advection * (c0 - shift(c0, 1, 0)) * normal_x
    fx1 = -advection * (c1 - shift(c1, 1, 0)) * normal_x
    fy0 = -advection * (c0 - shift(c0, 0, 1)) * normal_y
    fy1 = -advection * (c1 - shift(c1, 0, 1)) * normal_y
    row_id = lax.broadcasted_iota(jnp.int32, (height, width), 0)
    own = own_cols & (row_id >= halo) & (row_id < halo + rows)
    sums = []
    for at, taps, g0, g1 in ((0, taps_x, fx0, fx1), (6, taps_y, fy0, fy1)):
        raw = [g0 * t0[tap] + g1 * t1[tap] for tap in taps]
        mean = sum(raw[1:], raw[0]) * (1.0 / 6.0)
        for k in range(6):
            value = raw[k] - mean
            put_plane(planes, at + k, slot, value)
            sums.append(jnp.sum(jnp.where(own, value, 0.0), axis=0, keepdims=True))
    for r in range(0, deep, 2):
        store_shifted(state_in.at[1], r * slot, take_rows(planes, r * slot, 2 * slot))
    bias_out = jnp.concatenate(sums + [jnp.zeros((128 - coef, width), f32)], axis=0)

    w_in = w_in_ref[...]
    b_in = b_in_ref[...]
    for r in range(1, deep - 1, 2):
        fed = jnp.concatenate(
            [state_in[0, b, (r - 1) * slot : (r + 3) * slot, :] for b in range(3)], axis=0
        )
        linear = mm(w_in, fed) + b_in
        sigma = sigma_of(linear)
        act = linear * sigma
        store_shifted(act_one, (r - 1) * hid, act)
        slope_one[(r - 1) * hid : (r + 1) * hid, :] = sigma + act * (1.0 - sigma)

    b_mid = b_mid_ref[...]
    w_out_t = w_out_t_ref[...]
    bias_acc[...] = jnp.zeros(bias_acc.shape, f32)
    acc_mid[...] = jnp.zeros(acc_mid.shape, f32)
    acc_small[...] = jnp.zeros(acc_small.shape, f32)
    for r in range(2, deep - 2, 2):
        mine = halo <= r < halo + rows
        linear = b_mid
        window = [act_one[b, (r - 2) * hid : (r + 2) * hid, :] for b in range(3)]
        for b in range(3):
            linear = linear + mm(w_mid_ref[b], window[b])
        sigma = sigma_of(linear)
        act = linear * sigma
        act_short = act.astype(bf16)
        act_two_ref[(r - 2) * hid : r * hid, :] = act_short
        fed = jnp.concatenate(
            [state_in[1, b, (r - 1) * slot : (r + 3) * slot, :] for b in range(3)], axis=0
        )
        grad = mm(w_out_t, fed) * (sigma + act * (1.0 - sigma))
        store_shifted(grad_two, (r - 2) * hid, grad)
        if mine:
            kept = jnp.where(own_cols, grad, 0.0)
            bias_acc[0] += kept
            kept = kept.astype(bf16)
            for b in range(3):
                acc_mid[b] += mm_nt(kept, window[b])
            acc_small[0] += mm_nt(fed, jnp.where(own_cols, act, 0.0).astype(bf16))

    for r in range(3, deep - 3, 2):
        grad = mm(w_mid_t_ref[0], grad_two[0, (r - 3) * hid : (r + 1) * hid, :])
        for b in (1, 2):
            grad = grad + mm(w_mid_t_ref[b], grad_two[b, (r - 3) * hid : (r + 1) * hid, :])
        grad = grad * slope_one[(r - 1) * hid : (r + 1) * hid, :]
        grad_one_ref[(r - 3) * hid : (r - 1) * hid, :] = grad.astype(bf16)
        kept = jnp.where(own_cols, grad, 0.0)
        if r == 3:
            bias_acc[1, hid:, :] += kept[hid:, :]
        elif r == deep - 5:
            bias_acc[1, :hid, :] += kept[:hid, :]
        else:
            bias_acc[1] += kept
    for r in range(halo, halo + rows, 2):
        kept = grad_one_ref[(r - 3) * hid : (r - 1) * hid, :]
        kept = jnp.where(own_cols, kept, jnp.zeros((), bf16))
        fed = jnp.concatenate(
            [state_in[0, b, (r - 1) * slot : (r + 3) * slot, :] for b in range(3)], axis=0
        )
        acc_small[1] += mm_nt(fed, kept)

    pay_ref[...] = jnp.zeros(pay_ref.shape, pay_ref.dtype)
    for b in range(3):
        total = acc_mid[b, :hid, : 3 * hid] + acc_mid[b, hid:, hid:]
        for a in range(3):
            t = 3 * a + b
            pay_ref[:hid, t * hid : (t + 1) * hid] = total[:, a * hid : (a + 1) * hid].astype(bf16)
    for a in range(3):
        for b in range(3):
            t = 3 * a + b
            at = (2 - b) * 4 * slot + (2 - a) * slot
            block = (
                acc_small[0, at : at + slot, :hid] + acc_small[0, at + slot : at + 2 * slot, hid:]
            )
            pay_ref[hid:, t * hid : (t + 1) * hid] = block.astype(bf16)
    pieces = []
    for a in range(3):
        for b in range(3):
            at = b * 4 * slot + a * slot
            pieces.append(acc_small[1, at : at + 2, :hid] + acc_small[1, at + slot : at + slot + 2, hid:])
    sums_in, sums_mid = lane_sums(bias_acc[1]), lane_sums(bias_acc[0])
    pieces.append(sums_in[:, :hid] + sums_in[:, hid:])
    pieces.append(sums_mid[:, :hid] + sums_mid[:, hid:])
    pieces.append(lane_sums(bias_out)[:, :hid])
    pieces.append(jnp.zeros((hid - 21, hid), f32))
    pay_ref[:hid, 9 * hid :] = jnp.concatenate(pieces, axis=0).astype(bf16)


def advance_kernel(
    rows,
    cols,
    ext_ref,
    forcing_ref,
    w_head_ref,
    b_head_ref,
    w_in_t_ref,
    act_two_ref,
    grad_one_ref,
    new_ref,
    grad_ref,
    stage,
    head,
    back,
):
    height, width = stage.shape[1], stage.shape[2]
    deep = rows + 2 * halo
    stage[...] = jnp.zeros(stage.shape, f32)
    stage[:, 0:deep, 0 : cols + 2 * halo] = ext_ref[...]
    w0, w1, c0, c1 = stage[0], stage[1], stage[2], stage[3]
    head[...] = jnp.zeros(head.shape, f32)
    back[...] = jnp.zeros(back.shape, f32)
    w_head = w_head_ref[...]
    b_head = b_head_ref[...]
    for r in range(3, deep - 3, 2):
        part = mm(w_head, act_two_ref[(r - 3) * hid : (r + 1) * hid, :])
        size = 2 * slot
        out = b_head
        for b in range(3):
            out = out + shift(part[b * size : (b + 1) * size], 0, b - 1)
        put_rows(head, r * slot, out)
    w_in_t = w_in_t_ref[...]
    for r in range(halo, halo + rows, 2):
        part = mm(w_in_t, grad_one_ref[(r - 4) * hid : r * hid, :])
        out = part[16:32]
        for b in (0, 2):
            out = out + shift(part[b * 16 : (b + 1) * 16], 0, b - 1)
        put_rows(back, r * 8, out)

    coefs = [take_plane(head, k, deep, slot) for k in range(coef)]
    mean_x = sum(coefs[1:6], coefs[0]) * (1.0 / 6.0)
    mean_y = sum(coefs[7:12], coefs[6]) * (1.0 / 6.0)
    sx = [coefs[k] - mean_x + face_base[0][k] for k in range(6)]
    sy = [coefs[6 + k] - mean_y + face_base[1][k] for k in range(6)]
    normal_x, normal_y = faces(w0, w1)
    grad_x = [-advection * (c - shift(c, 1, 0)) for c in (c0, c1)]
    grad_y = [-advection * (c - shift(c, 0, 1)) for c in (c0, c1)]
    normal_grad_x, normal_grad_y = 0.0, 0.0
    for c, (w, cot) in enumerate(((w0, c0), (w1, c1))):
        table = shifted_fields(w)
        face_x = sum(s * table[tap] for s, tap in zip(sx, taps_x))
        face_y = sum(s * table[tap] for s, tap in zip(sy, taps_y))
        flux_x = normal_x * face_x
        flux_y = normal_y * face_y
        normal_grad_x = normal_grad_x + grad_x[c] * face_x
        normal_grad_y = normal_grad_y + grad_y[c] * face_y
        around = table[1, 0] + table[-1, 0] + table[0, 1] + table[0, -1]
        new = (
            w
            - advection
            * (flux_x - shift(flux_x, -1, 0) + flux_y - shift(flux_y, 0, -1))
            + viscosity * (around - 4.0 * w)
        )
        if c == 0:
            new = new + forcing_ref[...]
        new_ref[c] = new[halo : halo + rows, halo : halo + cols]
    for c, cot in enumerate((c0, c1)):
        around = shift(cot, 1, 0) + shift(cot, -1, 0) + shift(cot, 0, 1) + shift(cot, 0, -1)
        total = cot + viscosity * (around - 4.0 * cot)
        flow_x = normal_x * grad_x[c]
        flow_y = normal_y * grad_y[c]
        by_col = {-1: {}, 0: {}, 1: {}}
        for s, (a, b) in zip(sx, taps_x):
            by_col[b][a] = by_col[b].get(a, 0.0) + flow_x * s
        for s, (a, b) in zip(sy, taps_y):
            by_col[b][a] = by_col[b].get(a, 0.0) + flow_y * s
        for b, column in by_col.items():
            part = sum(shift(value, -a, 0) for a, value in column.items())
            total = total + shift(part, 0, -b)
        if c == 0:
            total = total + 0.5 * (normal_grad_x + shift(normal_grad_x, -1, 0))
        else:
            total = total + 0.5 * (normal_grad_y + shift(normal_grad_y, 0, -1))
        total = total + take_plane(back, c, deep, 8)
        grad_ref[c] = total[halo : halo + rows, halo : halo + cols]


def finish_kernel(scale, one_ref, two_ref, in_ref, b_in_ref, mid_ref, b_mid_ref, out_ref, b_out_ref):
    total = (one_ref[...].astype(f32) + two_ref[...].astype(f32)) * scale
    for t in range(9):
        mid_ref[t] = total[:hid, t * hid : (t + 1) * hid]
        out_ref[:, t, :] = total[hid : hid + coef, t * hid : (t + 1) * hid]
    tail = total[:hid, 9 * hid :]
    for t in range(9):
        in_ref[t] = tail[2 * t : 2 * t + 2]
    b_in_ref[...] = tail[18:19]
    b_mid_ref[...] = tail[19:20]
    b_out_ref[...] = tail[20:21, :coef]


def banded(blocks):
    lower = jnp.pad(blocks, ((0, 0), (0, 1), (0, 0), (0, 0)))
    upper = jnp.pad(blocks, ((0, 0), (1, 0), (0, 0), (0, 0)))
    both = jnp.stack([lower, upper], axis=1)
    both = jnp.transpose(both, (0, 1, 3, 2, 4))
    return both.reshape(3, 2 * blocks.shape[2], 4 * blocks.shape[3])


def pad_dim(array, dim, size):
    pads = [(0, 0)] * array.ndim
    pads[dim] = (0, size - array.shape[dim])
    return jnp.pad(array, pads)


def across(stacked):
    return jnp.transpose(stacked, (1, 0, 2)).reshape(stacked.shape[1], -1)


def weights(kernel_in, kernel_mid, kernel_out):
    k_in = jnp.transpose(kernel_in, (3, 2, 0, 1))
    k_mid = jnp.transpose(kernel_mid, (3, 2, 0, 1))
    k_out = jnp.transpose(kernel_out, (3, 2, 0, 1))

    def turned(k):
        return jnp.transpose(k[::-1, ::-1], (0, 1, 3, 2))

    w_in = across(banded(pad_dim(k_in, 3, slot)))
    w_mid = banded(k_mid)
    w_mid_t = banded(turned(k_mid))
    w_out_t = across(banded(pad_dim(turned(k_out), 3, slot)))
    w_head = banded(pad_dim(k_out, 2, slot)).reshape(6 * slot, 4 * hid)
    w_in_t = banded(pad_dim(turned(k_in), 2, 8)).reshape(48, 4 * hid)
    return w_in, w_mid, w_mid_t, w_out_t, w_head, w_in_t


def ring(count, step):
    return [(i, (i + step) % count) for i in range(count)]


def extended(fields):
    short = fields.astype(bf16)
    for axis, dim in (("gy", 2), ("gx", 1)):
        count = lax.axis_size(axis)
        size = short.shape[dim]
        low = lax.ppermute(lax.slice_in_dim(short, size - halo, size, axis=dim), axis, ring(count, 1))
        high = lax.ppermute(lax.slice_in_dim(short, 0, halo, axis=dim), axis, ring(count, -1))
        short = jnp.concatenate([low, short, high], axis=dim)
        fields = jnp.concatenate([low.astype(f32), fields, high.astype(f32)], axis=dim)
    return fields


def per_device(velocity, kernel_in, bias_in, kernel_mid, bias_mid, kernel_out, bias_out, cotangent):
    rows, cols = velocity.shape[1], velocity.shape[2]
    ny_total = lax.axis_size("gy") * cols
    cell_count = lax.axis_size("gx") * rows * ny_total
    deep = rows + 2 * halo
    height = deep
    width = -(-(cols + 2 * halo) // 128) * 128
    vmem = pl.BlockSpec(memory_space=pltpu.VMEM)
    params = pltpu.CompilerParams(vmem_limit_bytes=48 << 20)

    w_in, w_mid, w_mid_t, w_out_t, w_head, w_in_t = weights(kernel_in, kernel_mid, kernel_out)
    b_in = jnp.tile(bias_in, 2)[:, None]
    b_mid = jnp.tile(bias_mid, 2)[:, None]
    b_head = jnp.tile(pad_dim(bias_out, 0, slot), 2)[:, None]
    columns = lax.iota(jnp.int32, width) - halo + lax.axis_index("gy") * cols
    forcing = forcing_amp * jnp.sin(2.0 * math.pi * forcing_wave * columns.astype(f32) / ny_total)
    ext = extended(jnp.concatenate([velocity, cotangent], axis=0))

    payload, act_two, grad_one = pl.pallas_call(
        lambda *refs: backward_kernel(rows, cols, *refs),
        out_shape=(
            jax.ShapeDtypeStruct((hid + slot, 10 * hid), bf16),
            jax.ShapeDtypeStruct(((deep - 4) * hid, width), bf16),
            jax.ShapeDtypeStruct(((deep - 6) * hid, width), bf16),
        ),
        in_specs=[vmem] * 7,
        out_specs=(vmem,) * 3,
        scratch_shapes=[
            pltpu.VMEM((4, height, width), f32),
            pltpu.VMEM((2, 3, deep * slot, width), bf16),
            pltpu.VMEM((width // 128, deep * slot, 128), f32),
            pltpu.VMEM((3, (deep - 2) * hid, width), bf16),
            pltpu.VMEM(((deep - 2) * hid, width), f32),
            pltpu.VMEM((3, (deep - 4) * hid, width), bf16),
            pltpu.VMEM((3, 2 * hid, 4 * hid), f32),
            pltpu.VMEM((2, 12 * slot, 2 * hid), f32),
            pltpu.VMEM((2, 2 * hid, width), f32),
        ],
        compiler_params=params,
        name="backward",
    )(ext, w_in, w_mid, w_mid_t, w_out_t, b_in, b_mid)

    new_velocity, grad_velocity = pl.pallas_call(
        lambda *refs: advance_kernel(rows, cols, *refs),
        out_shape=(jax.ShapeDtypeStruct(velocity.shape, f32),) * 2,
        in_specs=[vmem] * 7,
        out_specs=(vmem,) * 2,
        scratch_shapes=[
            pltpu.VMEM((4, height, width), f32),
            pltpu.VMEM((width // 128, deep * slot, 128), f32),
            pltpu.VMEM((width // 128, deep * 8, 128), f32),
        ],
        compiler_params=params,
        name="advance",
    )(ext, forcing[None, :], w_head, b_head, w_in_t, act_two, grad_one)

    steps = []
    for axis in ("gy", "gx"):
        count = lax.axis_size(axis)
        steps += [(axis, count, 1 << k) for k in range(count.bit_length() - 1)]
    for at, (axis, count, bit) in enumerate(steps):
        arrived = lax.ppermute(payload, axis, [(i, i ^ bit) for i in range(count)])
        if at < len(steps) - 1:
            payload = (payload.astype(f32) + arrived.astype(f32)).astype(bf16)

    g_in, gb_in, g_mid, gb_mid, g_out, gb_out = pl.pallas_call(
        lambda *refs: finish_kernel(1.0 / math.sqrt(cell_count), *refs),
        out_shape=(
            jax.ShapeDtypeStruct((9, 2, hid), f32),
            jax.ShapeDtypeStruct((1, hid), f32),
            jax.ShapeDtypeStruct((9, hid, hid), f32),
            jax.ShapeDtypeStruct((1, hid), f32),
            jax.ShapeDtypeStruct((coef, 9, hid), f32),
            jax.ShapeDtypeStruct((1, coef), f32),
        ),
        in_specs=[vmem] * 2,
        out_specs=(vmem,) * 6,
        compiler_params=params,
        name="finish",
    )(payload, arrived)

    return (
        new_velocity,
        grad_velocity,
        jnp.transpose(g_in.reshape(3, 3, 2, hid), (3, 2, 0, 1)),
        gb_in.reshape(hid),
        jnp.transpose(g_mid.reshape(3, 3, hid, hid), (2, 3, 0, 1)),
        gb_mid.reshape(hid),
        jnp.transpose(g_out.reshape(coef, 3, 3, hid), (0, 3, 1, 2)),
        gb_out.reshape(coef),
    )


def solution(mesh):
    in_specs = (P("groups", "gx", "gy"), P(), P(), P(), P(), P(), P(), P("groups", "gx", "gy"))
    out_specs = (
        P("groups", "gx", "gy"),
        P("groups", "gx", "gy"),
        P("groups", None, None, None),
        P("groups"),
        P("groups", None, None, None),
        P("groups"),
        P("groups", None, None, None),
        P("groups"),
    )
    return jax.shard_map(
        per_device, mesh=mesh, in_specs=in_specs, out_specs=out_specs, check_vma=False
    )
```

profile of v0, /device:TPU:0, one launch (start us, length us, event | category | flops | bytes accessed | tf_op | source)
XLA Modules:
  0.0 40.4 jit_solution(2609817456539723013)
XLA Ops:
  0.7 0.8 %constant_dynamic-update-slice_fusion.1 = f32[4,16,256]{2,1,0:T(8,128)S(1)} fusion(f32[2,16,256]{2,1,0:T(8,128)} %param.8), kind=kLoop, calls=%fused_computation.27 | loop fusion | bytes 65536
  1.5 0.1 fusion
  1.6 0.5 %collective-permute-start = (bf16[4,16,4]{2,1,0:T(8,128)(2,1)S(1)}, bf16[4,16,4]{2,1,0:T(8,128)(2,1)S(1)}, u32[]{:S(2)}, u32[]{:S(2)}) collective-permute-start(bf16[4,16,4]{2,1,0:T(8,128)(2,1)S(1)} %get-tuple-element.50), channel_id=1, source_target_pairs={{0,1},{1,2},{2,3},{3,0},{4,5},{5,6},{6,7},{7,4},{8,9},{9,10},{10,1... | collective-permute-start | bytes 1544 | tf_op jit(solution)/shard_map/ppermute | solution.py:384
  2.0 2.0 %collective-permute-start.1 = (bf16[4,16,4]{2,1,0:T(8,128)(2,1)S(1)}, bf16[4,16,4]{2,1,0:T(8,128)(2,1)S(1)}, u32[]{:S(2)}, u32[]{:S(2)}) collective-permute-start(bf16[4,16,4]{2,1,0:T(8,128)(2,1)S(1)} %get-tuple-element.51), channel_id=1, source_target_pairs={{0,3},{1,0},{2,1},{3,2},{4,7},{5,4},{6,5},{7,6},{8,11},{9,8},{10,9... | collective-permute-start | bytes 1544 | tf_op jit(solution)/shard_map/ppermute | solution.py:385
  4.0 0.1 pad_bitcast_fusion.3
  4.1 0.1 pad_bitcast_fusion.1
  4.2 0.7 %copy-done.1 = bf16[12,64,3,3]{1,3,2,0:T(4,128)(2,1)S(1)} copy-done((bf16[12,64,3,3]{1,3,2,0:T(4,128)(2,1)S(1)}, bf16[12,64,3,3]{1,3,2,0:T(4,128)(2,1)}, u32[]{:S(2)}) %copy-start.1) | copy-done | bytes 13848
  4.8 0.1 rev.11
  5.1 0.6 %copy-done.3 = bf16[64,2,3,3]{0,1,3,2:T(2,128)(2,1)S(1)} copy-done((bf16[64,2,3,3]{0,1,3,2:T(2,128)(2,1)S(1)}, bf16[64,2,3,3]{0,1,3,2:T(2,128)(2,1)}, u32[]{:S(2)}) %copy-start.3) | copy-done | bytes 2328
  5.7 0.1 maximum_bitcast_fusion.1
  5.8 0.1 maximum_bitcast_fusion
  5.9 0.1 maximum_bitcast_fusion.3
  6.1 0.1 maximum_bitcast_fusion.2
  6.2 0.1 pad_maximum_fusion.3
  6.3 2.4 %collective-permute-start.2 = (bf16[4,4,264]{2,1,0:T(4,128)(2,1)S(1)}, bf16[4,4,264]{2,1,0:T(4,128)(2,1)S(1)}, u32[]{:S(2)}, u32[]{:S(2)}) collective-permute-start(bf16[4,4,264]{2,1,0:T(4,128)(2,1)S(1)} %get-tuple-element.42), channel_id=1, source_target_pairs={{0,4},{4,8},{8,12},{12,0},{1,5},{5,9},{9,13},{13,1},{2,6},{6,10},{... | collective-permute-start | bytes 25352 | tf_op jit(solution)/shard_map/ppermute | solution.py:384
  8.7 2.1 %collective-permute-start.3 = (bf16[4,4,264]{2,1,0:T(4,128)(2,1)S(1)}, bf16[4,4,264]{2,1,0:T(4,128)(2,1)S(1)}, u32[]{:S(2)}, u32[]{:S(2)}) collective-permute-start(bf16[4,4,264]{2,1,0:T(4,128)(2,1)S(1)} %get-tuple-element.43), channel_id=1, source_target_pairs={{0,12},{4,0},{8,4},{12,8},{1,13},{5,1},{9,5},{13,9},{2,14},{6,2},{... | collective-permute-start | bytes 25352 | tf_op jit(solution)/shard_map/ppermute | solution.py:385
  10.8 0.2 copy.27
  11.1 0.3 reshape.80.refs_3_
  11.4 0.3 copy.26
  11.7 0.3 reshape.79.refs_2_
  12.0 0.1 copy.28
  12.1 0.1 reshape.81
  12.2 0.1 copy.30.refs_4_
  12.3 0.1 copy.25
  12.4 0.1 reshape.77
  12.5 0.1 copy.29.refs_1_
  12.7 0.5 %copy-done.4 = f32[64]{0:T(128)S(1)} copy-done((f32[64]{0:T(128)S(1)}, f32[64]{0:T(128)}, u32[]{:S(2)}) %copy-start.4) | copy-done | bytes 280
  13.2 0.1 broadcast_in_dim_tile.13.refs_5_
  13.3 0.5 %copy-done.5 = f32[64]{0:T(128)S(1)} copy-done((f32[64]{0:T(128)S(1)}, f32[64]{0:T(128)}, u32[]{:S(2)}) %copy-start.5) | copy-done | bytes 280
  13.8 0.1 broadcast_in_dim_tile.14.refs_6_
  14.0 0.1 reshape_reshape.6.refs_2_
  14.2 0.1 pad_maximum_fusion.refs_0_
  14.4 6.8 %backward.1 = (bf16[80,640]{1,0:T(8,128)(2,1)S(1)}, bf16[1280,384]{1,0:T(8,128)(2,1)S(1)}, bf16[1152,384]{1,0:T(8,128)(2,1)S(1)}) custom-call(f32[4,24,264]{2,1,0:T(8,128)S(1)} %pad_maximum_fusion.refs_0_, bf16[128,192]{1,0:T(8,128)(2,1)S(1)} %copy.29.refs_1_, bf16[3,128,256]{2,1,0:T(8,128)(2,1)S(1)} %reshape.79.refs_2_, ...), custom_call_target="tpu_custom_call" | custom-call | tf_op jit(solution)/shard_map/backward/pallas_call | solution.py:409
  21.2 0.5 %collective-permute-start.4 = (bf16[80,640]{1,0:T(8,128)(2,1)S(1)}, bf16[80,640]{1,0:T(8,128)(2,1)S(1)}, u32[]{:S(2)}, u32[]{:S(2)}) collective-permute-start(bf16[80,640]{1,0:T(8,128)(2,1)S(1)} %get-tuple-element.23), channel_id=1, source_target_pairs={{0,1},{1,0},{2,3},{3,2},{4,5},{5,4},{6,7},{7,6},{8,9},{9,8},{10,11... | collective-permute-start | bytes 307208 | tf_op jit(solution)/shard_map/ppermute | solution.py:452
  21.8 0.9 %collective-permute-done.4 = bf16[80,640]{1,0:T(8,128)(2,1)S(1)} collective-permute-done((bf16[80,640]{1,0:T(8,128)(2,1)S(1)}, bf16[80,640]{1,0:T(8,128)(2,1)S(1)}, u32[]{:S(2)}, u32[]{:S(2)}) %collective-permute-start.4) | collective-permute-done | bytes 102432 | tf_op jit(solution)/shard_map/ppermute | solution.py:452
  22.7 1.6 %collective-permute-start.5 = (bf16[80,640]{1,0:T(8,128)(2,1)S(1)}, bf16[80,640]{1,0:T(8,128)(2,1)S(1)}, u32[]{:S(2)}, u32[]{:S(2)}) collective-permute-start(bf16[80,640]{1,0:T(8,128)(2,1)S(1)} %add_convert_fusion.2), channel_id=1, source_target_pairs={{0,2},{1,3},{2,0},{3,1},{4,6},{5,7},{6,4},{7,5},{8,10},{9,11},{10,... | collective-permute-start | bytes 307208 | tf_op jit(solution)/shard_map/ppermute | solution.py:452
  24.3 3.6 %collective-permute-done.5 = bf16[80,640]{1,0:T(8,128)(2,1)S(1)} collective-permute-done((bf16[80,640]{1,0:T(8,128)(2,1)S(1)}, bf16[80,640]{1,0:T(8,128)(2,1)S(1)}, u32[]{:S(2)}, u32[]{:S(2)}) %collective-permute-start.5) | collective-permute-done | bytes 102432 | tf_op jit(solution)/shard_map/ppermute | solution.py:452
  28.0 0.1 collective-permute-start.6
  28.1 0.1 reshape_reshape.7.refs_4_
  28.2 0.5 %copy-done.6 = f32[12]{0:T(128)S(1)} copy-done((f32[12]{0:T(128)S(1)}, f32[12]{0:T(128)}, u32[]{:S(2)}) %copy-start.6) | copy-done | bytes 72
  28.8 0.1 broadcast_in_dim_tile.12.refs_3_
  28.8 3.8 %collective-permute-done.6 = bf16[80,640]{1,0:T(8,128)(2,1)S(1)} collective-permute-done((bf16[80,640]{1,0:T(8,128)(2,1)S(1)}, bf16[80,640]{1,0:T(8,128)(2,1)S(1)}, u32[]{:S(2)}, u32[]{:S(2)}) %collective-permute-start.6) | collective-permute-done | bytes 102432 | tf_op jit(solution)/shard_map/ppermute | solution.py:452
  32.7 0.7 %collective-permute-start.7 = (bf16[80,640]{1,0:T(8,128)(2,1)S(1)}, bf16[80,640]{1,0:T(8,128)(2,1)S(1)}, u32[]{:S(2)}, u32[]{:S(2)}) collective-permute-start(bf16[80,640]{1,0:T(8,128)(2,1)S(1)} %add_convert_fusion.refs_0_), channel_id=1, source_target_pairs={{0,8},{4,12},{8,0},{12,4},{1,9},{5,13},{9,1},{13,5},{2,10},{6,14},... | collective-permute-start | bytes 307208 | tf_op jit(solution)/shard_map/ppermute | solution.py:452
  33.5 0.1 sine_multiply_fusion.refs_1_
  33.5 1.7 %advance.1 = (f32[2,16,256]{2,1,0:T(8,128)}, f32[2,16,256]{2,1,0:T(8,128)}) custom-call(f32[4,24,264]{2,1,0:T(8,128)S(1)} %pad_maximum_fusion.refs_0_, f32[1,384]{1,0:T(1,128)S(1)} %sine_multiply_fusion.refs_1_, bf16[96,256]{1,0:T(8,128)(2,1)S(1)} %reshape_reshape.6.refs_2_, f32[32,1]{1,0:T(8,128)S(1)} %broadcast_in_dim_tile.12.refs_3_, ...), custom_call_target="tpu_custom_call" | custom-call | tf_op jit(solution)/shard_map/advance/pallas_call | solution.py:433
  35.2 3.7 %collective-permute-done.7.refs_1_ = bf16[80,640]{1,0:T(8,128)(2,1)S(1)} collective-permute-done((bf16[80,640]{1,0:T(8,128)(2,1)S(1)}, bf16[80,640]{1,0:T(8,128)(2,1)S(1)}, u32[]{:S(2)}, u32[]{:S(2)}) %collective-permute-start.7) | collective-permute-done | bytes 102432 | tf_op jit(solution)/shard_map/ppermute | solution.py:452
  38.9 0.9 %finish.1 = (f32[9,2,64]{2,1,0:T(2,128)}, f32[1,64]{1,0:T(1,128)}, f32[9,64,64]{2,1,0:T(8,128)}, f32[1,64]{1,0:T(1,128)}, f32[12,9,64]{2,1,0:T(8,128)S(1)}, /*index=5*/f32[1,12]{1,0:T(1,128)}) custom-call(bf16[80,640]{1,0:T(8,128)(2,1)S(1)} %add_convert_fusion.refs_0_, bf16[80,640]{1,0:T(8,128)(2,1)S(1)} %collective-permute-done.7.refs_1_), custom_call_target="tpu_custom_call" | custom-call | tf_op jit(solution)/shard_map/finish/pallas_call | solution.py:456
  39.8 0.7 %copy.35 = f32[12,64,3,3]{1,3,2,0:T(4,128)} copy(f32[12,64,3,3]{1,0,3,2:T(8,128)S(1)} %bitcast.68) | data formatting | bytes 55296
  (41 shorter events, 0.5 us)
Async XLA Ops:
  0.6 0.8 %copy-start.2 = (f32[2,16,256]{2,1,0:T(8,128)S(1)}, f32[2,16,256]{2,1,0:T(8,128)}, u32[]{:S(2)}) copy-start(f32[2,16,256]{2,1,0:T(8,128)} %param.15) | copy-start | bytes 98308
  0.6 3.3 %copy-start = (bf16[64,64,3,3]{1,0,3,2:T(8,128)(2,1)S(1)}, bf16[64,64,3,3]{1,0,3,2:T(8,128)(2,1)}, u32[]{:S(2)}) copy-start(bf16[64,64,3,3]{1,0,3,2:T(8,128)(2,1)} %param.11) | copy-start | bytes 221188
  1.6 4.6 %collective-permute-start = (bf16[4,16,4]{2,1,0:T(8,128)(2,1)S(1)}, bf16[4,16,4]{2,1,0:T(8,128)(2,1)S(1)}, u32[]{:S(2)}, u32[]{:S(2)}) collective-permute-start(bf16[4,16,4]{2,1,0:T(8,128)(2,1)S(1)} %get-tuple-element.50), channel_id=1, source_target_pairs={{0,1},{1,2},{2,3},{3,0},{4,5},{5,6},{6,7},{7,4},{8,9},{9,10},{10,1... | collective-permute-start | bytes 1544 | tf_op jit(solution)/shard_map/ppermute | solution.py:384
  2.0 4.2 %collective-permute-start.1 = (bf16[4,16,4]{2,1,0:T(8,128)(2,1)S(1)}, bf16[4,16,4]{2,1,0:T(8,128)(2,1)S(1)}, u32[]{:S(2)}, u32[]{:S(2)}) collective-permute-start(bf16[4,16,4]{2,1,0:T(8,128)(2,1)S(1)} %get-tuple-element.51), channel_id=1, source_target_pairs={{0,3},{1,0},{2,1},{3,2},{4,7},{5,4},{6,5},{7,6},{8,11},{9,8},{10,9... | collective-permute-start | bytes 1544 | tf_op jit(solution)/shard_map/ppermute | solution.py:385
  4.1 0.8 %copy-start.1 = (bf16[12,64,3,3]{1,3,2,0:T(4,128)(2,1)S(1)}, bf16[12,64,3,3]{1,3,2,0:T(4,128)(2,1)}, u32[]{:S(2)}) copy-start(bf16[12,64,3,3]{1,3,2,0:T(4,128)(2,1)} %param.13) | copy-start | bytes 41476
  5.0 0.7 %copy-start.3 = (bf16[64,2,3,3]{0,1,3,2:T(2,128)(2,1)S(1)}, bf16[64,2,3,3]{0,1,3,2:T(2,128)(2,1)}, u32[]{:S(2)}) copy-start(bf16[64,2,3,3]{0,1,3,2:T(2,128)(2,1)} %param.9) | copy-start | bytes 6916
  6.3 7.9 %collective-permute-start.2 = (bf16[4,4,264]{2,1,0:T(4,128)(2,1)S(1)}, bf16[4,4,264]{2,1,0:T(4,128)(2,1)S(1)}, u32[]{:S(2)}, u32[]{:S(2)}) collective-permute-start(bf16[4,4,264]{2,1,0:T(4,128)(2,1)S(1)} %get-tuple-element.42), channel_id=1, source_target_pairs={{0,4},{4,8},{8,12},{12,0},{1,5},{5,9},{9,13},{13,1},{2,6},{6,10},{... | collective-permute-start | bytes 25352 | tf_op jit(solution)/shard_map/ppermute | solution.py:384
  8.7 5.5 %collective-permute-start.3 = (bf16[4,4,264]{2,1,0:T(4,128)(2,1)S(1)}, bf16[4,4,264]{2,1,0:T(4,128)(2,1)S(1)}, u32[]{:S(2)}, u32[]{:S(2)}) collective-permute-start(bf16[4,4,264]{2,1,0:T(4,128)(2,1)S(1)} %get-tuple-element.43), channel_id=1, source_target_pairs={{0,12},{4,0},{8,4},{12,8},{1,13},{5,1},{9,5},{13,9},{2,14},{6,2},{... | collective-permute-start | bytes 25352 | tf_op jit(solution)/shard_map/ppermute | solution.py:385
  12.5 0.7 %copy-start.4 = (f32[64]{0:T(128)S(1)}, f32[64]{0:T(128)}, u32[]{:S(2)}) copy-start(f32[64]{0:T(128)} %param.10) | copy-start | bytes 772
  13.2 0.7 %copy-start.5 = (f32[64]{0:T(128)S(1)}, f32[64]{0:T(128)}, u32[]{:S(2)}) copy-start(f32[64]{0:T(128)} %param.12) | copy-start | bytes 772
  21.2 1.5 %collective-permute-start.4 = (bf16[80,640]{1,0:T(8,128)(2,1)S(1)}, bf16[80,640]{1,0:T(8,128)(2,1)S(1)}, u32[]{:S(2)}, u32[]{:S(2)}) collective-permute-start(bf16[80,640]{1,0:T(8,128)(2,1)S(1)} %get-tuple-element.23), channel_id=1, source_target_pairs={{0,1},{1,0},{2,3},{3,2},{4,5},{5,4},{6,7},{7,6},{8,9},{9,8},{10,11... | collective-permute-start | bytes 307208 | tf_op jit(solution)/shard_map/ppermute | solution.py:452
  22.7 5.2 %collective-permute-start.5 = (bf16[80,640]{1,0:T(8,128)(2,1)S(1)}, bf16[80,640]{1,0:T(8,128)(2,1)S(1)}, u32[]{:S(2)}, u32[]{:S(2)}) collective-permute-start(bf16[80,640]{1,0:T(8,128)(2,1)S(1)} %add_convert_fusion.2), channel_id=1, source_target_pairs={{0,2},{1,3},{2,0},{3,1},{4,6},{5,7},{6,4},{7,5},{8,10},{9,11},{10,... | collective-permute-start | bytes 307208 | tf_op jit(solution)/shard_map/ppermute | solution.py:452
  28.0 4.7 %collective-permute-start.6 = (bf16[80,640]{1,0:T(8,128)(2,1)S(1)}, bf16[80,640]{1,0:T(8,128)(2,1)S(1)}, u32[]{:S(2)}, u32[]{:S(2)}) collective-permute-start(bf16[80,640]{1,0:T(8,128)(2,1)S(1)} %add_convert_fusion.1), channel_id=1, source_target_pairs={{0,4},{4,0},{8,12},{12,8},{1,5},{5,1},{9,13},{13,9},{2,6},{6,2},{1... | collective-permute-start | bytes 307208 | tf_op jit(solution)/shard_map/ppermute | solution.py:452
  28.1 0.7 %copy-start.6 = (f32[12]{0:T(128)S(1)}, f32[12]{0:T(128)}, u32[]{:S(2)}) copy-start(f32[12]{0:T(128)} %param.14) | copy-start | bytes 148
  32.7 6.2 %collective-permute-start.7 = (bf16[80,640]{1,0:T(8,128)(2,1)S(1)}, bf16[80,640]{1,0:T(8,128)(2,1)S(1)}, u32[]{:S(2)}, u32[]{:S(2)}) collective-permute-start(bf16[80,640]{1,0:T(8,128)(2,1)S(1)} %add_convert_fusion.refs_0_), channel_id=1, source_target_pairs={{0,8},{4,12},{8,0},{12,4},{1,9},{5,13},{9,1},{13,5},{2,10},{6,14},... | collective-permute-start | bytes 307208 | tf_op jit(solution)/shard_map/ppermute | solution.py:452
where the time goes:
time: 40.7 us; the launch traced here: 40.4 us
  waiting for transfers between devices  12.1 us (30%)
  starting transfers between devices  9.81 us (24%)
  Pallas kernels  9.37 us (23%)
  local copies, waits for them, and re-layouts  7.31 us (18%)
  between operations  1.01 us (2%)
  other arithmetic  0.82 us (2%)
    ppermute x4, waiting for transfers between devices, per_device(): arrived = lax.ppermute(payload, axis, [(i, i ^ bit) for i in range(count)])  12.1 us
    pallas_call x1, Pallas kernels, per_device(): pl.pallas_call(lambda *refs: backward_kernel(rows, cols, *refs), out_shap...  6.83 us
    unnamed x16, local copies, waits for them, and re-layouts  4.39 us
    ppermute x2, starting transfers between devices, extended(): lax.ppermute(lax.slice_in_dim(short, 0, halo, axis=dim), axis, ring(count...  4.07 us
    ppermute x4, starting transfers between devices, per_device(): arrived = lax.ppermute(payload, axis, [(i, i ^ bit) for i in range(count)])  2.89 us
    ppermute x2, starting transfers between devices, extended(): lax.ppermute(lax.slice_in_dim(short, size - halo, size, axis=dim), axis,...  2.84 us
    pallas_call x1, Pallas kernels, per_device(): pl.pallas_call(lambda *refs: advance_kernel(rows, cols, *refs), out_shape...  1.69 us
    pallas_call x1, Pallas kernels, per_device(): pl.pallas_call(lambda *refs: finish_kernel(1.0 / math.sqrt(cell_count), *...  0.86 us
  transfers between devices with their start and end apart: 8, of which 4 were waited for; matrix products, arithmetic and copies ran while one was open for 8% of the time, Pallas kernels for 4%

commit v1 on v0

--- a/solution.py
+++ b/solution.py
@@ -100,9 +100,12 @@
     w_out_t_ref,
     b_in_ref,
     b_mid_ref,
-    pay_ref,
+    core_ref,
+    keep_ref,
+    send_ref,
     act_two_ref,
     grad_one_ref,
+    pay,
     stage,
     state_in,
     head_in,
@@ -149,7 +152,7 @@
     bias_out = jnp.concatenate(sums + [jnp.zeros((128 - coef, width), f32)], axis=0)
 
     w_in = w_in_ref[...]
-    b_in = b_in_ref[...]
+    b_in = b_in_ref[:, 0:1]
     for r in range(1, deep - 1, 2):
         fed = jnp.concatenate(
             [state_in[0, b, (r - 1) * slot : (r + 3) * slot, :] for b in range(3)], axis=0
@@ -160,7 +163,7 @@
         store_shifted(act_one, (r - 1) * hid, act)
         slope_one[(r - 1) * hid : (r + 1) * hid, :] = sigma + act * (1.0 - sigma)
 
-    b_mid = b_mid_ref[...]
+    b_mid = b_mid_ref[:, 0:1]
     w_out_t = w_out_t_ref[...]
     bias_acc[...] = jnp.zeros(bias_acc.shape, f32)
     acc_mid[...] = jnp.zeros(acc_mid.shape, f32)
@@ -209,31 +212,40 @@
         )
         acc_small[1] += mm_nt(fed, kept)
 
-    pay_ref[...] = jnp.zeros(pay_ref.shape, pay_ref.dtype)
     for b in range(3):
         total = acc_mid[b, :hid, : 3 * hid] + acc_mid[b, hid:, hid:]
         for a in range(3):
             t = 3 * a + b
-            pay_ref[:hid, t * hid : (t + 1) * hid] = total[:, a * hid : (a + 1) * hid].astype(bf16)
-    for a in range(3):
-        for b in range(3):
-            t = 3 * a + b
-            at = (2 - b) * 4 * slot + (2 - a) * slot
-            block = (
-                acc_small[0, at : at + slot, :hid] + acc_small[0, at + slot : at + 2 * slot, hid:]
-            )
-            pay_ref[hid:, t * hid : (t + 1) * hid] = block.astype(bf16)
+            block = total[:, a * hid : (a + 1) * hid].astype(bf16)
+            for h in range(2):
+                pay[h, :, t * hid : (t + 1) * hid] = block[32 * h : 32 * h + 32]
+    slots = []
     pieces = []
     for a in range(3):
         for b in range(3):
+            at = (2 - b) * 4 * slot + (2 - a) * slot
+            slots.append(
+                acc_small[0, at : at + slot, :hid] + acc_small[0, at + slot : at + 2 * slot, hid:]
+            )
             at = b * 4 * slot + a * slot
-            pieces.append(acc_small[1, at : at + 2, :hid] + acc_small[1, at + slot : at + slot + 2, hid:])
+            pieces.append(
+                acc_small[1, at : at + 2, :hid] + acc_small[1, at + slot : at + slot + 2, hid:]
+            )
     sums_in, sums_mid = lane_sums(bias_acc[1]), lane_sums(bias_acc[0])
     pieces.append(sums_in[:, :hid] + sums_in[:, hid:])
     pieces.append(sums_mid[:, :hid] + sums_mid[:, hid:])
     pieces.append(lane_sums(bias_out)[:, :hid])
-    pieces.append(jnp.zeros((hid - 21, hid), f32))
-    pay_ref[:hid, 9 * hid :] = jnp.concatenate(pieces, axis=0).astype(bf16)
+    pieces.append(jnp.zeros((11, hid), f32))
+    rest = jnp.concatenate(pieces, axis=0)
+    slots += [rest[:slot], rest[slot:], jnp.zeros((slot, hid), f32)]
+    for h in range(2):
+        for q in range(3):
+            at = 6 * h + 2 * q
+            block = jnp.concatenate(slots[at : at + 2], axis=0).astype(bf16)
+            pay[h, :, (9 + q) * hid : (10 + q) * hid] = block
+    core = core_ref[0]
+    keep_ref[...] = pay[core]
+    send_ref[...] = pay[1 - core]
 
 
 def advance_kernel(
@@ -260,7 +272,7 @@
     head[...] = jnp.zeros(head.shape, f32)
     back[...] = jnp.zeros(back.shape, f32)
     w_head = w_head_ref[...]
-    b_head = b_head_ref[...]
+    b_head = b_head_ref[:, 0:1]
     for r in range(3, deep - 3, 2):
         part = mm(w_head, act_two_ref[(r - 3) * hid : (r + 1) * hid, :])
         size = 2 * slot
@@ -324,56 +336,88 @@
         grad_ref[c] = total[halo : halo + rows, halo : halo + cols]
 
 
-def finish_kernel(scale, one_ref, two_ref, in_ref, b_in_ref, mid_ref, b_mid_ref, out_ref, b_out_ref):
-    total = (one_ref[...].astype(f32) + two_ref[...].astype(f32)) * scale
+def finish_kernel(
+    scale, mine_ref, other_ref, core_ref, in_ref, b_in_ref, mid_ref, b_mid_ref, out_ref, b_out_ref
+):
+    mine = mine_ref[...].astype(f32) * scale
+    other = other_ref[...].astype(f32) * scale
+    first = core_ref[0] == 0
+    halves = (jnp.where(first, mine, other), jnp.where(first, other, mine))
+    slots = []
+    for h, half in enumerate(halves):
+        for t in range(9):
+            mid_ref[t, 32 * h : 32 * h + 32, :] = half[:, t * hid : (t + 1) * hid]
+        for q in range(3):
+            block = half[:, (9 + q) * hid : (10 + q) * hid]
+            slots += [block[:slot], block[slot:]]
+    for a in range(3):
+        for b in range(3):
+            out_ref[:, a, b, :] = slots[3 * a + b][:coef]
     for t in range(9):
-        mid_ref[t] = total[:hid, t * hid : (t + 1) * hid]
-        out_ref[:, t, :] = total[hid : hid + coef, t * hid : (t + 1) * hid]
-    tail = total[:hid, 9 * hid :]
-    for t in range(9):
-        in_ref[t] = tail[2 * t : 2 * t + 2]
-    b_in_ref[...] = tail[18:19]
-    b_mid_ref[...] = tail[19:20]
-    b_out_ref[...] = tail[20:21, :coef]
-
-
-def banded(blocks):
-    lower = jnp.pad(blocks, ((0, 0), (0, 1), (0, 0), (0, 0)))
-    upper = jnp.pad(blocks, ((0, 0), (1, 0), (0, 0), (0, 0)))
-    both = jnp.stack([lower, upper], axis=1)
-    both = jnp.transpose(both, (0, 1, 3, 2, 4))
-    return both.reshape(3, 2 * blocks.shape[2], 4 * blocks.shape[3])
-
-
-def pad_dim(array, dim, size):
-    pads = [(0, 0)] * array.ndim
-    pads[dim] = (0, size - array.shape[dim])
-    return jnp.pad(array, pads)
-
-
-def across(stacked):
-    return jnp.transpose(stacked, (1, 0, 2)).reshape(stacked.shape[1], -1)
-
-
-def weights(kernel_in, kernel_mid, kernel_out):
-    k_in = jnp.transpose(kernel_in, (3, 2, 0, 1))
-    k_mid = jnp.transpose(kernel_mid, (3, 2, 0, 1))
-    k_out = jnp.transpose(kernel_out, (3, 2, 0, 1))
-
-    def turned(k):
-        return jnp.transpose(k[::-1, ::-1], (0, 1, 3, 2))
-
-    w_in = across(banded(pad_dim(k_in, 3, slot)))
-    w_mid = banded(k_mid)
-    w_mid_t = banded(turned(k_mid))
-    w_out_t = across(banded(pad_dim(turned(k_out), 3, slot)))
-    w_head = banded(pad_dim(k_out, 2, slot)).reshape(6 * slot, 4 * hid)
-    w_in_t = banded(pad_dim(turned(k_in), 2, 8)).reshape(48, 4 * hid)
-    return w_in, w_mid, w_mid_t, w_out_t, w_head, w_in_t
-
-
-def ring(count, step):
-    return [(i, (i + step) % count) for i in range(count)]
+        in_ref[t] = slots[9 + t // 8][2 * t % 16 : 2 * t % 16 + 2]
+    b_in_ref[...] = slots[10][2:3]
+    b_mid_ref[...] = slots[10][3:4]
+    b_out_ref[...] = slots[10][4:5, :coef]
+
+
+def weights_kernel(
+    k_in_ref,
+    k_mid_ref,
+    k_out_ref,
+    b_in_ref,
+    b_mid_ref,
+    b_out_ref,
+    w_in_ref,
+    w_mid_ref,
+    w_mid_t_ref,
+    w_out_t_ref,
+    w_head_ref,
+    w_in_t_ref,
+    c_in_ref,
+    c_mid_ref,
+    c_head_ref,
+):
+    def band(block, upper):
+        none = jnp.zeros(block[0].shape, f32)
+        return jnp.concatenate([none, *block] if upper else [*block, none], axis=1)
+
+    def tall(block, rows):
+        return jnp.concatenate(
+            [block, jnp.zeros((rows - block.shape[0], block.shape[1]), f32)], axis=0
+        )
+
+    k_mid = [k_mid_ref[t].astype(f32) for t in range(9)]
+    k_mid_t = [k.T for k in k_mid]
+    k_out = [k_out_ref[:, t // 3, t % 3, :].astype(f32) for t in range(9)]
+    k_in = [k_in_ref[t].astype(f32) for t in range(9)]
+    in_rows = []
+    out_rows = []
+    zero = jnp.zeros((slot, hid), f32)
+    for b in range(3):
+        forward = [3 * a + b for a in range(3)]
+        backward = [8 - t for t in forward]
+        for u in range(2):
+            at = slice(u * hid, (u + 1) * hid)
+            w_mid_ref[b, at, :] = band([k_mid[t] for t in forward], u).astype(bf16)
+            w_mid_t_ref[b, at, :] = band([k_mid_t[t] for t in backward], u).astype(bf16)
+        head = [band([tall(k_out[t], slot) for t in forward], u) for u in range(2)]
+        w_head_ref[2 * slot * b : 2 * slot * (b + 1), :] = jnp.concatenate(head, 0).astype(bf16)
+        back = [band([tall(k_in[t], 8) for t in backward], u) for u in range(2)]
+        w_in_t_ref[16 * b : 16 * (b + 1), :] = jnp.concatenate(back, 0).astype(bf16)
+        for rows, blocks in (
+            (in_rows, [tall(k_in[t], slot) for t in forward]),
+            (out_rows, [tall(k_out[t], slot) for t in backward]),
+        ):
+            lower = jnp.concatenate(blocks + [zero], axis=0)
+            upper = jnp.concatenate([zero] + blocks, axis=0)
+            rows.append(jnp.concatenate([lower, upper], axis=1))
+    w_in_ref[...] = jnp.concatenate(in_rows, axis=0).T.astype(bf16)
+    w_out_t_ref[...] = jnp.concatenate(out_rows, axis=0).T.astype(bf16)
+    for ref, bias in ((c_in_ref, b_in_ref[...]), (c_mid_ref, b_mid_ref[...])):
+        ref[...] = jnp.broadcast_to(jnp.concatenate([bias, bias], axis=1), (128, 128)).T
+    bias = jnp.concatenate([b_out_ref[...], jnp.zeros((1, slot - coef), f32)], axis=1)
+    bias = jnp.concatenate([bias, bias, jnp.zeros((1, 128 - 2 * slot), f32)], axis=1)
+    c_head_ref[...] = jnp.broadcast_to(bias, (128, 128)).T[: 2 * slot]
 
 
 def extended(fields):
@@ -381,11 +425,52 @@
     for axis, dim in (("gy", 2), ("gx", 1)):
         count = lax.axis_size(axis)
         size = short.shape[dim]
-        low = lax.ppermute(lax.slice_in_dim(short, size - halo, size, axis=dim), axis, ring(count, 1))
-        high = lax.ppermute(lax.slice_in_dim(short, 0, halo, axis=dim), axis, ring(count, -1))
+        even = lax.axis_index(axis) % 2 == 0
+        first = lax.slice_in_dim(short, 0, halo, axis=dim)
+        last = lax.slice_in_dim(short, size - halo, size, axis=dim)
+        far_pairs = [(i, (i + 1 if i % 2 else i - 1) % count) for i in range(count)]
+        far = lax.ppermute(jnp.where(even, first, last), axis, far_pairs)
+        near = lax.ppermute(jnp.where(even, last, first), axis, [(i, i ^ 1) for i in range(count)])
+        low = jnp.where(even, far, near)
+        high = jnp.where(even, near, far)
         short = jnp.concatenate([low, short, high], axis=dim)
         fields = jnp.concatenate([low.astype(f32), fields, high.astype(f32)], axis=dim)
     return fields
+
+
+def swap(value, rows, cols):
+    height, width = lax.axis_size("gx"), lax.axis_size("gy")
+    pairs = [
+        (i * width + j, (i ^ rows) * width + (j ^ cols)) for i in range(height) for j in range(width)
+    ]
+    return lax.ppermute(value, ("gx", "gy"), pairs)
+
+
+def added(*values):
+    sums = [v.astype(f32) for v in values]
+    while len(sums) > 1:
+        sums = [sums[k] + sums[k + 1] for k in range(0, len(sums), 2)]
+    return sums[0].astype(bf16)
+
+
+def summed(keep, send):
+    half = added(keep, swap(send, 0, 1))
+    steps = [(0, 1 << k) for k in range(1, lax.axis_size("gy").bit_length() - 1)]
+    steps += [(1 << k, 0) for k in range(lax.axis_size("gx").bit_length() - 1)]
+    while steps:
+        if len(steps) >= 2 and steps[0][0] == 0 and steps[1][1] == 0:
+            (_, cols), (rows, _) = steps[:2]
+            half = added(
+                half,
+                swap(half, 0, cols),
+                swap(half, rows, 0),
+                swap(half, rows, cols),
+            )
+            steps = steps[2:]
+        else:
+            half = added(half, swap(half, *steps[0]))
+            steps = steps[1:]
+    return half, swap(half, 0, 1)
 
 
 def per_device(velocity, kernel_in, bias_in, kernel_mid, bias_mid, kernel_out, bias_out, cotangent):
@@ -398,24 +483,49 @@
     vmem = pl.BlockSpec(memory_space=pltpu.VMEM)
     params = pltpu.CompilerParams(vmem_limit_bytes=48 << 20)
 
-    w_in, w_mid, w_mid_t, w_out_t, w_head, w_in_t = weights(kernel_in, kernel_mid, kernel_out)
-    b_in = jnp.tile(bias_in, 2)[:, None]
-    b_mid = jnp.tile(bias_mid, 2)[:, None]
-    b_head = jnp.tile(pad_dim(bias_out, 0, slot), 2)[:, None]
+    core = (lax.axis_index("gy") % 2).astype(jnp.int32).reshape(1)
+    smem = pl.BlockSpec(memory_space=pltpu.SMEM)
+    w_in, w_mid, w_mid_t, w_out_t, w_head, w_in_t, b_in, b_mid, b_head = pl.pallas_call(
+        weights_kernel,
+        out_shape=(
+            jax.ShapeDtypeStruct((2 * hid, 12 * slot), bf16),
+            jax.ShapeDtypeStruct((3, 2 * hid, 4 * hid), bf16),
+            jax.ShapeDtypeStruct((3, 2 * hid, 4 * hid), bf16),
+            jax.ShapeDtypeStruct((2 * hid, 12 * slot), bf16),
+            jax.ShapeDtypeStruct((6 * slot, 4 * hid), bf16),
+            jax.ShapeDtypeStruct((48, 4 * hid), bf16),
+            jax.ShapeDtypeStruct((128, 128), f32),
+            jax.ShapeDtypeStruct((128, 128), f32),
+            jax.ShapeDtypeStruct((2 * slot, 128), f32),
+        ),
+        in_specs=[vmem] * 6,
+        out_specs=(vmem,) * 9,
+        compiler_params=params,
+        name="weights",
+    )(
+        jnp.transpose(kernel_in, (2, 3, 1, 0)).reshape(9, 2, hid),
+        jnp.transpose(kernel_mid, (2, 3, 0, 1)).reshape(9, hid, hid),
+        jnp.transpose(kernel_out, (0, 2, 3, 1)),
+        bias_in[None, :],
+        bias_mid[None, :],
+        bias_out[None, :],
+    )
     columns = lax.iota(jnp.int32, width) - halo + lax.axis_index("gy") * cols
     forcing = forcing_amp * jnp.sin(2.0 * math.pi * forcing_wave * columns.astype(f32) / ny_total)
     ext = extended(jnp.concatenate([velocity, cotangent], axis=0))
 
-    payload, act_two, grad_one = pl.pallas_call(
+    keep, send, act_two, grad_one = pl.pallas_call(
         lambda *refs: backward_kernel(rows, cols, *refs),
         out_shape=(
-            jax.ShapeDtypeStruct((hid + slot, 10 * hid), bf16),
+            jax.ShapeDtypeStruct((hid // 2, 12 * hid), bf16),
+            jax.ShapeDtypeStruct((hid // 2, 12 * hid), bf16),
             jax.ShapeDtypeStruct(((deep - 4) * hid, width), bf16),
             jax.ShapeDtypeStruct(((deep - 6) * hid, width), bf16),
         ),
-        in_specs=[vmem] * 7,
-        out_specs=(vmem,) * 3,
+        in_specs=[vmem] * 7 + [smem],
+        out_specs=(vmem,) * 4,
         scratch_shapes=[
+            pltpu.VMEM((2, hid // 2, 12 * hid), bf16),
             pltpu.VMEM((4, height, width), f32),
             pltpu.VMEM((2, 3, deep * slot, width), bf16),
             pltpu.VMEM((width // 128, deep * slot, 128), f32),
@@ -428,7 +538,7 @@
         ],
         compiler_params=params,
         name="backward",
-    )(ext, w_in, w_mid, w_mid_t, w_out_t, b_in, b_mid)
+    )(ext, w_in, w_mid, w_mid_t, w_out_t, b_in, b_mid, core)
 
     new_velocity, grad_velocity = pl.pallas_call(
         lambda *refs: advance_kernel(rows, cols, *refs),
@@ -444,15 +554,7 @@
         name="advance",
     )(ext, forcing[None, :], w_head, b_head, w_in_t, act_two, grad_one)
 
-    steps = []
-    for axis in ("gy", "gx"):
-        count = lax.axis_size(axis)
-        steps += [(axis, count, 1 << k) for k in range(count.bit_length() - 1)]
-    for at, (axis, count, bit) in enumerate(steps):
-        arrived = lax.ppermute(payload, axis, [(i, i ^ bit) for i in range(count)])
-        if at < len(steps) - 1:
-            payload = (payload.astype(f32) + arrived.astype(f32)).astype(bf16)
-
+    mine, other = summed(keep, send)
     g_in, gb_in, g_mid, gb_mid, g_out, gb_out = pl.pallas_call(
         lambda *refs: finish_kernel(1.0 / math.sqrt(cell_count), *refs),
         out_shape=(
@@ -460,14 +562,14 @@
             jax.ShapeDtypeStruct((1, hid), f32),
             jax.ShapeDtypeStruct((9, hid, hid), f32),
             jax.ShapeDtypeStruct((1, hid), f32),
-            jax.ShapeDtypeStruct((coef, 9, hid), f32),
+            jax.ShapeDtypeStruct((coef, 3, 3, hid), f32),
             jax.ShapeDtypeStruct((1, coef), f32),
         ),
-        in_specs=[vmem] * 2,
+        in_specs=[vmem] * 2 + [smem],
         out_specs=(vmem,) * 6,
         compiler_params=params,
         name="finish",
-    )(payload, arrived)
+    )(mine, other, core)
 
     return (
         new_velocity,
@@ -476,7 +578,7 @@
         gb_in.reshape(hid),
         jnp.transpose(g_mid.reshape(3, 3, hid, hid), (2, 3, 0, 1)),
         gb_mid.reshape(hid),
-        jnp.transpose(g_out.reshape(coef, 3, 3, hid), (0, 3, 1, 2)),
+        jnp.transpose(g_out, (0, 3, 1, 2)),
         gb_out.reshape(coef),
     )
 

time: 40.7 us -> 36.7 us (0.902)
  local copies, waits for them, and re-layouts: 7.31 us -> 1.46 us
  starting transfers between devices: 9.81 us -> 14.8 us
  waiting for transfers between devices: 12.1 us -> 9.09 us
  Pallas kernels: 9.37 us -> 9.81 us
    ppermute x8 -> x10, starting transfers between devices: 9.81 us -> 14.8 us  [the longest x6 6.8 us: swap(): return lax.ppermute(value, ('gx', 'gy'), pairs)]
    ppermute x8 -> x10, waiting for transfers between devices: 12.1 us -> 9.09 us  [the longest x6 6.31 us: swap(): return lax.ppermute(value, ('gx', 'gy'), pairs)]
    unnamed x16 -> x15, local copies, waits for them, and re-layouts: 4.39 us -> 1.46 us
    reshape x6 -> x0, local copies, waits for them, and re-layouts: 0.97 us -> none  [the longest x4 0.76 us: banded(): return both.reshape(3, 2 * blocks.shape[2], 4 * blocks.shape[3])]
    transpose x8 -> x0, local copies, waits for them, and re-layouts: 0.86 us -> none  [the longest x6 0.85 us: banded(): both = jnp.transpose(both, (0, 1, 3, 2, 4))]
    another operation x14 -> x0, local copies, waits for them, and re-layouts: 0.84 us -> none  [the longest x6 0.24 us: banded(): both = jnp.stack([lower, upper], axis=1)]
    transpose x6 -> x0, other arithmetic: 0.43 us -> none  [banded(): both = jnp.transpose(both, (0, 1, 3, 2, 4))]
  transfers between devices with their start and end apart: 8 -> 10, of which waited for: 4 -> 8; matrix products, arithmetic and copies ran while one was open for 8% -> 0% of each run, Pallas kernels for 4% -> 6%
where the time goes in v1:
time: 36.7 us; the launch traced here: 36.4 us
  starting transfers between devices  14.8 us (40%)
  Pallas kernels  9.81 us (27%)
  waiting for transfers between devices  9.09 us (25%)
  local copies, waits for them, and re-layouts  1.46 us (4%)
  between operations  0.78 us (2%)
  other arithmetic  0.45 us (1%)
    pallas_call x1, Pallas kernels, per_device(): pl.pallas_call(lambda *refs: backward_kernel(rows, cols, *refs), out_shap...  6.87 us
    ppermute x6, starting transfers between devices, swap(): return lax.ppermute(value, ('gx', 'gy'), pairs)  6.8 us
    ppermute x6, waiting for transfers between devices, swap(): return lax.ppermute(value, ('gx', 'gy'), pairs)  6.31 us
    ppermute x2, starting transfers between devices, extended(): far = lax.ppermute(jnp.where(even, first, last), axis, far_pairs)  4.86 us
    ppermute x2, starting transfers between devices, extended(): lax.ppermute(jnp.where(even, last, first), axis, [(i, i ^ 1) for i in ran...  3.17 us
    ppermute x2, waiting for transfers between devices, extended(): far = lax.ppermute(jnp.where(even, first, last), axis, far_pairs)  2.7 us
    pallas_call x1, Pallas kernels, per_device(): pl.pallas_call(lambda *refs: advance_kernel(rows, cols, *refs), out_shape...  1.69 us
    unnamed x15, local copies, waits for them, and re-layouts  1.46 us
  transfers between devices with their start and end apart: 10, of which 8 were waited for; matrix products, arithmetic and copies ran while one was open for 0% of the time, Pallas kernels for 6%

profile of v1, /device:TPU:0, one launch (start us, length us, event | category | flops | bytes accessed | tf_op | source)
XLA Modules:
  0.0 36.4 jit_solution(16671349503136262719)
XLA Ops:
  0.6 0.0 copy-start.6
  0.7 0.8 %constant_dynamic-update-slice_fusion.1 = f32[4,16,256]{2,1,0:T(8,128)S(1)} fusion(f32[2,16,256]{2,1,0:T(8,128)} %param.8), kind=kLoop, calls=%fused_computation.16 | loop fusion | bytes 65536
  1.4 0.0 copy-done.6
  1.4 0.1 broadcast_select_fusion.3
  1.5 2.4 %collective-permute-start = (bf16[4,16,4]{2,1,0:T(8,128)(2,1)S(1)}, bf16[4,16,4]{2,1,0:T(8,128)(2,1)S(1)}, u32[]{:S(2)}, u32[]{:S(2)}) collective-permute-start(bf16[4,16,4]{2,1,0:T(8,128)(2,1)S(1)} %get-tuple-element.59), channel_id=1, source_target_pairs={{0,3},{1,2},{2,1},{3,0},{4,7},{5,6},{6,5},{7,4},{8,11},{9,10},{10,... | collective-permute-start | bytes 1544 | tf_op jit(solution)/shard_map/ppermute | solution.py:432
  3.9 0.7 %collective-permute-start.1 = (bf16[4,16,4]{2,1,0:T(8,128)(2,1)S(1)}, bf16[4,16,4]{2,1,0:T(8,128)(2,1)S(1)}, u32[]{:S(2)}, u32[]{:S(2)}) collective-permute-start(bf16[4,16,4]{2,1,0:T(8,128)(2,1)S(1)} %get-tuple-element.60), channel_id=1, source_target_pairs={{0,1},{1,0},{2,3},{3,2},{4,5},{5,4},{6,7},{7,6},{8,9},{9,8},{10,11... | collective-permute-start | bytes 1544 | tf_op jit(solution)/shard_map/ppermute | solution.py:433
  4.6 0.0 copy-start
  4.6 0.8 %collective-permute-done = bf16[4,16,4]{2,1,0:T(8,128)(2,1)S(1)} collective-permute-done((bf16[4,16,4]{2,1,0:T(8,128)(2,1)S(1)}, bf16[4,16,4]{2,1,0:T(8,128)(2,1)S(1)}, u32[]{:S(2)}, u32[]{:S(2)}) %collective-permute-start) | collective-permute-done | bytes 544 | tf_op jit(solution)/shard_map/ppermute | solution.py:432
  5.4 0.1 collective-permute-done.1
  5.4 0.1 broadcast_select_fusion.5
  5.5 0.0 copy-start.1
  5.6 2.5 %collective-permute-start.3 = (bf16[4,4,264]{2,1,0:T(4,128)(2,1)S(1)}, bf16[4,4,264]{2,1,0:T(4,128)(2,1)S(1)}, u32[]{:S(2)}, u32[]{:S(2)}) collective-permute-start(bf16[4,4,264]{2,1,0:T(4,128)(2,1)S(1)} %bitcast.32), channel_id=1, source_target_pairs={{0,4},{4,0},{8,12},{12,8},{1,5},{5,1},{9,13},{13,9},{2,6},{6,2},{1... | collective-permute-start | bytes 25352 | tf_op jit(solution)/shard_map/ppermute | solution.py:433
  8.1 2.5 %collective-permute-start.2 = (bf16[4,4,264]{2,1,0:T(4,128)(2,1)S(1)}, bf16[4,4,264]{2,1,0:T(4,128)(2,1)S(1)}, u32[]{:S(2)}, u32[]{:S(2)}) collective-permute-start(bf16[4,4,264]{2,1,0:T(4,128)(2,1)S(1)} %get-tuple-element.54), channel_id=1, source_target_pairs={{0,12},{4,8},{8,4},{12,0},{1,13},{5,9},{9,5},{13,1},{2,14},{6,10},... | collective-permute-start | bytes 25352 | tf_op jit(solution)/shard_map/ppermute | solution.py:432
  10.5 0.0 copy-start.2
  10.5 0.0 copy-start.3
  10.5 0.0 copy-start.4
  10.5 0.0 copy-start.5
  10.5 0.0 copy-done
  10.6 0.0 copy-done.1
  10.6 0.7 %copy-done.2 = bf16[64,2,3,3]{0,1,3,2:T(2,128)(2,1)S(1)} copy-done((bf16[64,2,3,3]{0,1,3,2:T(2,128)(2,1)S(1)}, bf16[64,2,3,3]{0,1,3,2:T(2,128)(2,1)}, u32[]{:S(2)}) %copy-start.2) | copy-done | bytes 2328
  11.2 0.0 copy-done.3
  11.2 0.0 copy-done.4
  11.2 0.0 copy-done.5
  11.2 0.4 weights.1
  11.6 0.0 collective-permute-done.3
  11.6 1.9 %collective-permute-done.2 = bf16[4,4,264]{2,1,0:T(4,128)(2,1)S(1)} collective-permute-done((bf16[4,4,264]{2,1,0:T(4,128)(2,1)S(1)}, bf16[4,4,264]{2,1,0:T(4,128)(2,1)S(1)}, u32[]{:S(2)}, u32[]{:S(2)}) %collective-permute-start.2) | collective-permute-done | bytes 8480 | tf_op jit(solution)/shard_map/ppermute | solution.py:432
  13.6 0.1 pad_maximum_fusion.refs_0_
  13.7 6.9 %backward.1 = (bf16[32,768]{1,0:T(8,128)(2,1)S(1)}, bf16[32,768]{1,0:T(8,128)(2,1)S(1)}, bf16[1280,384]{1,0:T(8,128)(2,1)S(1)}, bf16[1152,384]{1,0:T(8,128)(2,1)S(1)}) custom-call(f32[4,24,264]{2,1,0:T(8,128)S(1)} %pad_maximum_fusion.refs_0_, bf16[128,192]{1,0:T(8,128)(2,1)S(1)} %get-tuple-element.32.refs_1_, ...), custom_call_target="tpu_custom_call" | custom-call | tf_op jit(solution)/shard_map/backward/pallas_call | solution.py:517
  20.6 0.1 collective-permute-start.4
  20.6 1.2 %collective-permute-done.4 = bf16[32,768]{1,0:T(8,128)(2,1)S(1)} collective-permute-done((bf16[32,768]{1,0:T(8,128)(2,1)S(1)}, bf16[32,768]{1,0:T(8,128)(2,1)S(1)}, u32[]{:S(2)}, u32[]{:S(2)}) %collective-permute-start.4) | collective-permute-done | bytes 49184 | tf_op jit(solution)/shard_map/ppermute | solution.py:446
  21.9 1.6 %collective-permute-start.5 = (bf16[32,768]{1,0:T(8,128)(2,1)S(1)}, bf16[32,768]{1,0:T(8,128)(2,1)S(1)}, u32[]{:S(2)}, u32[]{:S(2)}) collective-permute-start(bf16[32,768]{1,0:T(8,128)(2,1)S(1)} %add_convert_fusion.2), channel_id=1, source_target_pairs={{0,2},{1,3},{2,0},{3,1},{4,6},{5,7},{6,4},{7,5},{8,10},{9,11},{10,... | collective-permute-start | bytes 147464 | tf_op jit(solution)/shard_map/ppermute | solution.py:446
  23.5 0.0 collective-permute-start.6
  23.5 2.0 %collective-permute-start.7 = (bf16[32,768]{1,0:T(8,128)(2,1)S(1)}, bf16[32,768]{1,0:T(8,128)(2,1)S(1)}, u32[]{:S(2)}, u32[]{:S(2)}) collective-permute-start(bf16[32,768]{1,0:T(8,128)(2,1)S(1)} %add_convert_fusion.2), channel_id=1, source_target_pairs={{0,6},{1,7},{2,4},{3,5},{4,2},{5,3},{6,0},{7,1},{8,14},{9,15},{10,... | collective-permute-start | bytes 147464 | tf_op jit(solution)/shard_map/ppermute | solution.py:446
  25.4 0.6 %collective-permute-done.5 = bf16[32,768]{1,0:T(8,128)(2,1)S(1)} collective-permute-done((bf16[32,768]{1,0:T(8,128)(2,1)S(1)}, bf16[32,768]{1,0:T(8,128)(2,1)S(1)}, u32[]{:S(2)}, u32[]{:S(2)}) %collective-permute-start.5) | collective-permute-done | bytes 49184 | tf_op jit(solution)/shard_map/ppermute | solution.py:446
  26.0 1.5 %collective-permute-done.6 = bf16[32,768]{1,0:T(8,128)(2,1)S(1)} collective-permute-done((bf16[32,768]{1,0:T(8,128)(2,1)S(1)}, bf16[32,768]{1,0:T(8,128)(2,1)S(1)}, u32[]{:S(2)}, u32[]{:S(2)}) %collective-permute-start.6) | collective-permute-done | bytes 49184 | tf_op jit(solution)/shard_map/ppermute | solution.py:446
  27.6 0.9 %collective-permute-done.7 = bf16[32,768]{1,0:T(8,128)(2,1)S(1)} collective-permute-done((bf16[32,768]{1,0:T(8,128)(2,1)S(1)}, bf16[32,768]{1,0:T(8,128)(2,1)S(1)}, u32[]{:S(2)}, u32[]{:S(2)}) %collective-permute-start.7) | collective-permute-done | bytes 49184 | tf_op jit(solution)/shard_map/ppermute | solution.py:446
  28.5 3.1 %collective-permute-start.8 = (bf16[32,768]{1,0:T(8,128)(2,1)S(1)}, bf16[32,768]{1,0:T(8,128)(2,1)S(1)}, u32[]{:S(2)}, u32[]{:S(2)}) collective-permute-start(bf16[32,768]{1,0:T(8,128)(2,1)S(1)} %add_convert_fusion.1), channel_id=1, source_target_pairs={{0,8},{1,9},{2,10},{3,11},{4,12},{5,13},{6,14},{7,15},{8,0},{9,1},... | collective-permute-start | bytes 147464 | tf_op jit(solution)/shard_map/ppermute | solution.py:446
  31.6 2.1 %collective-permute-done.8 = bf16[32,768]{1,0:T(8,128)(2,1)S(1)} collective-permute-done((bf16[32,768]{1,0:T(8,128)(2,1)S(1)}, bf16[32,768]{1,0:T(8,128)(2,1)S(1)}, u32[]{:S(2)}, u32[]{:S(2)}) %collective-permute-start.8) | collective-permute-done | bytes 49184 | tf_op jit(solution)/shard_map/ppermute | solution.py:446
  33.7 0.1 collective-permute-start.9
  33.8 0.1 sine_multiply_fusion.refs_1_
  33.8 1.7 %advance.1 = (f32[2,16,256]{2,1,0:T(8,128)}, f32[2,16,256]{2,1,0:T(8,128)}) custom-call(f32[4,24,264]{2,1,0:T(8,128)S(1)} %pad_maximum_fusion.refs_0_, f32[1,384]{1,0:T(1,128)S(1)} %sine_multiply_fusion.refs_1_, bf16[96,256]{1,0:T(8,128)(2,1)S(1)} %get-tuple-element.29.refs_2_, f32[32,128]{1,0:T(8,128)S(1)} %get-tuple-element.30.refs_3_, ...), custom_call_target="tpu_custom_call" | custom-call | tf_op jit(solution)/shard_map/advance/pallas_call | solution.py:543
  35.5 0.0 collective-permute-done.9.refs_1_
  35.5 0.9 %finish.1 = (f32[9,2,64]{2,1,0:T(2,128)}, f32[1,64]{1,0:T(1,128)}, f32[9,64,64]{2,1,0:T(8,128)}, f32[1,64]{1,0:T(1,128)}, f32[12,3,3,64]{3,2,1,0:T(4,128)}, /*index=5*/f32[1,12]{1,0:T(1,128)}) custom-call(bf16[32,768]{1,0:T(8,128)(2,1)S(1)} %add_convert_fusion.refs_0_, bf16[32,768]{1,0:T(8,128)(2,1)S(1)} %collective-permute-done.9.refs_1_, ...), custom_call_target="tpu_custom_call" | custom-call | tf_op jit(solution)/shard_map/finish/pallas_call | solution.py:558
  (8 shorter events, 0.1 us)
Async XLA Ops:
  0.6 0.8 %copy-start.6 = (f32[2,16,256]{2,1,0:T(8,128)S(1)}, f32[2,16,256]{2,1,0:T(8,128)}, u32[]{:S(2)}) copy-start(f32[2,16,256]{2,1,0:T(8,128)} %param.15) | copy-start | bytes 98308
  1.5 3.8 %collective-permute-start = (bf16[4,16,4]{2,1,0:T(8,128)(2,1)S(1)}, bf16[4,16,4]{2,1,0:T(8,128)(2,1)S(1)}, u32[]{:S(2)}, u32[]{:S(2)}) collective-permute-start(bf16[4,16,4]{2,1,0:T(8,128)(2,1)S(1)} %get-tuple-element.59), channel_id=1, source_target_pairs={{0,3},{1,2},{2,1},{3,0},{4,7},{5,6},{6,5},{7,4},{8,11},{9,10},{10,... | collective-permute-start | bytes 1544 | tf_op jit(solution)/shard_map/ppermute | solution.py:432
  3.9 1.5 %collective-permute-start.1 = (bf16[4,16,4]{2,1,0:T(8,128)(2,1)S(1)}, bf16[4,16,4]{2,1,0:T(8,128)(2,1)S(1)}, u32[]{:S(2)}, u32[]{:S(2)}) collective-permute-start(bf16[4,16,4]{2,1,0:T(8,128)(2,1)S(1)} %get-tuple-element.60), channel_id=1, source_target_pairs={{0,1},{1,0},{2,3},{3,2},{4,5},{5,4},{6,7},{7,6},{8,9},{9,8},{10,11... | collective-permute-start | bytes 1544 | tf_op jit(solution)/shard_map/ppermute | solution.py:433
  4.6 6.0 %copy-start = (bf16[64,64,3,3]{1,0,3,2:T(8,128)(2,1)S(1)}, bf16[64,64,3,3]{1,0,3,2:T(8,128)(2,1)}, u32[]{:S(2)}) copy-start(bf16[64,64,3,3]{1,0,3,2:T(8,128)(2,1)} %param.11) | copy-start | bytes 221188
  5.5 5.0 %copy-start.1 = (bf16[12,64,3,3]{1,3,2,0:T(4,128)(2,1)S(1)}, bf16[12,64,3,3]{1,3,2,0:T(4,128)(2,1)}, u32[]{:S(2)}) copy-start(bf16[12,64,3,3]{1,3,2,0:T(4,128)(2,1)} %param.13) | copy-start | bytes 41476
  5.6 6.0 %collective-permute-start.3 = (bf16[4,4,264]{2,1,0:T(4,128)(2,1)S(1)}, bf16[4,4,264]{2,1,0:T(4,128)(2,1)S(1)}, u32[]{:S(2)}, u32[]{:S(2)}) collective-permute-start(bf16[4,4,264]{2,1,0:T(4,128)(2,1)S(1)} %bitcast.32), channel_id=1, source_target_pairs={{0,4},{4,0},{8,12},{12,8},{1,5},{5,1},{9,13},{13,9},{2,6},{6,2},{1... | collective-permute-start | bytes 25352 | tf_op jit(solution)/shard_map/ppermute | solution.py:433
  8.1 5.5 %collective-permute-start.2 = (bf16[4,4,264]{2,1,0:T(4,128)(2,1)S(1)}, bf16[4,4,264]{2,1,0:T(4,128)(2,1)S(1)}, u32[]{:S(2)}, u32[]{:S(2)}) collective-permute-start(bf16[4,4,264]{2,1,0:T(4,128)(2,1)S(1)} %get-tuple-element.54), channel_id=1, source_target_pairs={{0,12},{4,8},{8,4},{12,0},{1,13},{5,9},{9,5},{13,1},{2,14},{6,10},... | collective-permute-start | bytes 25352 | tf_op jit(solution)/shard_map/ppermute | solution.py:432
  10.5 0.7 %copy-start.2 = (bf16[64,2,3,3]{0,1,3,2:T(2,128)(2,1)S(1)}, bf16[64,2,3,3]{0,1,3,2:T(2,128)(2,1)}, u32[]{:S(2)}) copy-start(bf16[64,2,3,3]{0,1,3,2:T(2,128)(2,1)} %param.9) | copy-start | bytes 6916
  10.5 0.7 %copy-start.3 = (f32[64]{0:T(128)S(1)}, f32[64]{0:T(128)}, u32[]{:S(2)}) copy-start(f32[64]{0:T(128)} %param.10) | copy-start | bytes 772
  10.5 0.7 %copy-start.4 = (f32[64]{0:T(128)S(1)}, f32[64]{0:T(128)}, u32[]{:S(2)}) copy-start(f32[64]{0:T(128)} %param.12) | copy-start | bytes 772
  10.5 0.7 %copy-start.5 = (f32[12]{0:T(128)S(1)}, f32[12]{0:T(128)}, u32[]{:S(2)}) copy-start(f32[12]{0:T(128)} %param.14) | copy-start | bytes 148
  20.6 1.3 %collective-permute-start.4 = (bf16[32,768]{1,0:T(8,128)(2,1)S(1)}, bf16[32,768]{1,0:T(8,128)(2,1)S(1)}, u32[]{:S(2)}, u32[]{:S(2)}) collective-permute-start(bf16[32,768]{1,0:T(8,128)(2,1)S(1)} %get-tuple-element.43), channel_id=1, source_target_pairs={{0,1},{1,0},{2,3},{3,2},{4,5},{5,4},{6,7},{7,6},{8,9},{9,8},{10,11... | collective-permute-start | bytes 147464 | tf_op jit(solution)/shard_map/ppermute | solution.py:446
  21.9 4.2 %collective-permute-start.5 = (bf16[32,768]{1,0:T(8,128)(2,1)S(1)}, bf16[32,768]{1,0:T(8,128)(2,1)S(1)}, u32[]{:S(2)}, u32[]{:S(2)}) collective-permute-start(bf16[32,768]{1,0:T(8,128)(2,1)S(1)} %add_convert_fusion.2), channel_id=1, source_target_pairs={{0,2},{1,3},{2,0},{3,1},{4,6},{5,7},{6,4},{7,5},{8,10},{9,11},{10,... | collective-permute-start | bytes 147464 | tf_op jit(solution)/shard_map/ppermute | solution.py:446
  23.5 4.1 %collective-permute-start.6 = (bf16[32,768]{1,0:T(8,128)(2,1)S(1)}, bf16[32,768]{1,0:T(8,128)(2,1)S(1)}, u32[]{:S(2)}, u32[]{:S(2)}) collective-permute-start(bf16[32,768]{1,0:T(8,128)(2,1)S(1)} %add_convert_fusion.2), channel_id=1, source_target_pairs={{0,4},{1,5},{2,6},{3,7},{4,0},{5,1},{6,2},{7,3},{8,12},{9,13},{10,... | collective-permute-start | bytes 147464 | tf_op jit(solution)/shard_map/ppermute | solution.py:446
  23.5 5.0 %collective-permute-start.7 = (bf16[32,768]{1,0:T(8,128)(2,1)S(1)}, bf16[32,768]{1,0:T(8,128)(2,1)S(1)}, u32[]{:S(2)}, u32[]{:S(2)}) collective-permute-start(bf16[32,768]{1,0:T(8,128)(2,1)S(1)} %add_convert_fusion.2), channel_id=1, source_target_pairs={{0,6},{1,7},{2,4},{3,5},{4,2},{5,3},{6,0},{7,1},{8,14},{9,15},{10,... | collective-permute-start | bytes 147464 | tf_op jit(solution)/shard_map/ppermute | solution.py:446
  28.5 5.2 %collective-permute-start.8 = (bf16[32,768]{1,0:T(8,128)(2,1)S(1)}, bf16[32,768]{1,0:T(8,128)(2,1)S(1)}, u32[]{:S(2)}, u32[]{:S(2)}) collective-permute-start(bf16[32,768]{1,0:T(8,128)(2,1)S(1)} %add_convert_fusion.1), channel_id=1, source_target_pairs={{0,8},{1,9},{2,10},{3,11},{4,12},{5,13},{6,14},{7,15},{8,0},{9,1},... | collective-permute-start | bytes 147464 | tf_op jit(solution)/shard_map/ppermute | solution.py:446
  33.7 1.8 %collective-permute-start.9 = (bf16[32,768]{1,0:T(8,128)(2,1)S(1)}, bf16[32,768]{1,0:T(8,128)(2,1)S(1)}, u32[]{:S(2)}, u32[]{:S(2)}) collective-permute-start(bf16[32,768]{1,0:T(8,128)(2,1)S(1)} %add_convert_fusion.refs_0_), channel_id=1, source_target_pairs={{0,1},{1,0},{2,3},{3,2},{4,5},{5,4},{6,7},{7,6},{8,9},{9,8},{10,11... | collective-permute-start | bytes 147464 | tf_op jit(solution)/shard_map/ppermute | solution.py:446

commit v2 on v1

--- a/solution.py
+++ b/solution.py
@@ -42,10 +42,34 @@
     return 0.5 * jnp.tanh(0.5 * linear) + 0.5
 
 
-def store_shifted(refs, at, value):
-    rows = value.shape[0]
-    for b in range(3):
-        refs[b, at : at + rows, :] = shift(value, 0, b - 1).astype(refs.dtype)
+class Rows:
+    def __init__(self, size, *pieces):
+        self.size = size
+        self.pieces = pieces
+
+    def get(self, lo, hi, lead=()):
+        parts = []
+        for start, stop, ref in self.pieces:
+            first, last = max(lo, start), min(hi, stop)
+            if first < last:
+                rows = slice((first - start) * self.size, (last - start) * self.size)
+                parts.append((first, ref[(*lead, rows, slice(None))]))
+        parts = [part for _, part in sorted(parts, key=lambda item: item[0])]
+        return parts[0] if len(parts) == 1 else jnp.concatenate(parts, axis=0)
+
+    def put(self, lo, value, lead=()):
+        for start, stop, ref in self.pieces:
+            if start <= lo < stop:
+                rows = slice((lo - start) * self.size, (lo - start) * self.size + value.shape[0])
+                ref[(*lead, rows, slice(None))] = value
+
+    def put_shifted(self, lo, value, lead=()):
+        value = value.astype(bf16)
+        for b in range(3):
+            self.put(lo, shift(value, 0, b - 1), (*lead, b))
+
+    def window(self, lo, hi, lead=()):
+        return jnp.concatenate([self.get(lo, hi, (*lead, b)) for b in range(3)], axis=0)
 
 
 def put_plane(planes, k, stride, value):
@@ -90,46 +114,18 @@
     return jnp.sum(part.T, axis=0, keepdims=True)
 
 
-def backward_kernel(
-    rows,
-    cols,
-    ext_ref,
-    w_in_ref,
-    w_mid_ref,
-    w_mid_t_ref,
-    w_out_t_ref,
-    b_in_ref,
-    b_mid_ref,
-    core_ref,
-    keep_ref,
-    send_ref,
-    act_two_ref,
-    grad_one_ref,
-    pay,
-    stage,
-    state_in,
-    head_in,
-    act_one,
-    slope_one,
-    grad_two,
-    acc_mid,
-    acc_small,
-    bias_acc,
-):
+def prepare(first, rows, cols, ext_ref, stage, planes, state_in, state_rows, head_rows):
+    count = ext_ref.shape[1]
     height, width = stage.shape[1], stage.shape[2]
-    deep = rows + 2 * halo
     stage[...] = jnp.zeros(stage.shape, f32)
-    stage[:, 0:deep, 0 : cols + 2 * halo] = ext_ref[...]
+    stage[:, 0:count, 0 : cols + 2 * halo] = ext_ref[...]
     w0, w1, c0, c1 = stage[0], stage[1], stage[2], stage[3]
-    lane = lax.broadcasted_iota(jnp.int32, (1, width), 1)
-    own_cols = (lane >= halo) & (lane < halo + cols)
-
-    planes = head_in
+
     planes[...] = jnp.zeros(planes.shape, f32)
     put_plane(planes, 0, slot, w0)
     put_plane(planes, 1, slot, w1)
-    for r in range(0, deep, 2):
-        store_shifted(state_in.at[0], r * slot, take_rows(planes, r * slot, 2 * slot))
+    for r in state_rows:
+        state_in.put_shifted(r, take_rows(planes, (r - first) * slot, 2 * slot), (0,))
 
     normal_x, normal_y = faces(w0, w1)
     t0, t1 = shifted_fields(w0), shifted_fields(w1)
@@ -137,8 +133,9 @@
     fx1 = -advection * (c1 - shift(c1, 1, 0)) * normal_x
     fy0 = -advection * (c0 - shift(c0, 0, 1)) * normal_y
     fy1 = -advection * (c1 - shift(c1, 0, 1)) * normal_y
-    row_id = lax.broadcasted_iota(jnp.int32, (height, width), 0)
-    own = own_cols & (row_id >= halo) & (row_id < halo + rows)
+    lane = lax.broadcasted_iota(jnp.int32, (height, width), 1)
+    row_id = lax.broadcasted_iota(jnp.int32, (height, width), 0) + first
+    own = (lane >= halo) & (lane < halo + cols) & (row_id >= halo) & (row_id < halo + rows)
     sums = []
     for at, taps, g0, g1 in ((0, taps_x, fx0, fx1), (6, taps_y, fy0, fy1)):
         raw = [g0 * t0[tap] + g1 * t1[tap] for tap in taps]
@@ -147,43 +144,55 @@
             value = raw[k] - mean
             put_plane(planes, at + k, slot, value)
             sums.append(jnp.sum(jnp.where(own, value, 0.0), axis=0, keepdims=True))
-    for r in range(0, deep, 2):
-        store_shifted(state_in.at[1], r * slot, take_rows(planes, r * slot, 2 * slot))
-    bias_out = jnp.concatenate(sums + [jnp.zeros((128 - coef, width), f32)], axis=0)
+    for r in head_rows:
+        state_in.put_shifted(r, take_rows(planes, (r - first) * slot, 2 * slot), (1,))
+    return sums
+
+
+def layers(
+    rows,
+    cols,
+    groups,
+    refs,
+    state_in,
+    act_one,
+    slope_one,
+    grad_two,
+    act_two,
+    grad_one,
+    acc_mid,
+    acc_small,
+    bias_acc,
+):
+    w_in_ref, w_mid_ref, w_mid_t_ref, w_out_t_ref, b_in_ref, b_mid_ref = refs
+    width = bias_acc.shape[2]
+    lane = lax.broadcasted_iota(jnp.int32, (1, width), 1)
+    own_cols = (lane >= halo) & (lane < halo + cols)
+    groups_one, groups_two, groups_back, groups_in = groups
 
     w_in = w_in_ref[...]
     b_in = b_in_ref[:, 0:1]
-    for r in range(1, deep - 1, 2):
-        fed = jnp.concatenate(
-            [state_in[0, b, (r - 1) * slot : (r + 3) * slot, :] for b in range(3)], axis=0
-        )
-        linear = mm(w_in, fed) + b_in
+    for r in groups_one:
+        linear = mm(w_in, state_in.window(r - 1, r + 3, (0,))) + b_in
         sigma = sigma_of(linear)
         act = linear * sigma
-        store_shifted(act_one, (r - 1) * hid, act)
-        slope_one[(r - 1) * hid : (r + 1) * hid, :] = sigma + act * (1.0 - sigma)
+        act_one.put_shifted(r, act)
+        slope_one.put(r, sigma + act * (1.0 - sigma))
 
     b_mid = b_mid_ref[:, 0:1]
     w_out_t = w_out_t_ref[...]
-    bias_acc[...] = jnp.zeros(bias_acc.shape, f32)
-    acc_mid[...] = jnp.zeros(acc_mid.shape, f32)
-    acc_small[...] = jnp.zeros(acc_small.shape, f32)
-    for r in range(2, deep - 2, 2):
-        mine = halo <= r < halo + rows
-        linear = b_mid
-        window = [act_one[b, (r - 2) * hid : (r + 2) * hid, :] for b in range(3)]
-        for b in range(3):
-            linear = linear + mm(w_mid_ref[b], window[b])
+    w_mid = jnp.concatenate([w_mid_ref[b] for b in range(3)], axis=1)
+    w_mid_t = jnp.concatenate([w_mid_t_ref[b] for b in range(3)], axis=1)
+    for r in groups_two:
+        window = [act_one.get(r - 1, r + 3, (b,)) for b in range(3)]
+        linear = mm(w_mid, jnp.concatenate(window, axis=0)) + b_mid
         sigma = sigma_of(linear)
         act = linear * sigma
-        act_short = act.astype(bf16)
-        act_two_ref[(r - 2) * hid : r * hid, :] = act_short
-        fed = jnp.concatenate(
-            [state_in[1, b, (r - 1) * slot : (r + 3) * slot, :] for b in range(3)], axis=0
-        )
+        act_two.put(r, act.astype(bf16))
+        fed = state_in.window(r - 1, r + 3, (1,))
         grad = mm(w_out_t, fed) * (sigma + act * (1.0 - sigma))
-        store_shifted(grad_two, (r - 2) * hid, grad)
-        if mine:
+        grad_two.put_shifted(r, grad)
+        if halo <= r < halo + rows:
             kept = jnp.where(own_cols, grad, 0.0)
             bias_acc[0] += kept
             kept = kept.astype(bf16)
@@ -191,26 +200,92 @@
                 acc_mid[b] += mm_nt(kept, window[b])
             acc_small[0] += mm_nt(fed, jnp.where(own_cols, act, 0.0).astype(bf16))
 
-    for r in range(3, deep - 3, 2):
-        grad = mm(w_mid_t_ref[0], grad_two[0, (r - 3) * hid : (r + 1) * hid, :])
-        for b in (1, 2):
-            grad = grad + mm(w_mid_t_ref[b], grad_two[b, (r - 3) * hid : (r + 1) * hid, :])
-        grad = grad * slope_one[(r - 1) * hid : (r + 1) * hid, :]
-        grad_one_ref[(r - 3) * hid : (r - 1) * hid, :] = grad.astype(bf16)
+    for r in groups_back:
+        grad = mm(w_mid_t, grad_two.window(r - 1, r + 3)) * slope_one.get(r, r + 2)
+        grad_one.put(r, grad.astype(bf16))
         kept = jnp.where(own_cols, grad, 0.0)
-        if r == 3:
+        if r < halo:
             bias_acc[1, hid:, :] += kept[hid:, :]
-        elif r == deep - 5:
+        elif r + 2 > halo + rows:
             bias_acc[1, :hid, :] += kept[:hid, :]
         else:
             bias_acc[1] += kept
-    for r in range(halo, halo + rows, 2):
-        kept = grad_one_ref[(r - 3) * hid : (r - 1) * hid, :]
-        kept = jnp.where(own_cols, kept, jnp.zeros((), bf16))
-        fed = jnp.concatenate(
-            [state_in[0, b, (r - 1) * slot : (r + 3) * slot, :] for b in range(3)], axis=0
-        )
-        acc_small[1] += mm_nt(fed, kept)
+    for r in groups_in:
+        kept = jnp.where(own_cols, grad_one.get(r, r + 2), jnp.zeros((), bf16))
+        acc_small[1] += mm_nt(state_in.window(r - 1, r + 3, (0,)), kept)
+
+
+def inner_kernel(rows, cols, ext_ref, *refs):
+    weight_refs, refs = refs[:6], refs[6:]
+    act_one, slope_one, grad_two, act_two, grad_one, acc_mid, acc_small, bias_acc, *refs = refs
+    stage, planes, state_in = refs
+    low, high = halo, halo + rows
+    state_in = Rows(slot, (low, high, state_in))
+    acc_mid[...] = jnp.zeros(acc_mid.shape, f32)
+    acc_small[...] = jnp.zeros(acc_small.shape, f32)
+    bias_acc[...] = jnp.zeros(bias_acc.shape, f32)
+    pairs = range(low, high, 2)
+    prepare(low, rows, cols, ext_ref, stage, planes, state_in, pairs, pairs)
+    groups = [range(low + k, high - k, 2) for k in (1, 2, 3, 4)]
+    layers(
+        rows,
+        cols,
+        groups,
+        weight_refs,
+        state_in,
+        Rows(hid, (low + 1, high - 1, act_one)),
+        Rows(hid, (low + 1, high - 1, slope_one)),
+        Rows(hid, (low + 2, high - 2, grad_two)),
+        Rows(hid, (low + 2, high - 2, act_two)),
+        Rows(hid, (low + 3, high - 3, grad_one)),
+        acc_mid,
+        acc_small,
+        bias_acc,
+    )
+
+
+def split_rows(size, first, low, high, last, lower_ref, inner_ref, upper_ref):
+    return Rows(size, (first, low, lower_ref), (low, high, inner_ref), (high, last, upper_ref))
+
+
+def outer_kernel(rows, cols, ext_ref, *refs):
+    weight_refs, core_ref, refs = refs[:6], refs[6], refs[7:]
+    act_one_in, slope_one_in, grad_two_in, grad_one_in, acc_mid_in, acc_small_in, bias_in, *refs = refs
+    keep_ref, send_ref, act_two, grad_one, *refs = refs
+    pay, stage, planes, state_in, act_one, slope_one, grad_two, acc_mid, acc_small, bias_acc = refs
+    low, high, deep = halo, halo + rows, rows + 2 * halo
+    acc_mid[...] = acc_mid_in[...]
+    acc_small[...] = acc_small_in[...]
+    bias_acc[...] = bias_in[...]
+    state_in = Rows(slot, (0, deep, state_in))
+    state_rows = [r for r in range(0, deep, 2) if r < low + 6 or r + 2 > high - 6]
+    head_rows = [r for r in range(0, deep, 2) if r < low + 4 or r + 2 > high - 4]
+    sums = prepare(0, rows, cols, ext_ref, stage, planes, state_in, state_rows, head_rows)
+    bias_out = jnp.concatenate(sums + [jnp.zeros((128 - coef, stage.shape[2]), f32)], axis=0)
+    groups = [
+        [*range(k, low + k, 2), *range(high - k, deep - k, 2)] for k in (1, 2, 3)
+    ]
+    groups.append([low, low + 2, high - 4, high - 2])
+
+    def both(k, edge, inner):
+        edges = [edge.at[i] for i in range(2)]
+        return split_rows(hid, k, low + k, high - k, deep - k, edges[0], inner, edges[1])
+
+    layers(
+        rows,
+        cols,
+        groups,
+        weight_refs,
+        state_in,
+        both(1, act_one, act_one_in),
+        both(1, slope_one, slope_one_in),
+        both(2, grad_two, grad_two_in),
+        Rows(hid, (2, low + 2, act_two.at[0]), (high - 2, deep - 2, act_two.at[1])),
+        both(3, grad_one, grad_one_in),
+        acc_mid,
+        acc_small,
+        bias_acc,
+    )
 
     for b in range(3):
         total = acc_mid[b, :hid, : 3 * hid] + acc_mid[b, hid:, hid:]
@@ -256,16 +331,21 @@
     w_head_ref,
     b_head_ref,
     w_in_t_ref,
-    act_two_ref,
-    grad_one_ref,
+    act_two_in,
+    act_two_edge,
+    grad_one_in,
+    grad_one_edge,
     new_ref,
     grad_ref,
     stage,
     head,
     back,
 ):
-    height, width = stage.shape[1], stage.shape[2]
-    deep = rows + 2 * halo
+    low, high, deep = halo, halo + rows, rows + 2 * halo
+    act_two, grad_one = (
+        split_rows(hid, k, low + k, high - k, deep - k, edge.at[0], inner, edge.at[1])
+        for k, inner, edge in ((2, act_two_in, act_two_edge), (3, grad_one_in, grad_one_edge))
+    )
     stage[...] = jnp.zeros(stage.shape, f32)
     stage[:, 0:deep, 0 : cols + 2 * halo] = ext_ref[...]
     w0, w1, c0, c1 = stage[0], stage[1], stage[2], stage[3]
@@ -274,7 +354,7 @@
     w_head = w_head_ref[...]
     b_head = b_head_ref[:, 0:1]
     for r in range(3, deep - 3, 2):
-        part = mm(w_head, act_two_ref[(r - 3) * hid : (r + 1) * hid, :])
+        part = mm(w_head, act_two.get(r - 1, r + 3))
         size = 2 * slot
         out = b_head
         for b in range(3):
@@ -282,7 +362,7 @@
         put_rows(head, r * slot, out)
     w_in_t = w_in_t_ref[...]
     for r in range(halo, halo + rows, 2):
-        part = mm(w_in_t, grad_one_ref[(r - 4) * hid : r * hid, :])
+        part = mm(w_in_t, grad_one.get(r - 1, r + 3))
         out = part[16:32]
         for b in (0, 2):
             out = out + shift(part[b * 16 : (b + 1) * 16], 0, b - 1)
@@ -360,23 +440,41 @@
     b_out_ref[...] = slots[10][4:5, :coef]
 
 
-def weights_kernel(
-    k_in_ref,
-    k_mid_ref,
-    k_out_ref,
-    b_in_ref,
-    b_mid_ref,
-    b_out_ref,
-    w_in_ref,
-    w_mid_ref,
-    w_mid_t_ref,
-    w_out_t_ref,
-    w_head_ref,
-    w_in_t_ref,
-    c_in_ref,
-    c_mid_ref,
-    c_head_ref,
-):
+def in_hbm(array):
+    return pltpu.with_memory_space_constraint(array, pltpu.HBM)
+
+
+def fetched(sources, targets, sems):
+    copies = [
+        pltpu.make_async_copy(source, target, sems.at[k])
+        for k, (source, target) in enumerate(zip(sources, targets))
+    ]
+    for copy in copies:
+        copy.start()
+    for copy in copies:
+        copy.wait()
+
+
+def pack_kernel(even_ref, velocity_ref, cotangent_ref, fields_ref, far_ref, near_ref, sems):
+    cols = fields_ref.shape[2]
+    fetched(
+        (velocity_ref, cotangent_ref), (fields_ref.at[0:2], fields_ref.at[2:4]), sems
+    )
+    first = fields_ref[:, :, 0:halo].astype(bf16)
+    last = fields_ref[:, :, cols - halo : cols].astype(bf16)
+    even = even_ref[0] == 1
+    far_ref[...] = jnp.where(even, first, last)
+    near_ref[...] = jnp.where(even, last, first)
+
+
+def weights_kernel(*refs):
+    sources, refs = refs[:6], refs[6:]
+    outs, (*inputs, sems) = refs[:9], refs[9:]
+    fetched(sources, inputs, sems)
+    k_in_ref, k_mid_ref, k_out_ref, b_in_ref, b_mid_ref, b_out_ref = inputs
+    w_in_ref, w_mid_ref, w_mid_t_ref, w_out_t_ref, w_head_ref, w_in_t_ref, *outs = outs
+    c_in_ref, c_mid_ref, c_head_ref = outs
+
     def band(block, upper):
         none = jnp.zeros(block[0].shape, f32)
         return jnp.concatenate([none, *block] if upper else [*block, none], axis=1)
@@ -420,22 +518,23 @@
     c_head_ref[...] = jnp.broadcast_to(bias, (128, 128)).T[: 2 * slot]
 
 
-def extended(fields):
-    short = fields.astype(bf16)
-    for axis, dim in (("gy", 2), ("gx", 1)):
-        count = lax.axis_size(axis)
-        size = short.shape[dim]
-        even = lax.axis_index(axis) % 2 == 0
-        first = lax.slice_in_dim(short, 0, halo, axis=dim)
-        last = lax.slice_in_dim(short, size - halo, size, axis=dim)
-        far_pairs = [(i, (i + 1 if i % 2 else i - 1) % count) for i in range(count)]
-        far = lax.ppermute(jnp.where(even, first, last), axis, far_pairs)
-        near = lax.ppermute(jnp.where(even, last, first), axis, [(i, i ^ 1) for i in range(count)])
-        low = jnp.where(even, far, near)
-        high = jnp.where(even, near, far)
-        short = jnp.concatenate([low, short, high], axis=dim)
-        fields = jnp.concatenate([low.astype(f32), fields, high.astype(f32)], axis=dim)
-    return fields
+def edges(fields, axis, dim):
+    size = fields.shape[dim]
+    even = lax.axis_index(axis) % 2 == 0
+    first = lax.slice_in_dim(fields, 0, halo, axis=dim).astype(bf16)
+    last = lax.slice_in_dim(fields, size - halo, size, axis=dim).astype(bf16)
+    return jnp.where(even, first, last), jnp.where(even, last, first)
+
+
+def widened(fields, far, near, axis, dim):
+    count = lax.axis_size(axis)
+    even = lax.axis_index(axis) % 2 == 0
+    far_pairs = [(i, (i + 1 if i % 2 else i - 1) % count) for i in range(count)]
+    far = lax.ppermute(far, axis, far_pairs)
+    near = lax.ppermute(near, axis, [(i, i ^ 1) for i in range(count)])
+    low = jnp.where(even, far, near).astype(f32)
+    high = jnp.where(even, near, far).astype(f32)
+    return jnp.concatenate([low, fields, high], axis=dim)
 
 
 def swap(value, rows, cols):
@@ -453,7 +552,7 @@
     return sums[0].astype(bf16)
 
 
-def summed(keep, send):
+def summed(keep, send, beside):
     half = added(keep, swap(send, 0, 1))
     steps = [(0, 1 << k) for k in range(1, lax.axis_size("gy").bit_length() - 1)]
     steps += [(1 << k, 0) for k in range(lax.axis_size("gx").bit_length() - 1)]
@@ -468,9 +567,12 @@
             )
             steps = steps[2:]
         else:
-            half = added(half, swap(half, *steps[0]))
+            arrived = swap(half, *steps[0])
             steps = steps[1:]
-    return half, swap(half, 0, 1)
+            if not steps:
+                arrived, beside = lax.optimization_barrier((arrived, beside))
+            half = added(half, arrived)
+    return half, swap(half, 0, 1), beside
 
 
 def per_device(velocity, kernel_in, bias_in, kernel_mid, bias_mid, kernel_out, bias_out, cotangent):
@@ -481,10 +583,11 @@
     height = deep
     width = -(-(cols + 2 * halo) // 128) * 128
     vmem = pl.BlockSpec(memory_space=pltpu.VMEM)
-    params = pltpu.CompilerParams(vmem_limit_bytes=48 << 20)
+    params = pltpu.CompilerParams(vmem_limit_bytes=18 << 20)
 
     core = (lax.axis_index("gy") % 2).astype(jnp.int32).reshape(1)
     smem = pl.BlockSpec(memory_space=pltpu.SMEM)
+    hbm = pl.BlockSpec(memory_space=pltpu.HBM)
     w_in, w_mid, w_mid_t, w_out_t, w_head, w_in_t, b_in, b_mid, b_head = pl.pallas_call(
         weights_kernel,
         out_shape=(
@@ -498,52 +601,99 @@
             jax.ShapeDtypeStruct((128, 128), f32),
             jax.ShapeDtypeStruct((2 * slot, 128), f32),
         ),
-        in_specs=[vmem] * 6,
+        in_specs=[hbm] * 6,
         out_specs=(vmem,) * 9,
+        scratch_shapes=[
+            pltpu.VMEM((9, 2, hid), bf16),
+            pltpu.VMEM((9, hid, hid), bf16),
+            pltpu.VMEM((coef, 3, 3, hid), bf16),
+            pltpu.VMEM((1, hid), f32),
+            pltpu.VMEM((1, hid), f32),
+            pltpu.VMEM((1, coef), f32),
+            pltpu.SemaphoreType.DMA((6,)),
+        ],
         compiler_params=params,
         name="weights",
     )(
-        jnp.transpose(kernel_in, (2, 3, 1, 0)).reshape(9, 2, hid),
-        jnp.transpose(kernel_mid, (2, 3, 0, 1)).reshape(9, hid, hid),
-        jnp.transpose(kernel_out, (0, 2, 3, 1)),
-        bias_in[None, :],
-        bias_mid[None, :],
-        bias_out[None, :],
+        in_hbm(jnp.transpose(kernel_in, (2, 3, 1, 0)).reshape(9, 2, hid)),
+        in_hbm(jnp.transpose(kernel_mid, (2, 3, 0, 1)).reshape(9, hid, hid)),
+        in_hbm(jnp.transpose(kernel_out, (0, 2, 3, 1))),
+        in_hbm(bias_in[None, :]),
+        in_hbm(bias_mid[None, :]),
+        in_hbm(bias_out[None, :]),
     )
     columns = lax.iota(jnp.int32, width) - halo + lax.axis_index("gy") * cols
     forcing = forcing_amp * jnp.sin(2.0 * math.pi * forcing_wave * columns.astype(f32) / ny_total)
-    ext = extended(jnp.concatenate([velocity, cotangent], axis=0))
-
-    keep, send, act_two, grad_one = pl.pallas_call(
-        lambda *refs: backward_kernel(rows, cols, *refs),
+    even = (lax.axis_index("gy") % 2 == 0).astype(jnp.int32).reshape(1)
+    edge = jax.ShapeDtypeStruct((4, rows, halo), bf16)
+    fields, far, near = pl.pallas_call(
+        pack_kernel,
+        out_shape=(jax.ShapeDtypeStruct((4, rows, cols), f32), edge, edge),
+        in_specs=[smem, hbm, hbm],
+        out_specs=(vmem,) * 3,
+        scratch_shapes=[pltpu.SemaphoreType.DMA((2,))],
+        compiler_params=params,
+        name="pack",
+    )(even, in_hbm(velocity), in_hbm(cotangent))
+    wide = widened(fields, far, near, "gy", 2)
+    maps = (w_in, w_mid, w_mid_t, w_out_t, b_in, b_mid)
+    far_near, maps = lax.optimization_barrier((edges(wide, "gx", 1), maps))
+    ext = widened(wide, *far_near, "gx", 1)
+
+    accs = (
+        jax.ShapeDtypeStruct((3, 2 * hid, 4 * hid), f32),
+        jax.ShapeDtypeStruct((2, 12 * slot, 2 * hid), f32),
+        jax.ShapeDtypeStruct((2, 2 * hid, width), f32),
+    )
+    act_one, slope_one, grad_two, act_two_in, grad_one_in, *totals = pl.pallas_call(
+        lambda *refs: inner_kernel(rows, cols, *refs),
+        out_shape=(
+            jax.ShapeDtypeStruct((3, (rows - 2) * hid, width), bf16),
+            jax.ShapeDtypeStruct(((rows - 2) * hid, width), f32),
+            jax.ShapeDtypeStruct((3, (rows - 4) * hid, width), bf16),
+            jax.ShapeDtypeStruct(((rows - 4) * hid, width), bf16),
+            jax.ShapeDtypeStruct(((rows - 6) * hid, width), bf16),
+            *accs,
+        ),
+        in_specs=[vmem] * 7,
+        out_specs=(vmem,) * 8,
+        scratch_shapes=[
+            pltpu.VMEM((4, rows, width), f32),
+            pltpu.VMEM((width // 128, rows * slot, 128), f32),
+            pltpu.VMEM((2, 3, rows * slot, width), bf16),
+        ],
+        compiler_params=params,
+        name="inner",
+    )(wide, *maps)
+
+    keep, send, act_two_edge, grad_one_edge = pl.pallas_call(
+        lambda *refs: outer_kernel(rows, cols, *refs),
         out_shape=(
             jax.ShapeDtypeStruct((hid // 2, 12 * hid), bf16),
             jax.ShapeDtypeStruct((hid // 2, 12 * hid), bf16),
-            jax.ShapeDtypeStruct(((deep - 4) * hid, width), bf16),
-            jax.ShapeDtypeStruct(((deep - 6) * hid, width), bf16),
+            jax.ShapeDtypeStruct((2, halo * hid, width), bf16),
+            jax.ShapeDtypeStruct((2, halo * hid, width), bf16),
         ),
-        in_specs=[vmem] * 7 + [smem],
+        in_specs=[vmem] * 7 + [smem] + [vmem] * 7,
         out_specs=(vmem,) * 4,
         scratch_shapes=[
             pltpu.VMEM((2, hid // 2, 12 * hid), bf16),
-            pltpu.VMEM((4, height, width), f32),
+            pltpu.VMEM((4, deep, width), f32),
+            pltpu.VMEM((width // 128, deep * slot, 128), f32),
             pltpu.VMEM((2, 3, deep * slot, width), bf16),
-            pltpu.VMEM((width // 128, deep * slot, 128), f32),
-            pltpu.VMEM((3, (deep - 2) * hid, width), bf16),
-            pltpu.VMEM(((deep - 2) * hid, width), f32),
-            pltpu.VMEM((3, (deep - 4) * hid, width), bf16),
-            pltpu.VMEM((3, 2 * hid, 4 * hid), f32),
-            pltpu.VMEM((2, 12 * slot, 2 * hid), f32),
-            pltpu.VMEM((2, 2 * hid, width), f32),
+            pltpu.VMEM((2, 3, halo * hid, width), bf16),
+            pltpu.VMEM((2, halo * hid, width), f32),
+            pltpu.VMEM((2, 3, halo * hid, width), bf16),
+            *(pltpu.VMEM(acc.shape, f32) for acc in accs),
         ],
         compiler_params=params,
-        name="backward",
-    )(ext, w_in, w_mid, w_mid_t, w_out_t, b_in, b_mid, core)
+        name="outer",
+    )(ext, *maps, core, act_one, slope_one, grad_two, grad_one_in, *totals)
 
     new_velocity, grad_velocity = pl.pallas_call(
         lambda *refs: advance_kernel(rows, cols, *refs),
         out_shape=(jax.ShapeDtypeStruct(velocity.shape, f32),) * 2,
-        in_specs=[vmem] * 7,
+        in_specs=[vmem] * 9,
         out_specs=(vmem,) * 2,
         scratch_shapes=[
             pltpu.VMEM((4, height, width), f32),
@@ -552,9 +702,11 @@
         ],
         compiler_params=params,
         name="advance",
-    )(ext, forcing[None, :], w_head, b_head, w_in_t, act_two, grad_one)
-
-    mine, other = summed(keep, send)
+    )(ext, forcing[None, :], w_head, b_head, w_in_t, act_two_in, act_two_edge, grad_one_in, grad_one_edge)
+
+    mine, other, (new_velocity, grad_velocity) = summed(
+        keep, send, (new_velocity, grad_velocity)
+    )
     g_in, gb_in, g_mid, gb_mid, g_out, gb_out = pl.pallas_call(
         lambda *refs: finish_kernel(1.0 / math.sqrt(cell_count), *refs),
         out_shape=(

time: 36.7 us -> 35.2 us (0.959)
  starting transfers between devices: 14.8 us -> 10.9 us
  Pallas kernels: 9.81 us -> 12.2 us
  waiting for transfers between devices: 9.09 us -> 10.7 us
  local copies, waits for them, and re-layouts: 1.46 us -> 0 us
    ppermute x6, waiting for transfers between devices: 6.31 us -> 10.6 us  [swap(): return lax.ppermute(value, ('gx', 'gy'), pairs)]
    ppermute x6, starting transfers between devices: 6.8 us -> 3.83 us  [swap(): return lax.ppermute(value, ('gx', 'gy'), pairs)]
    ppermute x4, waiting for transfers between devices: 2.78 us -> 0.01 us  [the longest x2 0.01 us: widened(): far = lax.ppermute(far, axis, far_pairs)]
    unnamed x15 -> x0, local copies, waits for them, and re-layouts: 1.46 us -> none
    pallas_call x1 -> x3, Pallas kernels: 6.87 us -> 8.3 us  [the longest x1 4.42 us: per_device(): pl.pallas_call(lambda *refs: inner_kernel(rows, cols, *refs), out_shape=(...]
    pallas_call x1, Pallas kernels: 0.36 us -> 1.35 us  [per_device(): pl.pallas_call(weights_kernel, out_shape=(jax.ShapeDtypeStruct((2 * hid,...]
    ppermute x4, starting transfers between devices: 8.03 us -> 7.09 us  [the longest x2 6.41 us: widened(): far = lax.ppermute(far, axis, far_pairs)]
  transfers between devices with their start and end apart: 10 -> 10, of which waited for: 8 -> 6; matrix products, arithmetic and copies ran while one was open for 0% -> 0% of each run, Pallas kernels for 6% -> 21%
where the time goes in v2:
time: 35.2 us; the launch traced here: 35 us
  Pallas kernels  12.2 us (35%)
  starting transfers between devices  10.9 us (31%)
  waiting for transfers between devices  10.7 us (30%)
  between operations  0.79 us (2%)
  other arithmetic  0.39 us (1%)
    ppermute x6, waiting for transfers between devices, swap(): return lax.ppermute(value, ('gx', 'gy'), pairs)  10.6 us
    ppermute x2, starting transfers between devices, widened(): far = lax.ppermute(far, axis, far_pairs)  6.41 us
    pallas_call x1, Pallas kernels, per_device(): pl.pallas_call(lambda *refs: inner_kernel(rows, cols, *refs), out_shape=(...  4.42 us
    ppermute x6, starting transfers between devices, swap(): return lax.ppermute(value, ('gx', 'gy'), pairs)  3.83 us
    pallas_call x1, Pallas kernels, per_device(): pl.pallas_call(lambda *refs: outer_kernel(rows, cols, *refs), out_shape=(...  2.95 us
    pallas_call x1, Pallas kernels, per_device(): pl.pallas_call(lambda *refs: advance_kernel(rows, cols, *refs), out_shape...  1.69 us
    pallas_call x1, Pallas kernels, per_device(): pl.pallas_call(weights_kernel, out_shape=(jax.ShapeDtypeStruct((2 * hid,...  1.35 us
    pallas_call x1, Pallas kernels, per_device(): pl.pallas_call(pack_kernel, out_shape=(jax.ShapeDtypeStruct((4, rows, col...  0.94 us
  transfers between devices with their start and end apart: 10, of which 6 were waited for; matrix products, arithmetic and copies ran while one was open for 0% of the time, Pallas kernels for 21%

profile of v2, /device:TPU:0, one launch (start us, length us, event | category | flops | bytes accessed | tf_op | source)
XLA Modules:
  0.0 35.0 jit_solution(7085183035940215166)
XLA Ops:
  0.6 0.9 %pack.1 = (f32[4,16,256]{2,1,0:T(8,128)S(1)}, bf16[4,16,4]{2,1,0:T(8,128)(2,1)S(1)}, bf16[4,16,4]{2,1,0:T(8,128)(2,1)S(1)}) custom-call(s32[1]{0:T(128)} %bitcast.even_ref, f32[2,16,256]{2,1,0:T(8,128)} %velocity_ref.1, f32[2,16,256]{2,1,0:T(8,128)} %cotangent_ref.1), custom_call_target="tpu_custom_call" | custom-call | tf_op jit(solution)/shard_map/pack/pallas_call | solution.py:629
  1.6 2.4 %collective-permute-start = (bf16[4,16,4]{2,1,0:T(8,128)(2,1)S(1)}, bf16[4,16,4]{2,1,0:T(8,128)(2,1)S(1)}, u32[]{:S(2)}, u32[]{:S(2)}) collective-permute-start(bf16[4,16,4]{2,1,0:T(8,128)(2,1)S(1)} %get-tuple-element.51), channel_id=1, source_target_pairs={{0,3},{1,2},{2,1},{3,0},{4,7},{5,6},{6,5},{7,4},{8,11},{9,10},{10,... | collective-permute-start | bytes 1544 | tf_op jit(solution)/shard_map/ppermute | solution.py:533
  4.0 0.7 %collective-permute-start.1 = (bf16[4,16,4]{2,1,0:T(8,128)(2,1)S(1)}, bf16[4,16,4]{2,1,0:T(8,128)(2,1)S(1)}, u32[]{:S(2)}, u32[]{:S(2)}) collective-permute-start(bf16[4,16,4]{2,1,0:T(8,128)(2,1)S(1)} %get-tuple-element.52), channel_id=1, source_target_pairs={{0,1},{1,0},{2,3},{3,2},{4,5},{5,4},{6,7},{7,6},{8,9},{9,8},{10,11... | collective-permute-start | bytes 1544 | tf_op jit(solution)/shard_map/ppermute | solution.py:534
  4.7 1.4 %weights.1 = (bf16[128,192]{1,0:T(8,128)(2,1)S(1)}, bf16[3,128,256]{2,1,0:T(8,128)(2,1)S(1)}, bf16[3,128,256]{2,1,0:T(8,128)(2,1)S(1)}, bf16[128,192]{1,0:T(8,12...) custom-call(bf16[9,2,64]{2,1,0:T(2,128)(2,1)} %bitcast.24, ...), custom_call_target="tpu_custom_call" | custom-call | tf_op jit(solution)/shard_map/weights/pallas_call | solution.py:591
  6.1 0.0 collective-permute-done
  6.1 0.0 collective-permute-done.1
  6.1 0.1 fusion
  6.2 4.0 %collective-permute-start.2 = (bf16[4,4,264]{2,1,0:T(4,128)(2,1)S(1)}, bf16[4,4,264]{2,1,0:T(4,128)(2,1)S(1)}, u32[]{:S(2)}, u32[]{:S(2)}) collective-permute-start(bf16[4,4,264]{2,1,0:T(4,128)(2,1)S(1)} %get-tuple-element.60), channel_id=1, source_target_pairs={{0,12},{4,8},{8,4},{12,0},{1,13},{5,9},{9,5},{13,1},{2,14},{6,10},... | collective-permute-start | bytes 25352 | tf_op jit(solution)/shard_map/ppermute | solution.py:533
  10.2 0.0 collective-permute-start.3
  10.2 4.4 %inner.1 = (bf16[3,896,384]{2,1,0:T(8,128)(2,1)S(1)}, f32[896,384]{1,0:T(8,128)S(1)}, bf16[3,768,384]{2,1,0:T(8,128)(2,1)S(1)}, bf16[768,384]{1,0:T(8,128)(2,1)S...) custom-call(f32[4,16,264]{2,1,0:T(8,128)S(1)} %get-tuple-element.95., ...), custom_call_target="tpu_custom_call" | custom-call | tf_op jit(solution)/shard_map/inner/pallas_call | solution.py:648
  14.6 0.0 collective-permute-done.2
  14.7 0.0 collective-permute-done.3
  14.7 0.1 pad_maximum_fusion.refs_0_
  14.8 2.9 %outer.1 = (bf16[32,768]{1,0:T(8,128)(2,1)S(1)}, bf16[32,768]{1,0:T(8,128)(2,1)S(1)}, bf16[2,256,384]{2,1,0:T(8,128)(2,1)S(1)}, bf16[2,256,384]{2,1,0:T(8,128)(2,1)S(1)}) custom-call(f32[4,24,264]{2,1,0:T(8,128)S(1)} %pad_maximum_fusion.refs_0_, bf16[128,192]{1,0:T(8,128)(2,1)S(1)} %get-tuple-element.62.refs_1_, ...), custom_call_target="tpu_custom_call" | custom-call | tf_op jit(solution)/shard_map/outer/pallas_call | solution.py:669
  17.8 0.1 collective-permute-start.4
  17.8 1.2 %collective-permute-done.4 = bf16[32,768]{1,0:T(8,128)(2,1)S(1)} collective-permute-done((bf16[32,768]{1,0:T(8,128)(2,1)S(1)}, bf16[32,768]{1,0:T(8,128)(2,1)S(1)}, u32[]{:S(2)}, u32[]{:S(2)}) %collective-permute-start.4) | collective-permute-done | bytes 49184 | tf_op jit(solution)/shard_map/ppermute | solution.py:545
  19.1 1.6 %collective-permute-start.5 = (bf16[32,768]{1,0:T(8,128)(2,1)S(1)}, bf16[32,768]{1,0:T(8,128)(2,1)S(1)}, u32[]{:S(2)}, u32[]{:S(2)}) collective-permute-start(bf16[32,768]{1,0:T(8,128)(2,1)S(1)} %add_convert_fusion.2), channel_id=1, source_target_pairs={{0,2},{1,3},{2,0},{3,1},{4,6},{5,7},{6,4},{7,5},{8,10},{9,11},{10,... | collective-permute-start | bytes 147464 | tf_op jit(solution)/shard_map/ppermute | solution.py:545
  20.7 2.0 %collective-permute-start.6 = (bf16[32,768]{1,0:T(8,128)(2,1)S(1)}, bf16[32,768]{1,0:T(8,128)(2,1)S(1)}, u32[]{:S(2)}, u32[]{:S(2)}) collective-permute-start(bf16[32,768]{1,0:T(8,128)(2,1)S(1)} %add_convert_fusion.2), channel_id=1, source_target_pairs={{0,4},{1,5},{2,6},{3,7},{4,0},{5,1},{6,2},{7,3},{8,12},{9,13},{10,... | collective-permute-start | bytes 147464 | tf_op jit(solution)/shard_map/ppermute | solution.py:545
  22.7 0.0 collective-permute-start.7
  22.7 0.5 %collective-permute-done.5 = bf16[32,768]{1,0:T(8,128)(2,1)S(1)} collective-permute-done((bf16[32,768]{1,0:T(8,128)(2,1)S(1)}, bf16[32,768]{1,0:T(8,128)(2,1)S(1)}, u32[]{:S(2)}, u32[]{:S(2)}) %collective-permute-start.5) | collective-permute-done | bytes 49184 | tf_op jit(solution)/shard_map/ppermute | solution.py:545
  23.2 1.5 %collective-permute-done.6 = bf16[32,768]{1,0:T(8,128)(2,1)S(1)} collective-permute-done((bf16[32,768]{1,0:T(8,128)(2,1)S(1)}, bf16[32,768]{1,0:T(8,128)(2,1)S(1)}, u32[]{:S(2)}, u32[]{:S(2)}) %collective-permute-start.6) | collective-permute-done | bytes 49184 | tf_op jit(solution)/shard_map/ppermute | solution.py:545
  24.8 2.9 %collective-permute-done.7 = bf16[32,768]{1,0:T(8,128)(2,1)S(1)} collective-permute-done((bf16[32,768]{1,0:T(8,128)(2,1)S(1)}, bf16[32,768]{1,0:T(8,128)(2,1)S(1)}, u32[]{:S(2)}, u32[]{:S(2)}) %collective-permute-start.7) | collective-permute-done | bytes 49184 | tf_op jit(solution)/shard_map/ppermute | solution.py:545
  27.7 0.1 collective-permute-start.8
  27.8 0.1 sine_multiply_fusion.refs_1_
  27.9 1.7 %advance.1 = (f32[2,16,256]{2,1,0:T(8,128)}, f32[2,16,256]{2,1,0:T(8,128)}) custom-call(f32[4,24,264]{2,1,0:T(8,128)S(1)} %pad_maximum_fusion.refs_0_, f32[1,384]{1,0:T(1,128)S(1)} %sine_multiply_fusion.refs_1_, bf16[96,256]{1,0:T(8,128)(2,1)S(1)} %get-tuple-element.77.refs_2_, f32[32,128]{1,0:T(8,128)S(1)} %get-tuple-element.78.refs_3_, ...), custom_call_target="tpu_custom_call" | custom-call | tf_op jit(solution)/shard_map/advance/pallas_call | solution.py:693
  29.5 3.2 %collective-permute-done.8 = bf16[32,768]{1,0:T(8,128)(2,1)S(1)} collective-permute-done((bf16[32,768]{1,0:T(8,128)(2,1)S(1)}, bf16[32,768]{1,0:T(8,128)(2,1)S(1)}, u32[]{:S(2)}, u32[]{:S(2)}) %collective-permute-start.8) | collective-permute-done | bytes 49184 | tf_op jit(solution)/shard_map/ppermute | solution.py:545
  32.8 0.1 collective-permute-start.9
  32.9 1.2 %collective-permute-done.9.refs_1_ = bf16[32,768]{1,0:T(8,128)(2,1)S(1)} collective-permute-done((bf16[32,768]{1,0:T(8,128)(2,1)S(1)}, bf16[32,768]{1,0:T(8,128)(2,1)S(1)}, u32[]{:S(2)}, u32[]{:S(2)}) %collective-permute-start.9) | collective-permute-done | bytes 49184 | tf_op jit(solution)/shard_map/ppermute | solution.py:545
  34.1 0.9 %finish.1 = (f32[9,2,64]{2,1,0:T(2,128)}, f32[1,64]{1,0:T(1,128)}, f32[9,64,64]{2,1,0:T(8,128)}, f32[1,64]{1,0:T(1,128)}, f32[12,3,3,64]{3,2,1,0:T(4,128)}, /*index=5*/f32[1,12]{1,0:T(1,128)}) custom-call(bf16[32,768]{1,0:T(8,128)(2,1)S(1)} %add_convert_fusion.refs_0_, bf16[32,768]{1,0:T(8,128)(2,1)S(1)} %collective-permute-done.9.refs_1_, ...), custom_call_target="tpu_custom_call" | custom-call | tf_op jit(solution)/shard_map/finish/pallas_call | solution.py:710
  (6 shorter events, 0.1 us)
Async XLA Ops:
  1.6 4.5 %collective-permute-start = (bf16[4,16,4]{2,1,0:T(8,128)(2,1)S(1)}, bf16[4,16,4]{2,1,0:T(8,128)(2,1)S(1)}, u32[]{:S(2)}, u32[]{:S(2)}) collective-permute-start(bf16[4,16,4]{2,1,0:T(8,128)(2,1)S(1)} %get-tuple-element.51), channel_id=1, source_target_pairs={{0,3},{1,2},{2,1},{3,0},{4,7},{5,6},{6,5},{7,4},{8,11},{9,10},{10,... | collective-permute-start | bytes 1544 | tf_op jit(solution)/shard_map/ppermute | solution.py:533
  4.0 2.1 %collective-permute-start.1 = (bf16[4,16,4]{2,1,0:T(8,128)(2,1)S(1)}, bf16[4,16,4]{2,1,0:T(8,128)(2,1)S(1)}, u32[]{:S(2)}, u32[]{:S(2)}) collective-permute-start(bf16[4,16,4]{2,1,0:T(8,128)(2,1)S(1)} %get-tuple-element.52), channel_id=1, source_target_pairs={{0,1},{1,0},{2,3},{3,2},{4,5},{5,4},{6,7},{7,6},{8,9},{9,8},{10,11... | collective-permute-start | bytes 1544 | tf_op jit(solution)/shard_map/ppermute | solution.py:534
  6.2 8.4 %collective-permute-start.2 = (bf16[4,4,264]{2,1,0:T(4,128)(2,1)S(1)}, bf16[4,4,264]{2,1,0:T(4,128)(2,1)S(1)}, u32[]{:S(2)}, u32[]{:S(2)}) collective-permute-start(bf16[4,4,264]{2,1,0:T(4,128)(2,1)S(1)} %get-tuple-element.60), channel_id=1, source_target_pairs={{0,12},{4,8},{8,4},{12,0},{1,13},{5,9},{9,5},{13,1},{2,14},{6,10},... | collective-permute-start | bytes 25352 | tf_op jit(solution)/shard_map/ppermute | solution.py:533
  10.2 4.4 %collective-permute-start.3 = (bf16[4,4,264]{2,1,0:T(4,128)(2,1)S(1)}, bf16[4,4,264]{2,1,0:T(4,128)(2,1)S(1)}, u32[]{:S(2)}, u32[]{:S(2)}) collective-permute-start(bf16[4,4,264]{2,1,0:T(4,128)(2,1)S(1)} %get-tuple-element.61), channel_id=1, source_target_pairs={{0,4},{4,0},{8,12},{12,8},{1,5},{5,1},{9,13},{13,9},{2,6},{6,2},{1... | collective-permute-start | bytes 25352 | tf_op jit(solution)/shard_map/ppermute | solution.py:534
  17.8 1.3 %collective-permute-start.4 = (bf16[32,768]{1,0:T(8,128)(2,1)S(1)}, bf16[32,768]{1,0:T(8,128)(2,1)S(1)}, u32[]{:S(2)}, u32[]{:S(2)}) collective-permute-start(bf16[32,768]{1,0:T(8,128)(2,1)S(1)} %get-tuple-element.76), channel_id=1, source_target_pairs={{0,1},{1,0},{2,3},{3,2},{4,5},{5,4},{6,7},{7,6},{8,9},{9,8},{10,11... | collective-permute-start | bytes 147464 | tf_op jit(solution)/shard_map/ppermute | solution.py:545
  19.1 4.2 %collective-permute-start.5 = (bf16[32,768]{1,0:T(8,128)(2,1)S(1)}, bf16[32,768]{1,0:T(8,128)(2,1)S(1)}, u32[]{:S(2)}, u32[]{:S(2)}) collective-permute-start(bf16[32,768]{1,0:T(8,128)(2,1)S(1)} %add_convert_fusion.2), channel_id=1, source_target_pairs={{0,2},{1,3},{2,0},{3,1},{4,6},{5,7},{6,4},{7,5},{8,10},{9,11},{10,... | collective-permute-start | bytes 147464 | tf_op jit(solution)/shard_map/ppermute | solution.py:545
  20.7 4.1 %collective-permute-start.6 = (bf16[32,768]{1,0:T(8,128)(2,1)S(1)}, bf16[32,768]{1,0:T(8,128)(2,1)S(1)}, u32[]{:S(2)}, u32[]{:S(2)}) collective-permute-start(bf16[32,768]{1,0:T(8,128)(2,1)S(1)} %add_convert_fusion.2), channel_id=1, source_target_pairs={{0,4},{1,5},{2,6},{3,7},{4,0},{5,1},{6,2},{7,3},{8,12},{9,13},{10,... | collective-permute-start | bytes 147464 | tf_op jit(solution)/shard_map/ppermute | solution.py:545
  22.7 5.0 %collective-permute-start.7 = (bf16[32,768]{1,0:T(8,128)(2,1)S(1)}, bf16[32,768]{1,0:T(8,128)(2,1)S(1)}, u32[]{:S(2)}, u32[]{:S(2)}) collective-permute-start(bf16[32,768]{1,0:T(8,128)(2,1)S(1)} %add_convert_fusion.2), channel_id=1, source_target_pairs={{0,6},{1,7},{2,4},{3,5},{4,2},{5,3},{6,0},{7,1},{8,14},{9,15},{10,... | collective-permute-start | bytes 147464 | tf_op jit(solution)/shard_map/ppermute | solution.py:545
  27.7 5.1 %collective-permute-start.8 = (bf16[32,768]{1,0:T(8,128)(2,1)S(1)}, bf16[32,768]{1,0:T(8,128)(2,1)S(1)}, u32[]{:S(2)}, u32[]{:S(2)}) collective-permute-start(bf16[32,768]{1,0:T(8,128)(2,1)S(1)} %add_convert_fusion.1), channel_id=1, source_target_pairs={{0,8},{1,9},{2,10},{3,11},{4,12},{5,13},{6,14},{7,15},{8,0},{9,1},... | collective-permute-start | bytes 147464 | tf_op jit(solution)/shard_map/ppermute | solution.py:545
  32.8 1.3 %collective-permute-start.9 = (bf16[32,768]{1,0:T(8,128)(2,1)S(1)}, bf16[32,768]{1,0:T(8,128)(2,1)S(1)}, u32[]{:S(2)}, u32[]{:S(2)}) collective-permute-start(bf16[32,768]{1,0:T(8,128)(2,1)S(1)} %add_convert_fusion.refs_0_), channel_id=1, source_target_pairs={{0,1},{1,0},{2,3},{3,2},{4,5},{5,4},{6,7},{7,6},{8,9},{9,8},{10,11... | collective-permute-start | bytes 147464 | tf_op jit(solution)/shard_map/ppermute | solution.py:545

commit v3 on v2

--- a/solution.py
+++ b/solution.py
@@ -183,6 +183,7 @@
     w_out_t = w_out_t_ref[...]
     w_mid = jnp.concatenate([w_mid_ref[b] for b in range(3)], axis=1)
     w_mid_t = jnp.concatenate([w_mid_t_ref[b] for b in range(3)], axis=1)
+    held = []
     for r in groups_two:
         window = [act_one.get(r - 1, r + 3, (b,)) for b in range(3)]
         linear = mm(w_mid, jnp.concatenate(window, axis=0)) + b_mid
@@ -196,9 +197,14 @@
             kept = jnp.where(own_cols, grad, 0.0)
             bias_acc[0] += kept
             kept = kept.astype(bf16)
+            held.append((kept, window, fed, jnp.where(own_cols, act, 0.0).astype(bf16)))
+        if held and (len(held) == 2 or r == groups_two[-1]):
+            kepts, windows, feds, acts = zip(*held)
+            held = []
+            kepts = jnp.concatenate(kepts, axis=1)
             for b in range(3):
-                acc_mid[b] += mm_nt(kept, window[b])
-            acc_small[0] += mm_nt(fed, jnp.where(own_cols, act, 0.0).astype(bf16))
+                acc_mid[b] += mm_nt(kepts, jnp.concatenate([w[b] for w in windows], axis=1))
+            acc_small[0] += mm_nt(jnp.concatenate(feds, axis=1), jnp.concatenate(acts, axis=1))
 
     for r in groups_back:
         grad = mm(w_mid_t, grad_two.window(r - 1, r + 3)) * slope_one.get(r, r + 2)
@@ -637,8 +643,9 @@
     )(even, in_hbm(velocity), in_hbm(cotangent))
     wide = widened(fields, far, near, "gy", 2)
     maps = (w_in, w_mid, w_mid_t, w_out_t, b_in, b_mid)
-    far_near, maps = lax.optimization_barrier((edges(wide, "gx", 1), maps))
-    ext = widened(wide, *far_near, "gx", 1)
+    far, near = edges(wide, "gx", 1)
+    near, maps = lax.optimization_barrier((near, maps))
+    ext = widened(wide, far, near, "gx", 1)
 
     accs = (
         jax.ShapeDtypeStruct((3, 2 * hid, 4 * hid), f32),

time: 35.2 us -> 33.8 us (0.960)
  waiting for transfers between devices: 10.7 us -> 8.08 us
  starting transfers between devices: 10.9 us -> 12.6 us
  Pallas kernels: 12.2 us -> 11.7 us
    ppermute x6, waiting for transfers between devices: 10.6 us -> 8.07 us  [swap(): return lax.ppermute(value, ('gx', 'gy'), pairs)]
    ppermute x2, starting transfers between devices: 0.68 us -> 2.62 us  [widened(): near = lax.ppermute(near, axis, [(i, i ^ 1) for i in range(count)])]
    ppermute x2, starting transfers between devices: 6.41 us -> 4.92 us  [widened(): far = lax.ppermute(far, axis, far_pairs)]
    ppermute x6, starting transfers between devices: 3.83 us -> 5.06 us  [swap(): return lax.ppermute(value, ('gx', 'gy'), pairs)]
    pallas_call x1, Pallas kernels: 4.42 us -> 4.05 us  [per_device(): pl.pallas_call(lambda *refs: inner_kernel(rows, cols, *refs), out_shape=(...]
where the time goes in v3:
time: 33.8 us; the launch traced here: 33.6 us
  starting transfers between devices  12.6 us (37%)
  Pallas kernels  11.7 us (35%)
  waiting for transfers between devices  8.08 us (24%)
  between operations  0.78 us (2%)
  other arithmetic  0.39 us (1%)
    ppermute x6, waiting for transfers between devices, swap(): return lax.ppermute(value, ('gx', 'gy'), pairs)  8.07 us
    ppermute x6, starting transfers between devices, swap(): return lax.ppermute(value, ('gx', 'gy'), pairs)  5.06 us
    ppermute x2, starting transfers between devices, widened(): far = lax.ppermute(far, axis, far_pairs)  4.92 us
    pallas_call x1, Pallas kernels, per_device(): pl.pallas_call(lambda *refs: inner_kernel(rows, cols, *refs), out_shape=(...  4.05 us
    pallas_call x1, Pallas kernels, per_device(): pl.pallas_call(lambda *refs: outer_kernel(rows, cols, *refs), out_shape=(...  2.82 us
    ppermute x2, starting transfers between devices, widened(): near = lax.ppermute(near, axis, [(i, i ^ 1) for i in range(count)])  2.62 us
    pallas_call x1, Pallas kernels, per_device(): pl.pallas_call(lambda *refs: advance_kernel(rows, cols, *refs), out_shape...  1.69 us
    pallas_call x1, Pallas kernels, per_device(): pl.pallas_call(weights_kernel, out_shape=(jax.ShapeDtypeStruct((2 * hid,...  1.35 us
  transfers between devices with their start and end apart: 10, of which 6 were waited for; matrix products, arithmetic and copies ran while one was open for 0% of the time, Pallas kernels for 21%

profile of v3, /device:TPU:0, one launch (start us, length us, event | category | flops | bytes accessed | tf_op | source)
XLA Modules:
  0.0 33.6 jit_solution(3639613635566258980)
XLA Ops:
  0.6 0.9 %pack.1 = (f32[4,16,256]{2,1,0:T(8,128)S(1)}, bf16[4,16,4]{2,1,0:T(8,128)(2,1)S(1)}, bf16[4,16,4]{2,1,0:T(8,128)(2,1)S(1)}) custom-call(s32[1]{0:T(128)} %bitcast.even_ref, f32[2,16,256]{2,1,0:T(8,128)} %velocity_ref.1, f32[2,16,256]{2,1,0:T(8,128)} %cotangent_ref.1), custom_call_target="tpu_custom_call" | custom-call | tf_op jit(solution)/shard_map/pack/pallas_call | solution.py:635
  1.6 2.4 %collective-permute-start = (bf16[4,16,4]{2,1,0:T(8,128)(2,1)S(1)}, bf16[4,16,4]{2,1,0:T(8,128)(2,1)S(1)}, u32[]{:S(2)}, u32[]{:S(2)}) collective-permute-start(bf16[4,16,4]{2,1,0:T(8,128)(2,1)S(1)} %get-tuple-element.50), channel_id=1, source_target_pairs={{0,3},{1,2},{2,1},{3,0},{4,7},{5,6},{6,5},{7,4},{8,11},{9,10},{10,... | collective-permute-start | bytes 1544 | tf_op jit(solution)/shard_map/ppermute | solution.py:539
  4.0 0.7 %collective-permute-start.1 = (bf16[4,16,4]{2,1,0:T(8,128)(2,1)S(1)}, bf16[4,16,4]{2,1,0:T(8,128)(2,1)S(1)}, u32[]{:S(2)}, u32[]{:S(2)}) collective-permute-start(bf16[4,16,4]{2,1,0:T(8,128)(2,1)S(1)} %get-tuple-element.51), channel_id=1, source_target_pairs={{0,1},{1,0},{2,3},{3,2},{4,5},{5,4},{6,7},{7,6},{8,9},{9,8},{10,11... | collective-permute-start | bytes 1544 | tf_op jit(solution)/shard_map/ppermute | solution.py:540
  4.7 1.4 %weights.1 = (bf16[128,192]{1,0:T(8,128)(2,1)S(1)}, bf16[3,128,256]{2,1,0:T(8,128)(2,1)S(1)}, bf16[3,128,256]{2,1,0:T(8,128)(2,1)S(1)}, bf16[128,192]{1,0:T(8,12...) custom-call(bf16[9,2,64]{2,1,0:T(2,128)(2,1)} %bitcast.24, ...), custom_call_target="tpu_custom_call" | custom-call | tf_op jit(solution)/shard_map/weights/pallas_call | solution.py:597
  6.1 0.0 collective-permute-done
  6.1 0.0 collective-permute-done.1
  6.1 0.1 fusion
  6.2 1.9 %collective-permute-start.3 = (bf16[4,4,264]{2,1,0:T(4,128)(2,1)S(1)}, bf16[4,4,264]{2,1,0:T(4,128)(2,1)S(1)}, u32[]{:S(2)}, u32[]{:S(2)}) collective-permute-start(bf16[4,4,264]{2,1,0:T(4,128)(2,1)S(1)} %get-tuple-element.59), channel_id=1, source_target_pairs={{0,4},{4,0},{8,12},{12,8},{1,5},{5,1},{9,13},{13,9},{2,6},{6,2},{1... | collective-permute-start | bytes 25352 | tf_op jit(solution)/shard_map/ppermute | solution.py:540
  8.2 2.5 %collective-permute-start.2 = (bf16[4,4,264]{2,1,0:T(4,128)(2,1)S(1)}, bf16[4,4,264]{2,1,0:T(4,128)(2,1)S(1)}, u32[]{:S(2)}, u32[]{:S(2)}) collective-permute-start(bf16[4,4,264]{2,1,0:T(4,128)(2,1)S(1)} %get-tuple-element.94), channel_id=1, source_target_pairs={{0,12},{4,8},{8,4},{12,0},{1,13},{5,9},{9,5},{13,1},{2,14},{6,10},... | collective-permute-start | bytes 25352 | tf_op jit(solution)/shard_map/ppermute | solution.py:539
  10.7 4.1 %inner.1 = (bf16[3,896,384]{2,1,0:T(8,128)(2,1)S(1)}, f32[896,384]{1,0:T(8,128)S(1)}, bf16[3,768,384]{2,1,0:T(8,128)(2,1)S(1)}, bf16[768,384]{1,0:T(8,128)(2,1)S...) custom-call(f32[4,16,264]{2,1,0:T(8,128)S(1)} %get-tuple-element.93., ...), custom_call_target="tpu_custom_call" | custom-call | tf_op jit(solution)/shard_map/inner/pallas_call | solution.py:655
  14.7 0.0 collective-permute-done.3
  14.7 0.0 collective-permute-done.2
  14.8 0.1 pad_maximum_fusion.refs_0_
  14.9 2.8 %outer.1 = (bf16[32,768]{1,0:T(8,128)(2,1)S(1)}, bf16[32,768]{1,0:T(8,128)(2,1)S(1)}, bf16[2,256,384]{2,1,0:T(8,128)(2,1)S(1)}, bf16[2,256,384]{2,1,0:T(8,128)(2,1)S(1)}) custom-call(f32[4,24,264]{2,1,0:T(8,128)S(1)} %pad_maximum_fusion.refs_0_, bf16[128,192]{1,0:T(8,128)(2,1)S(1)} %get-tuple-element.60.refs_1_, ...), custom_call_target="tpu_custom_call" | custom-call | tf_op jit(solution)/shard_map/outer/pallas_call | solution.py:676
  17.7 0.1 collective-permute-start.4
  17.8 1.2 %collective-permute-done.4 = bf16[32,768]{1,0:T(8,128)(2,1)S(1)} collective-permute-done((bf16[32,768]{1,0:T(8,128)(2,1)S(1)}, bf16[32,768]{1,0:T(8,128)(2,1)S(1)}, u32[]{:S(2)}, u32[]{:S(2)}) %collective-permute-start.4) | collective-permute-done | bytes 49184 | tf_op jit(solution)/shard_map/ppermute | solution.py:551
  19.0 1.6 %collective-permute-start.5 = (bf16[32,768]{1,0:T(8,128)(2,1)S(1)}, bf16[32,768]{1,0:T(8,128)(2,1)S(1)}, u32[]{:S(2)}, u32[]{:S(2)}) collective-permute-start(bf16[32,768]{1,0:T(8,128)(2,1)S(1)} %add_convert_fusion.2), channel_id=1, source_target_pairs={{0,2},{1,3},{2,0},{3,1},{4,6},{5,7},{6,4},{7,5},{8,10},{9,11},{10,... | collective-permute-start | bytes 147464 | tf_op jit(solution)/shard_map/ppermute | solution.py:551
  20.6 0.7 %collective-permute-start.6 = (bf16[32,768]{1,0:T(8,128)(2,1)S(1)}, bf16[32,768]{1,0:T(8,128)(2,1)S(1)}, u32[]{:S(2)}, u32[]{:S(2)}) collective-permute-start(bf16[32,768]{1,0:T(8,128)(2,1)S(1)} %add_convert_fusion.2), channel_id=1, source_target_pairs={{0,4},{1,5},{2,6},{3,7},{4,0},{5,1},{6,2},{7,3},{8,12},{9,13},{10,... | collective-permute-start | bytes 147464 | tf_op jit(solution)/shard_map/ppermute | solution.py:551
  21.3 1.3 %collective-permute-start.7 = (bf16[32,768]{1,0:T(8,128)(2,1)S(1)}, bf16[32,768]{1,0:T(8,128)(2,1)S(1)}, u32[]{:S(2)}, u32[]{:S(2)}) collective-permute-start(bf16[32,768]{1,0:T(8,128)(2,1)S(1)} %add_convert_fusion.2), channel_id=1, source_target_pairs={{0,6},{1,7},{2,4},{3,5},{4,2},{5,3},{6,0},{7,1},{8,14},{9,15},{10,... | collective-permute-start | bytes 147464 | tf_op jit(solution)/shard_map/ppermute | solution.py:551
  22.6 0.6 %collective-permute-done.5 = bf16[32,768]{1,0:T(8,128)(2,1)S(1)} collective-permute-done((bf16[32,768]{1,0:T(8,128)(2,1)S(1)}, bf16[32,768]{1,0:T(8,128)(2,1)S(1)}, u32[]{:S(2)}, u32[]{:S(2)}) %collective-permute-start.5) | collective-permute-done | bytes 49184 | tf_op jit(solution)/shard_map/ppermute | solution.py:551
  23.2 1.5 %collective-permute-done.6 = bf16[32,768]{1,0:T(8,128)(2,1)S(1)} collective-permute-done((bf16[32,768]{1,0:T(8,128)(2,1)S(1)}, bf16[32,768]{1,0:T(8,128)(2,1)S(1)}, u32[]{:S(2)}, u32[]{:S(2)}) %collective-permute-start.6) | collective-permute-done | bytes 49184 | tf_op jit(solution)/shard_map/ppermute | solution.py:551
  24.7 1.6 %collective-permute-done.7 = bf16[32,768]{1,0:T(8,128)(2,1)S(1)} collective-permute-done((bf16[32,768]{1,0:T(8,128)(2,1)S(1)}, bf16[32,768]{1,0:T(8,128)(2,1)S(1)}, u32[]{:S(2)}, u32[]{:S(2)}) %collective-permute-start.7) | collective-permute-done | bytes 49184 | tf_op jit(solution)/shard_map/ppermute | solution.py:551
  26.3 1.4 %collective-permute-start.8 = (bf16[32,768]{1,0:T(8,128)(2,1)S(1)}, bf16[32,768]{1,0:T(8,128)(2,1)S(1)}, u32[]{:S(2)}, u32[]{:S(2)}) collective-permute-start(bf16[32,768]{1,0:T(8,128)(2,1)S(1)} %add_convert_fusion.1), channel_id=1, source_target_pairs={{0,8},{1,9},{2,10},{3,11},{4,12},{5,13},{6,14},{7,15},{8,0},{9,1},... | collective-permute-start | bytes 147464 | tf_op jit(solution)/shard_map/ppermute | solution.py:551
  27.7 0.1 sine_multiply_fusion.refs_1_
  27.7 1.7 %advance.1 = (f32[2,16,256]{2,1,0:T(8,128)}, f32[2,16,256]{2,1,0:T(8,128)}) custom-call(f32[4,24,264]{2,1,0:T(8,128)S(1)} %pad_maximum_fusion.refs_0_, f32[1,384]{1,0:T(1,128)S(1)} %sine_multiply_fusion.refs_1_, bf16[96,256]{1,0:T(8,128)(2,1)S(1)} %get-tuple-element.75.refs_2_, f32[32,128]{1,0:T(8,128)S(1)} %get-tuple-element.76.refs_3_, ...), custom_call_target="tpu_custom_call" | custom-call | tf_op jit(solution)/shard_map/advance/pallas_call | solution.py:700
  29.4 1.9 %collective-permute-done.8 = bf16[32,768]{1,0:T(8,128)(2,1)S(1)} collective-permute-done((bf16[32,768]{1,0:T(8,128)(2,1)S(1)}, bf16[32,768]{1,0:T(8,128)(2,1)S(1)}, u32[]{:S(2)}, u32[]{:S(2)}) %collective-permute-start.8) | collective-permute-done | bytes 49184 | tf_op jit(solution)/shard_map/ppermute | solution.py:551
  31.4 0.1 collective-permute-start.9
  31.5 1.2 %collective-permute-done.9.refs_1_ = bf16[32,768]{1,0:T(8,128)(2,1)S(1)} collective-permute-done((bf16[32,768]{1,0:T(8,128)(2,1)S(1)}, bf16[32,768]{1,0:T(8,128)(2,1)S(1)}, u32[]{:S(2)}, u32[]{:S(2)}) %collective-permute-start.9) | collective-permute-done | bytes 49184 | tf_op jit(solution)/shard_map/ppermute | solution.py:551
  32.7 0.9 %finish.1 = (f32[9,2,64]{2,1,0:T(2,128)}, f32[1,64]{1,0:T(1,128)}, f32[9,64,64]{2,1,0:T(8,128)}, f32[1,64]{1,0:T(1,128)}, f32[12,3,3,64]{3,2,1,0:T(4,128)}, /*index=5*/f32[1,12]{1,0:T(1,128)}) custom-call(bf16[32,768]{1,0:T(8,128)(2,1)S(1)} %add_convert_fusion.refs_0_, bf16[32,768]{1,0:T(8,128)(2,1)S(1)} %collective-permute-done.9.refs_1_, ...), custom_call_target="tpu_custom_call" | custom-call | tf_op jit(solution)/shard_map/finish/pallas_call | solution.py:717
  (6 shorter events, 0.1 us)
Async XLA Ops:
  1.6 4.5 %collective-permute-start = (bf16[4,16,4]{2,1,0:T(8,128)(2,1)S(1)}, bf16[4,16,4]{2,1,0:T(8,128)(2,1)S(1)}, u32[]{:S(2)}, u32[]{:S(2)}) collective-permute-start(bf16[4,16,4]{2,1,0:T(8,128)(2,1)S(1)} %get-tuple-element.50), channel_id=1, source_target_pairs={{0,3},{1,2},{2,1},{3,0},{4,7},{5,6},{6,5},{7,4},{8,11},{9,10},{10,... | collective-permute-start | bytes 1544 | tf_op jit(solution)/shard_map/ppermute | solution.py:539
  4.0 2.1 %collective-permute-start.1 = (bf16[4,16,4]{2,1,0:T(8,128)(2,1)S(1)}, bf16[4,16,4]{2,1,0:T(8,128)(2,1)S(1)}, u32[]{:S(2)}, u32[]{:S(2)}) collective-permute-start(bf16[4,16,4]{2,1,0:T(8,128)(2,1)S(1)} %get-tuple-element.51), channel_id=1, source_target_pairs={{0,1},{1,0},{2,3},{3,2},{4,5},{5,4},{6,7},{7,6},{8,9},{9,8},{10,11... | collective-permute-start | bytes 1544 | tf_op jit(solution)/shard_map/ppermute | solution.py:540
  6.2 8.5 %collective-permute-start.3 = (bf16[4,4,264]{2,1,0:T(4,128)(2,1)S(1)}, bf16[4,4,264]{2,1,0:T(4,128)(2,1)S(1)}, u32[]{:S(2)}, u32[]{:S(2)}) collective-permute-start(bf16[4,4,264]{2,1,0:T(4,128)(2,1)S(1)} %get-tuple-element.59), channel_id=1, source_target_pairs={{0,4},{4,0},{8,12},{12,8},{1,5},{5,1},{9,13},{13,9},{2,6},{6,2},{1... | collective-permute-start | bytes 25352 | tf_op jit(solution)/shard_map/ppermute | solution.py:540
  8.2 6.5 %collective-permute-start.2 = (bf16[4,4,264]{2,1,0:T(4,128)(2,1)S(1)}, bf16[4,4,264]{2,1,0:T(4,128)(2,1)S(1)}, u32[]{:S(2)}, u32[]{:S(2)}) collective-permute-start(bf16[4,4,264]{2,1,0:T(4,128)(2,1)S(1)} %get-tuple-element.94), channel_id=1, source_target_pairs={{0,12},{4,8},{8,4},{12,0},{1,13},{5,9},{9,5},{13,1},{2,14},{6,10},... | collective-permute-start | bytes 25352 | tf_op jit(solution)/shard_map/ppermute | solution.py:539
  17.7 1.3 %collective-permute-start.4 = (bf16[32,768]{1,0:T(8,128)(2,1)S(1)}, bf16[32,768]{1,0:T(8,128)(2,1)S(1)}, u32[]{:S(2)}, u32[]{:S(2)}) collective-permute-start(bf16[32,768]{1,0:T(8,128)(2,1)S(1)} %get-tuple-element.74), channel_id=1, source_target_pairs={{0,1},{1,0},{2,3},{3,2},{4,5},{5,4},{6,7},{7,6},{8,9},{9,8},{10,11... | collective-permute-start | bytes 147464 | tf_op jit(solution)/shard_map/ppermute | solution.py:551
  19.0 4.2 %collective-permute-start.5 = (bf16[32,768]{1,0:T(8,128)(2,1)S(1)}, bf16[32,768]{1,0:T(8,128)(2,1)S(1)}, u32[]{:S(2)}, u32[]{:S(2)}) collective-permute-start(bf16[32,768]{1,0:T(8,128)(2,1)S(1)} %add_convert_fusion.2), channel_id=1, source_target_pairs={{0,2},{1,3},{2,0},{3,1},{4,6},{5,7},{6,4},{7,5},{8,10},{9,11},{10,... | collective-permute-start | bytes 147464 | tf_op jit(solution)/shard_map/ppermute | solution.py:551
  20.6 4.1 %collective-permute-start.6 = (bf16[32,768]{1,0:T(8,128)(2,1)S(1)}, bf16[32,768]{1,0:T(8,128)(2,1)S(1)}, u32[]{:S(2)}, u32[]{:S(2)}) collective-permute-start(bf16[32,768]{1,0:T(8,128)(2,1)S(1)} %add_convert_fusion.2), channel_id=1, source_target_pairs={{0,4},{1,5},{2,6},{3,7},{4,0},{5,1},{6,2},{7,3},{8,12},{9,13},{10,... | collective-permute-start | bytes 147464 | tf_op jit(solution)/shard_map/ppermute | solution.py:551
  21.3 5.0 %collective-permute-start.7 = (bf16[32,768]{1,0:T(8,128)(2,1)S(1)}, bf16[32,768]{1,0:T(8,128)(2,1)S(1)}, u32[]{:S(2)}, u32[]{:S(2)}) collective-permute-start(bf16[32,768]{1,0:T(8,128)(2,1)S(1)} %add_convert_fusion.2), channel_id=1, source_target_pairs={{0,6},{1,7},{2,4},{3,5},{4,2},{5,3},{6,0},{7,1},{8,14},{9,15},{10,... | collective-permute-start | bytes 147464 | tf_op jit(solution)/shard_map/ppermute | solution.py:551
  26.3 5.1 %collective-permute-start.8 = (bf16[32,768]{1,0:T(8,128)(2,1)S(1)}, bf16[32,768]{1,0:T(8,128)(2,1)S(1)}, u32[]{:S(2)}, u32[]{:S(2)}) collective-permute-start(bf16[32,768]{1,0:T(8,128)(2,1)S(1)} %add_convert_fusion.1), channel_id=1, source_target_pairs={{0,8},{1,9},{2,10},{3,11},{4,12},{5,13},{6,14},{7,15},{8,0},{9,1},... | collective-permute-start | bytes 147464 | tf_op jit(solution)/shard_map/ppermute | solution.py:551
  31.4 1.3 %collective-permute-start.9 = (bf16[32,768]{1,0:T(8,128)(2,1)S(1)}, bf16[32,768]{1,0:T(8,128)(2,1)S(1)}, u32[]{:S(2)}, u32[]{:S(2)}) collective-permute-start(bf16[32,768]{1,0:T(8,128)(2,1)S(1)} %add_convert_fusion.refs_0_), channel_id=1, source_target_pairs={{0,1},{1,0},{2,3},{3,2},{4,5},{5,4},{6,7},{7,6},{8,9},{9,8},{10,11... | collective-permute-start | bytes 147464 | tf_op jit(solution)/shard_map/ppermute | solution.py:551

commit v4 on v3

--- a/solution.py
+++ b/solution.py
@@ -16,6 +16,9 @@
 hid = 64
 coef = 12
 slot = 16
+side = 2 * halo
+pitch = 2 * side
+left_of, right_of = halo - 1, side + halo
 taps_x = [(a, b) for a in (0, 1) for b in (-1, 0, 1)]
 taps_y = [(a, b) for a in (-1, 0, 1) for b in (0, 1)]
 f32 = jnp.float32
@@ -40,6 +43,48 @@
 
 def sigma_of(linear):
     return 0.5 * jnp.tanh(0.5 * linear) + 0.5
+
+
+def with_lane(value, at, column):
+    tiles = [value[:, k : k + 128] for k in range(0, value.shape[1], 128)]
+    lane = lax.broadcasted_iota(jnp.int32, (1, 128), 1)
+    tiles[at // 128] = jnp.where(lane == at % 128, column, tiles[at // 128])
+    return jnp.concatenate(tiles, axis=1)
+
+
+def strip_column(strip, row, at, to):
+    source = row * pitch + at
+    tile = strip[:, source // 128 * 128 : source // 128 * 128 + 128]
+    return pltpu.roll(tile, (to - source) % 128, 1) if (to - source) % 128 else tile
+
+
+def beside(low, middle, high, before, after):
+    return (
+        with_lane(shift(low, 0, -1), 0, before),
+        middle,
+        with_lane(shift(high, 0, 1), high.shape[1] - 1, after),
+    )
+
+
+def strip_taps(strip, columns=(-1, 0, 1)):
+    return jnp.concatenate(
+        [shift(strip, 0, a * pitch + b) for b in columns for a in (-1, 0, 1)], axis=0
+    )
+
+
+def strip_of(planes, rows, cols):
+    lane = lax.broadcasted_iota(jnp.int32, (1, 128), 1)
+    per_tile = 128 // pitch
+    tiles = []
+    for start in range(0, rows, per_tile):
+        tile = jnp.zeros((slot, 128), f32)
+        for k in range(min(per_tile, rows - start)):
+            at = slice((start + k) * slot, (start + k + 1) * slot)
+            pair = jnp.where(lane < side, planes[0, at, :], pltpu.roll(planes[cols // 128, at, :], side, 1))
+            pair = pltpu.roll(pair, k * pitch, 1) if k else pair
+            tile = jnp.where((lane >= k * pitch) & (lane < (k + 1) * pitch), pair, tile)
+        tiles.append(tile)
+    return jnp.concatenate(tiles, axis=1).astype(bf16)
 
 
 class Rows:
@@ -63,10 +108,20 @@
                 rows = slice((lo - start) * self.size, (lo - start) * self.size + value.shape[0])
                 ref[(*lead, rows, slice(None))] = value
 
-    def put_shifted(self, lo, value, lead=()):
+    def put_shifted(self, lo, value, strip, first):
         value = value.astype(bf16)
+        ends = [
+            jnp.concatenate([strip_column(strip, lo + k - first, at, to) for k in range(2)], axis=0)
+            for at, to in ((left_of, 0), (right_of, value.shape[1] - 1))
+        ]
+        for b, shifted in enumerate(beside(value, value, value, *ends)):
+            self.put(lo, shifted, (b,))
+
+    def put_cut(self, lo, value, lead):
+        value = value.astype(bf16)
+        cols = self.pieces[0][2].shape[-1]
         for b in range(3):
-            self.put(lo, shift(value, 0, b - 1), (*lead, b))
+            self.put(lo, shift(value, 0, halo - 1 + b)[:, :cols], (*lead, b))
 
     def window(self, lo, hi, lead=()):
         return jnp.concatenate([self.get(lo, hi, (*lead, b)) for b in range(3)], axis=0)
@@ -125,7 +180,8 @@
     put_plane(planes, 0, slot, w0)
     put_plane(planes, 1, slot, w1)
     for r in state_rows:
-        state_in.put_shifted(r, take_rows(planes, (r - first) * slot, 2 * slot), (0,))
+        state_in.put_cut(r, take_rows(planes, (r - first) * slot, 2 * slot), (0,))
+    strips = [strip_of(planes, count, cols)]
 
     normal_x, normal_y = faces(w0, w1)
     t0, t1 = shifted_fields(w0), shifted_fields(w1)
@@ -145,15 +201,50 @@
             put_plane(planes, at + k, slot, value)
             sums.append(jnp.sum(jnp.where(own, value, 0.0), axis=0, keepdims=True))
     for r in head_rows:
-        state_in.put_shifted(r, take_rows(planes, (r - first) * slot, 2 * slot), (1,))
-    return sums
+        state_in.put_cut(r, take_rows(planes, (r - first) * slot, 2 * slot), (1,))
+    strips.append(strip_of(planes, count, cols))
+    return sums, strips
+
+
+class Strips:
+    def __init__(self, refs, state, head):
+        self.refs, self.state, self.head = refs, state, head
+
+    def spread(self, k):
+        ref = self.refs[k]
+        if k in (0, 3):
+            parts = [ref[:hid, 4 * slot * b : (4 * b + 3) * slot] for b in range(3)]
+        else:
+            parts = [ref[b, :hid, : 3 * hid] for b in range(3)]
+        return jnp.concatenate(parts, axis=1)
+
+    def first(self):
+        linear = mm(self.spread(0), strip_taps(self.state)) + self.refs[4][:hid, 0:1]
+        sigma = sigma_of(linear)
+        act = linear * sigma
+        self.slope = sigma + act * (1.0 - sigma)
+        self.act_one = act.astype(bf16)
+
+    def second(self):
+        linear = mm(self.spread(1), strip_taps(self.act_one)) + self.refs[5][:hid, 0:1]
+        sigma = sigma_of(linear)
+        act = linear * sigma
+        grad = mm(self.spread(3), strip_taps(self.head)) * (sigma + act * (1.0 - sigma))
+        self.act_two = act.astype(bf16)
+        self.grad_two = grad.astype(bf16)
+
+    def back(self):
+        grad = mm(self.spread(2), strip_taps(self.grad_two)) * self.slope
+        self.grad_one = grad.astype(bf16)
 
 
 def layers(
     rows,
-    cols,
     groups,
     refs,
+    strips,
+    with_back,
+    first,
     state_in,
     act_one,
     slope_one,
@@ -165,19 +256,19 @@
     bias_acc,
 ):
     w_in_ref, w_mid_ref, w_mid_t_ref, w_out_t_ref, b_in_ref, b_mid_ref = refs
-    width = bias_acc.shape[2]
-    lane = lax.broadcasted_iota(jnp.int32, (1, width), 1)
-    own_cols = (lane >= halo) & (lane < halo + cols)
     groups_one, groups_two, groups_back, groups_in = groups
 
     w_in = w_in_ref[...]
     b_in = b_in_ref[:, 0:1]
+    strips.first()
     for r in groups_one:
         linear = mm(w_in, state_in.window(r - 1, r + 3, (0,))) + b_in
         sigma = sigma_of(linear)
         act = linear * sigma
-        act_one.put_shifted(r, act)
+        act_one.put_shifted(r, act, strips.act_one, first)
         slope_one.put(r, sigma + act * (1.0 - sigma))
+        if r == groups_one[0]:
+            strips.second()
 
     b_mid = b_mid_ref[:, 0:1]
     w_out_t = w_out_t_ref[...]
@@ -189,36 +280,35 @@
         linear = mm(w_mid, jnp.concatenate(window, axis=0)) + b_mid
         sigma = sigma_of(linear)
         act = linear * sigma
-        act_two.put(r, act.astype(bf16))
+        act_short = act.astype(bf16)
+        act_two.put(r, act_short)
         fed = state_in.window(r - 1, r + 3, (1,))
         grad = mm(w_out_t, fed) * (sigma + act * (1.0 - sigma))
-        grad_two.put_shifted(r, grad)
+        grad_two.put_shifted(r, grad, strips.grad_two, first)
+        if with_back and r == groups_two[0]:
+            strips.back()
         if halo <= r < halo + rows:
-            kept = jnp.where(own_cols, grad, 0.0)
-            bias_acc[0] += kept
-            kept = kept.astype(bf16)
-            held.append((kept, window, fed, jnp.where(own_cols, act, 0.0).astype(bf16)))
+            bias_acc[0] += grad
+            held.append((grad.astype(bf16), window, fed, act_short))
         if held and (len(held) == 2 or r == groups_two[-1]):
-            kepts, windows, feds, acts = zip(*held)
+            grads, windows, feds, acts = zip(*held)
             held = []
-            kepts = jnp.concatenate(kepts, axis=1)
+            grads = jnp.concatenate(grads, axis=1)
             for b in range(3):
-                acc_mid[b] += mm_nt(kepts, jnp.concatenate([w[b] for w in windows], axis=1))
+                acc_mid[b] += mm_nt(grads, jnp.concatenate([w[b] for w in windows], axis=1))
             acc_small[0] += mm_nt(jnp.concatenate(feds, axis=1), jnp.concatenate(acts, axis=1))
 
     for r in groups_back:
         grad = mm(w_mid_t, grad_two.window(r - 1, r + 3)) * slope_one.get(r, r + 2)
         grad_one.put(r, grad.astype(bf16))
-        kept = jnp.where(own_cols, grad, 0.0)
         if r < halo:
-            bias_acc[1, hid:, :] += kept[hid:, :]
+            bias_acc[1, hid:, :] += grad[hid:, :]
         elif r + 2 > halo + rows:
-            bias_acc[1, :hid, :] += kept[:hid, :]
+            bias_acc[1, :hid, :] += grad[:hid, :]
         else:
-            bias_acc[1] += kept
+            bias_acc[1] += grad
     for r in groups_in:
-        kept = jnp.where(own_cols, grad_one.get(r, r + 2), jnp.zeros((), bf16))
-        acc_small[1] += mm_nt(state_in.window(r - 1, r + 3, (0,)), kept)
+        acc_small[1] += mm_nt(state_in.window(r - 1, r + 3, (0,)), grad_one.get(r, r + 2))
 
 
 def inner_kernel(rows, cols, ext_ref, *refs):
@@ -231,13 +321,15 @@
     acc_small[...] = jnp.zeros(acc_small.shape, f32)
     bias_acc[...] = jnp.zeros(bias_acc.shape, f32)
     pairs = range(low, high, 2)
-    prepare(low, rows, cols, ext_ref, stage, planes, state_in, pairs, pairs)
+    _, strips = prepare(low, rows, cols, ext_ref, stage, planes, state_in, pairs, pairs)
     groups = [range(low + k, high - k, 2) for k in (1, 2, 3, 4)]
     layers(
         rows,
-        cols,
         groups,
         weight_refs,
+        Strips(weight_refs, *strips),
+        False,
+        low,
         state_in,
         Rows(hid, (low + 1, high - 1, act_one)),
         Rows(hid, (low + 1, high - 1, slope_one)),
@@ -257,7 +349,7 @@
 def outer_kernel(rows, cols, ext_ref, *refs):
     weight_refs, core_ref, refs = refs[:6], refs[6], refs[7:]
     act_one_in, slope_one_in, grad_two_in, grad_one_in, acc_mid_in, acc_small_in, bias_in, *refs = refs
-    keep_ref, send_ref, act_two, grad_one, *refs = refs
+    keep_ref, send_ref, act_two, grad_one, act_two_strip, grad_one_strip, *refs = refs
     pay, stage, planes, state_in, act_one, slope_one, grad_two, acc_mid, acc_small, bias_acc = refs
     low, high, deep = halo, halo + rows, rows + 2 * halo
     acc_mid[...] = acc_mid_in[...]
@@ -266,7 +358,7 @@
     state_in = Rows(slot, (0, deep, state_in))
     state_rows = [r for r in range(0, deep, 2) if r < low + 6 or r + 2 > high - 6]
     head_rows = [r for r in range(0, deep, 2) if r < low + 4 or r + 2 > high - 4]
-    sums = prepare(0, rows, cols, ext_ref, stage, planes, state_in, state_rows, head_rows)
+    sums, strips = prepare(0, rows, cols, ext_ref, stage, planes, state_in, state_rows, head_rows)
     bias_out = jnp.concatenate(sums + [jnp.zeros((128 - coef, stage.shape[2]), f32)], axis=0)
     groups = [
         [*range(k, low + k, 2), *range(high - k, deep - k, 2)] for k in (1, 2, 3)
@@ -277,11 +369,14 @@
         edges = [edge.at[i] for i in range(2)]
         return split_rows(hid, k, low + k, high - k, deep - k, edges[0], inner, edges[1])
 
+    strips = Strips(weight_refs, *strips)
     layers(
         rows,
-        cols,
         groups,
         weight_refs,
+        strips,
+        True,
+        0,
         state_in,
         both(1, act_one, act_one_in),
         both(1, slope_one, slope_one_in),
@@ -292,6 +387,9 @@
         acc_small,
         bias_acc,
     )
+
+    act_two_strip[...] = strips.act_two
+    grad_one_strip[...] = strips.grad_one
 
     for b in range(3):
         total = acc_mid[b, :hid, : 3 * hid] + acc_mid[b, hid:, hid:]
@@ -341,6 +439,8 @@
     act_two_edge,
     grad_one_in,
     grad_one_edge,
+    act_two_strip,
+    grad_one_strip,
     new_ref,
     grad_ref,
     stage,
@@ -357,22 +457,42 @@
     w0, w1, c0, c1 = stage[0], stage[1], stage[2], stage[3]
     head[...] = jnp.zeros(head.shape, f32)
     back[...] = jnp.zeros(back.shape, f32)
-    w_head = w_head_ref[...]
     b_head = b_head_ref[:, 0:1]
+    width = stage.shape[2]
+    blank = jnp.zeros((2 * slot, width - cols), f32)
+
+    def weighed(weight_ref, size, strip_ref):
+        weight = weight_ref[...]
+        alone = [weight[2 * size * b : (2 * b + 1) * size, : 3 * hid] for b in range(3)]
+        taps = strip_taps(strip_ref[...], (0,))
+        ends = mm(jnp.concatenate(alone, axis=0), taps)
+        ends = [ends[b * size : (b + 1) * size] for b in range(3)]
+
+        def pair(field, r):
+            part = mm(weight, field.get(r - 1, r + 3))
+            part = [part[2 * size * b : 2 * size * (b + 1)] for b in range(3)]
+            around = [
+                jnp.concatenate([strip_column(end, r + k, at, to) for k in range(2)], axis=0)
+                for end, at, to in ((ends[0], left_of, 0), (ends[2], right_of, cols - 1))
+            ]
+            low, middle, high = beside(*part, *around)
+            return low + middle + high
+
+        return ends, pair
+
+    ends, pair = weighed(w_head_ref, slot, act_two_strip)
+    head_strip = b_head[:slot] + ends[1] + shift(ends[0], 0, -1) + shift(ends[2], 0, 1)
     for r in range(3, deep - 3, 2):
-        part = mm(w_head, act_two.get(r - 1, r + 3))
-        size = 2 * slot
-        out = b_head
-        for b in range(3):
-            out = out + shift(part[b * size : (b + 1) * size], 0, b - 1)
+        out = jnp.concatenate([pair(act_two, r) + b_head, blank], axis=1)
+        out = pltpu.roll(out, halo, 1)
+        for at, to in ((left_of, halo - 1), (right_of, halo + cols)):
+            column = [strip_column(head_strip, r + k, at, to) for k in range(2)]
+            out = with_lane(out, to, jnp.concatenate(column, axis=0))
         put_rows(head, r * slot, out)
-    w_in_t = w_in_t_ref[...]
+    _, pair = weighed(w_in_t_ref, 8, grad_one_strip)
     for r in range(halo, halo + rows, 2):
-        part = mm(w_in_t, grad_one.get(r - 1, r + 3))
-        out = part[16:32]
-        for b in (0, 2):
-            out = out + shift(part[b * 16 : (b + 1) * 16], 0, b - 1)
-        put_rows(back, r * 8, out)
+        out = jnp.concatenate([pair(grad_one, r), blank[:16]], axis=1)
+        put_rows(back, r * 8, pltpu.roll(out, halo, 1))
 
     coefs = [take_plane(head, k, deep, slot) for k in range(coef)]
     mean_x = sum(coefs[1:6], coefs[0]) * (1.0 / 6.0)
@@ -586,7 +706,6 @@
     ny_total = lax.axis_size("gy") * cols
     cell_count = lax.axis_size("gx") * rows * ny_total
     deep = rows + 2 * halo
-    height = deep
     width = -(-(cols + 2 * halo) // 128) * 128
     vmem = pl.BlockSpec(memory_space=pltpu.VMEM)
     params = pltpu.CompilerParams(vmem_limit_bytes=18 << 20)
@@ -650,16 +769,17 @@
     accs = (
         jax.ShapeDtypeStruct((3, 2 * hid, 4 * hid), f32),
         jax.ShapeDtypeStruct((2, 12 * slot, 2 * hid), f32),
-        jax.ShapeDtypeStruct((2, 2 * hid, width), f32),
-    )
+        jax.ShapeDtypeStruct((2, 2 * hid, cols), f32),
+    )
+    strip = jax.ShapeDtypeStruct((hid, deep * pitch), bf16)
     act_one, slope_one, grad_two, act_two_in, grad_one_in, *totals = pl.pallas_call(
         lambda *refs: inner_kernel(rows, cols, *refs),
         out_shape=(
-            jax.ShapeDtypeStruct((3, (rows - 2) * hid, width), bf16),
-            jax.ShapeDtypeStruct(((rows - 2) * hid, width), f32),
-            jax.ShapeDtypeStruct((3, (rows - 4) * hid, width), bf16),
-            jax.ShapeDtypeStruct(((rows - 4) * hid, width), bf16),
-            jax.ShapeDtypeStruct(((rows - 6) * hid, width), bf16),
+            jax.ShapeDtypeStruct((3, (rows - 2) * hid, cols), bf16),
+            jax.ShapeDtypeStruct(((rows - 2) * hid, cols), f32),
+            jax.ShapeDtypeStruct((3, (rows - 4) * hid, cols), bf16),
+            jax.ShapeDtypeStruct(((rows - 4) * hid, cols), bf16),
+            jax.ShapeDtypeStruct(((rows - 6) * hid, cols), bf16),
             *accs,
         ),
         in_specs=[vmem] * 7,
@@ -667,30 +787,32 @@
         scratch_shapes=[
             pltpu.VMEM((4, rows, width), f32),
             pltpu.VMEM((width // 128, rows * slot, 128), f32),
-            pltpu.VMEM((2, 3, rows * slot, width), bf16),
+            pltpu.VMEM((2, 3, rows * slot, cols), bf16),
         ],
         compiler_params=params,
         name="inner",
     )(wide, *maps)
 
-    keep, send, act_two_edge, grad_one_edge = pl.pallas_call(
+    keep, send, act_two_edge, grad_one_edge, *strips = pl.pallas_call(
         lambda *refs: outer_kernel(rows, cols, *refs),
         out_shape=(
             jax.ShapeDtypeStruct((hid // 2, 12 * hid), bf16),
             jax.ShapeDtypeStruct((hid // 2, 12 * hid), bf16),
-            jax.ShapeDtypeStruct((2, halo * hid, width), bf16),
-            jax.ShapeDtypeStruct((2, halo * hid, width), bf16),
+            jax.ShapeDtypeStruct((2, halo * hid, cols), bf16),
+            jax.ShapeDtypeStruct((2, halo * hid, cols), bf16),
+            strip,
+            strip,
         ),
         in_specs=[vmem] * 7 + [smem] + [vmem] * 7,
-        out_specs=(vmem,) * 4,
+        out_specs=(vmem,) * 6,
         scratch_shapes=[
             pltpu.VMEM((2, hid // 2, 12 * hid), bf16),
             pltpu.VMEM((4, deep, width), f32),
             pltpu.VMEM((width // 128, deep * slot, 128), f32),
-            pltpu.VMEM((2, 3, deep * slot, width), bf16),
-            pltpu.VMEM((2, 3, halo * hid, width), bf16),
-            pltpu.VMEM((2, halo * hid, width), f32),
-            pltpu.VMEM((2, 3, halo * hid, width), bf16),
+            pltpu.VMEM((2, 3, deep * slot, cols), bf16),
+            pltpu.VMEM((2, 3, halo * hid, cols), bf16),
+            pltpu.VMEM((2, halo * hid, cols), f32),
+            pltpu.VMEM((2, 3, halo * hid, cols), bf16),
             *(pltpu.VMEM(acc.shape, f32) for acc in accs),
         ],
         compiler_params=params,
@@ -700,16 +822,16 @@
     new_velocity, grad_velocity = pl.pallas_call(
         lambda *refs: advance_kernel(rows, cols, *refs),
         out_shape=(jax.ShapeDtypeStruct(velocity.shape, f32),) * 2,
-        in_specs=[vmem] * 9,
+        in_specs=[vmem] * 11,
         out_specs=(vmem,) * 2,
         scratch_shapes=[
-            pltpu.VMEM((4, height, width), f32),
+            pltpu.VMEM((4, deep, width), f32),
             pltpu.VMEM((width // 128, deep * slot, 128), f32),
             pltpu.VMEM((width // 128, deep * 8, 128), f32),
         ],
         compiler_params=params,
         name="advance",
-    )(ext, forcing[None, :], w_head, b_head, w_in_t, act_two_in, act_two_edge, grad_one_in, grad_one_edge)
+    )(ext, forcing[None, :], w_head, b_head, w_in_t, act_two_in, act_two_edge, grad_one_in, grad_one_edge, *strips)
 
     mine, other, (new_velocity, grad_velocity) = summed(
         keep, send, (new_velocity, grad_velocity)

time: 33.8 us -> 33 us (0.976)
  waiting for transfers between devices: 8.08 us -> 6.82 us
  starting transfers between devices: 12.6 us -> 13.4 us
    ppermute x6, waiting for transfers between devices: 8.07 us -> 6.81 us  [swap(): return lax.ppermute(value, ('gx', 'gy'), pairs)]
    pallas_call x1, Pallas kernels: 4.05 us -> 3.24 us  [per_device(): pl.pallas_call(lambda *refs: inner_kernel(rows, cols, *refs), out_shape=(...]
    ppermute x6, starting transfers between devices: 5.06 us -> 5.86 us  [swap(): return lax.ppermute(value, ('gx', 'gy'), pairs)]
    pallas_call x1, Pallas kernels: 1.69 us -> 2.15 us  [per_device(): pl.pallas_call(lambda *refs: advance_kernel(rows, cols, *refs), out_shape...]
where the time goes in v4:
time: 33 us; the launch traced here: 32.8 us
  starting transfers between devices  13.4 us (41%)
  Pallas kernels  11.5 us (35%)
  waiting for transfers between devices  6.82 us (21%)
  between operations  0.78 us (2%)
  other arithmetic  0.38 us (1%)
    ppermute x6, waiting for transfers between devices, swap(): return lax.ppermute(value, ('gx', 'gy'), pairs)  6.81 us
    ppermute x6, starting transfers between devices, swap(): return lax.ppermute(value, ('gx', 'gy'), pairs)  5.86 us
    ppermute x2, starting transfers between devices, widened(): far = lax.ppermute(far, axis, far_pairs)  4.92 us
    pallas_call x1, Pallas kernels, per_device(): pl.pallas_call(lambda *refs: inner_kernel(rows, cols, *refs), out_shape=(...  3.24 us
    pallas_call x1, Pallas kernels, per_device(): pl.pallas_call(lambda *refs: outer_kernel(rows, cols, *refs), out_shape=(...  2.88 us
    ppermute x2, starting transfers between devices, widened(): near = lax.ppermute(near, axis, [(i, i ^ 1) for i in range(count)])  2.62 us
    pallas_call x1, Pallas kernels, per_device(): pl.pallas_call(lambda *refs: advance_kernel(rows, cols, *refs), out_shape...  2.15 us
    pallas_call x1, Pallas kernels, per_device(): pl.pallas_call(weights_kernel, out_shape=(jax.ShapeDtypeStruct((2 * hid,...  1.35 us
  transfers between devices with their start and end apart: 10, of which 6 were waited for; matrix products, arithmetic and copies ran while one was open for 0% of the time, Pallas kernels for 21%

profile of v4, /device:TPU:0, one launch (start us, length us, event | category | flops | bytes accessed | tf_op | source)
XLA Modules:
  0.0 32.8 jit_solution(4236430952859150609)
XLA Ops:
  0.6 0.9 %pack.1 = (f32[4,16,256]{2,1,0:T(8,128)S(1)}, bf16[4,16,4]{2,1,0:T(8,128)(2,1)S(1)}, bf16[4,16,4]{2,1,0:T(8,128)(2,1)S(1)}) custom-call(s32[1]{0:T(128)} %bitcast.even_ref, f32[2,16,256]{2,1,0:T(8,128)} %velocity_ref.1, f32[2,16,256]{2,1,0:T(8,128)} %cotangent_ref.1), custom_call_target="tpu_custom_call" | custom-call | tf_op jit(solution)/shard_map/pack/pallas_call | solution.py:754
  1.6 2.4 %collective-permute-start = (bf16[4,16,4]{2,1,0:T(8,128)(2,1)S(1)}, bf16[4,16,4]{2,1,0:T(8,128)(2,1)S(1)}, u32[]{:S(2)}, u32[]{:S(2)}) collective-permute-start(bf16[4,16,4]{2,1,0:T(8,128)(2,1)S(1)} %get-tuple-element.52), channel_id=1, source_target_pairs={{0,3},{1,2},{2,1},{3,0},{4,7},{5,6},{6,5},{7,4},{8,11},{9,10},{10,... | collective-permute-start | bytes 1544 | tf_op jit(solution)/shard_map/ppermute | solution.py:659
  4.0 0.7 %collective-permute-start.1 = (bf16[4,16,4]{2,1,0:T(8,128)(2,1)S(1)}, bf16[4,16,4]{2,1,0:T(8,128)(2,1)S(1)}, u32[]{:S(2)}, u32[]{:S(2)}) collective-permute-start(bf16[4,16,4]{2,1,0:T(8,128)(2,1)S(1)} %get-tuple-element.53), channel_id=1, source_target_pairs={{0,1},{1,0},{2,3},{3,2},{4,5},{5,4},{6,7},{7,6},{8,9},{9,8},{10,11... | collective-permute-start | bytes 1544 | tf_op jit(solution)/shard_map/ppermute | solution.py:660
  4.7 1.4 %weights.1 = (bf16[128,192]{1,0:T(8,128)(2,1)S(1)}, bf16[3,128,256]{2,1,0:T(8,128)(2,1)S(1)}, bf16[3,128,256]{2,1,0:T(8,128)(2,1)S(1)}, bf16[128,192]{1,0:T(8,12...) custom-call(bf16[9,2,64]{2,1,0:T(2,128)(2,1)} %bitcast.24, ...), custom_call_target="tpu_custom_call" | custom-call | tf_op jit(solution)/shard_map/weights/pallas_call | solution.py:716
  6.1 0.0 collective-permute-done
  6.1 0.0 collective-permute-done.1
  6.1 0.1 fusion
  6.2 1.9 %collective-permute-start.3 = (bf16[4,4,264]{2,1,0:T(4,128)(2,1)S(1)}, bf16[4,4,264]{2,1,0:T(4,128)(2,1)S(1)}, u32[]{:S(2)}, u32[]{:S(2)}) collective-permute-start(bf16[4,4,264]{2,1,0:T(4,128)(2,1)S(1)} %get-tuple-element.61), channel_id=1, source_target_pairs={{0,4},{4,0},{8,12},{12,8},{1,5},{5,1},{9,13},{13,9},{2,6},{6,2},{1... | collective-permute-start | bytes 25352 | tf_op jit(solution)/shard_map/ppermute | solution.py:660
  8.2 2.5 %collective-permute-start.2 = (bf16[4,4,264]{2,1,0:T(4,128)(2,1)S(1)}, bf16[4,4,264]{2,1,0:T(4,128)(2,1)S(1)}, u32[]{:S(2)}, u32[]{:S(2)}) collective-permute-start(bf16[4,4,264]{2,1,0:T(4,128)(2,1)S(1)} %get-tuple-element.98), channel_id=1, source_target_pairs={{0,12},{4,8},{8,4},{12,0},{1,13},{5,9},{9,5},{13,1},{2,14},{6,10},... | collective-permute-start | bytes 25352 | tf_op jit(solution)/shard_map/ppermute | solution.py:659
  10.7 3.2 %inner.1 = (bf16[3,896,256]{2,1,0:T(8,128)(2,1)S(1)}, f32[896,256]{1,0:T(8,128)S(1)}, bf16[3,768,256]{2,1,0:T(8,128)(2,1)S(1)}, bf16[768,256]{1,0:T(8,128)(2,1)S...) custom-call(f32[4,16,264]{2,1,0:T(8,128)S(1)} %get-tuple-element.97., ...), custom_call_target="tpu_custom_call" | custom-call | tf_op jit(solution)/shard_map/inner/pallas_call | solution.py:775
  13.9 0.0 collective-permute-done.3
  13.9 0.0 collective-permute-done.2
  14.0 0.1 pad_maximum_fusion.refs_0_
  14.1 2.9 %outer.1 = (bf16[32,768]{1,0:T(8,128)(2,1)S(1)}, bf16[32,768]{1,0:T(8,128)(2,1)S(1)}, bf16[2,256,256]{2,1,0:T(8,128)(2,1)S(1)}, bf16[2,256,256]{2,1,0:T(8,128)(2...) custom-call(f32[4,24,264]{2,1,0:T(8,128)S(1)} %pad_maximum_fusion.refs_0_, ...), custom_call_target="tpu_custom_call" | custom-call | tf_op jit(solution)/shard_map/outer/pallas_call | solution.py:796
  17.0 0.1 collective-permute-start.4
  17.0 1.2 %collective-permute-done.4 = bf16[32,768]{1,0:T(8,128)(2,1)S(1)} collective-permute-done((bf16[32,768]{1,0:T(8,128)(2,1)S(1)}, bf16[32,768]{1,0:T(8,128)(2,1)S(1)}, u32[]{:S(2)}, u32[]{:S(2)}) %collective-permute-start.4) | collective-permute-done | bytes 49184 | tf_op jit(solution)/shard_map/ppermute | solution.py:671
  18.3 1.6 %collective-permute-start.5 = (bf16[32,768]{1,0:T(8,128)(2,1)S(1)}, bf16[32,768]{1,0:T(8,128)(2,1)S(1)}, u32[]{:S(2)}, u32[]{:S(2)}) collective-permute-start(bf16[32,768]{1,0:T(8,128)(2,1)S(1)} %add_convert_fusion.2), channel_id=1, source_target_pairs={{0,2},{1,3},{2,0},{3,1},{4,6},{5,7},{6,4},{7,5},{8,10},{9,11},{10,... | collective-permute-start | bytes 147464 | tf_op jit(solution)/shard_map/ppermute | solution.py:671
  19.9 0.7 %collective-permute-start.6 = (bf16[32,768]{1,0:T(8,128)(2,1)S(1)}, bf16[32,768]{1,0:T(8,128)(2,1)S(1)}, u32[]{:S(2)}, u32[]{:S(2)}) collective-permute-start(bf16[32,768]{1,0:T(8,128)(2,1)S(1)} %add_convert_fusion.2), channel_id=1, source_target_pairs={{0,4},{1,5},{2,6},{3,7},{4,0},{5,1},{6,2},{7,3},{8,12},{9,13},{10,... | collective-permute-start | bytes 147464 | tf_op jit(solution)/shard_map/ppermute | solution.py:671
  20.6 1.3 %collective-permute-start.7 = (bf16[32,768]{1,0:T(8,128)(2,1)S(1)}, bf16[32,768]{1,0:T(8,128)(2,1)S(1)}, u32[]{:S(2)}, u32[]{:S(2)}) collective-permute-start(bf16[32,768]{1,0:T(8,128)(2,1)S(1)} %add_convert_fusion.2), channel_id=1, source_target_pairs={{0,6},{1,7},{2,4},{3,5},{4,2},{5,3},{6,0},{7,1},{8,14},{9,15},{10,... | collective-permute-start | bytes 147464 | tf_op jit(solution)/shard_map/ppermute | solution.py:671
  21.8 0.6 %collective-permute-done.5 = bf16[32,768]{1,0:T(8,128)(2,1)S(1)} collective-permute-done((bf16[32,768]{1,0:T(8,128)(2,1)S(1)}, bf16[32,768]{1,0:T(8,128)(2,1)S(1)}, u32[]{:S(2)}, u32[]{:S(2)}) %collective-permute-start.5) | collective-permute-done | bytes 49184 | tf_op jit(solution)/shard_map/ppermute | solution.py:671
  22.4 1.5 %collective-permute-done.6 = bf16[32,768]{1,0:T(8,128)(2,1)S(1)} collective-permute-done((bf16[32,768]{1,0:T(8,128)(2,1)S(1)}, bf16[32,768]{1,0:T(8,128)(2,1)S(1)}, u32[]{:S(2)}, u32[]{:S(2)}) %collective-permute-start.6) | collective-permute-done | bytes 49184 | tf_op jit(solution)/shard_map/ppermute | solution.py:671
  24.0 1.6 %collective-permute-done.7 = bf16[32,768]{1,0:T(8,128)(2,1)S(1)} collective-permute-done((bf16[32,768]{1,0:T(8,128)(2,1)S(1)}, bf16[32,768]{1,0:T(8,128)(2,1)S(1)}, u32[]{:S(2)}, u32[]{:S(2)}) %collective-permute-start.7) | collective-permute-done | bytes 49184 | tf_op jit(solution)/shard_map/ppermute | solution.py:671
  25.6 2.2 %collective-permute-start.8 = (bf16[32,768]{1,0:T(8,128)(2,1)S(1)}, bf16[32,768]{1,0:T(8,128)(2,1)S(1)}, u32[]{:S(2)}, u32[]{:S(2)}) collective-permute-start(bf16[32,768]{1,0:T(8,128)(2,1)S(1)} %add_convert_fusion.1), channel_id=1, source_target_pairs={{0,8},{1,9},{2,10},{3,11},{4,12},{5,13},{6,14},{7,15},{8,0},{9,1},... | collective-permute-start | bytes 147464 | tf_op jit(solution)/shard_map/ppermute | solution.py:671
  27.7 0.1 sine_multiply_fusion.refs_1_
  27.8 2.1 %advance.1 = (f32[2,16,256]{2,1,0:T(8,128)}, f32[2,16,256]{2,1,0:T(8,128)}) custom-call(f32[4,24,264]{2,1,0:T(8,128)S(1)} %pad_maximum_fusion.refs_0_, f32[1,384]{1,0:T(1,128)S(1)} %sine_multiply_fusion.refs_1_, bf16[96,256]{1,0:T(8,128)(2,1)S(1)} %get-tuple-element.77.refs_2_, f32[32,128]{1,0:T(8,128)S(1)} %get-tuple-element.78.refs_3_, ...), custom_call_target="tpu_custom_call" | custom-call | tf_op jit(solution)/shard_map/advance/pallas_call | solution.py:822
  29.9 0.7 %collective-permute-done.8 = bf16[32,768]{1,0:T(8,128)(2,1)S(1)} collective-permute-done((bf16[32,768]{1,0:T(8,128)(2,1)S(1)}, bf16[32,768]{1,0:T(8,128)(2,1)S(1)}, u32[]{:S(2)}, u32[]{:S(2)}) %collective-permute-start.8) | collective-permute-done | bytes 49184 | tf_op jit(solution)/shard_map/ppermute | solution.py:671
  30.6 0.1 collective-permute-start.9
  30.7 1.2 %collective-permute-done.9.refs_1_ = bf16[32,768]{1,0:T(8,128)(2,1)S(1)} collective-permute-done((bf16[32,768]{1,0:T(8,128)(2,1)S(1)}, bf16[32,768]{1,0:T(8,128)(2,1)S(1)}, u32[]{:S(2)}, u32[]{:S(2)}) %collective-permute-start.9) | collective-permute-done | bytes 49184 | tf_op jit(solution)/shard_map/ppermute | solution.py:671
  31.9 0.9 %finish.1 = (f32[9,2,64]{2,1,0:T(2,128)}, f32[1,64]{1,0:T(1,128)}, f32[9,64,64]{2,1,0:T(8,128)}, f32[1,64]{1,0:T(1,128)}, f32[12,3,3,64]{3,2,1,0:T(4,128)}, /*index=5*/f32[1,12]{1,0:T(1,128)}) custom-call(bf16[32,768]{1,0:T(8,128)(2,1)S(1)} %add_convert_fusion.refs_0_, bf16[32,768]{1,0:T(8,128)(2,1)S(1)} %collective-permute-done.9.refs_1_, ...), custom_call_target="tpu_custom_call" | custom-call | tf_op jit(solution)/shard_map/finish/pallas_call | solution.py:839
  (6 shorter events, 0.1 us)
Async XLA Ops:
  1.6 4.5 %collective-permute-start = (bf16[4,16,4]{2,1,0:T(8,128)(2,1)S(1)}, bf16[4,16,4]{2,1,0:T(8,128)(2,1)S(1)}, u32[]{:S(2)}, u32[]{:S(2)}) collective-permute-start(bf16[4,16,4]{2,1,0:T(8,128)(2,1)S(1)} %get-tuple-element.52), channel_id=1, source_target_pairs={{0,3},{1,2},{2,1},{3,0},{4,7},{5,6},{6,5},{7,4},{8,11},{9,10},{10,... | collective-permute-start | bytes 1544 | tf_op jit(solution)/shard_map/ppermute | solution.py:659
  4.0 2.1 %collective-permute-start.1 = (bf16[4,16,4]{2,1,0:T(8,128)(2,1)S(1)}, bf16[4,16,4]{2,1,0:T(8,128)(2,1)S(1)}, u32[]{:S(2)}, u32[]{:S(2)}) collective-permute-start(bf16[4,16,4]{2,1,0:T(8,128)(2,1)S(1)} %get-tuple-element.53), channel_id=1, source_target_pairs={{0,1},{1,0},{2,3},{3,2},{4,5},{5,4},{6,7},{7,6},{8,9},{9,8},{10,11... | collective-permute-start | bytes 1544 | tf_op jit(solution)/shard_map/ppermute | solution.py:660
  6.2 7.7 %collective-permute-start.3 = (bf16[4,4,264]{2,1,0:T(4,128)(2,1)S(1)}, bf16[4,4,264]{2,1,0:T(4,128)(2,1)S(1)}, u32[]{:S(2)}, u32[]{:S(2)}) collective-permute-start(bf16[4,4,264]{2,1,0:T(4,128)(2,1)S(1)} %get-tuple-element.61), channel_id=1, source_target_pairs={{0,4},{4,0},{8,12},{12,8},{1,5},{5,1},{9,13},{13,9},{2,6},{6,2},{1... | collective-permute-start | bytes 25352 | tf_op jit(solution)/shard_map/ppermute | solution.py:660
  8.2 5.7 %collective-permute-start.2 = (bf16[4,4,264]{2,1,0:T(4,128)(2,1)S(1)}, bf16[4,4,264]{2,1,0:T(4,128)(2,1)S(1)}, u32[]{:S(2)}, u32[]{:S(2)}) collective-permute-start(bf16[4,4,264]{2,1,0:T(4,128)(2,1)S(1)} %get-tuple-element.98), channel_id=1, source_target_pairs={{0,12},{4,8},{8,4},{12,0},{1,13},{5,9},{9,5},{13,1},{2,14},{6,10},... | collective-permute-start | bytes 25352 | tf_op jit(solution)/shard_map/ppermute | solution.py:659
  17.0 1.3 %collective-permute-start.4 = (bf16[32,768]{1,0:T(8,128)(2,1)S(1)}, bf16[32,768]{1,0:T(8,128)(2,1)S(1)}, u32[]{:S(2)}, u32[]{:S(2)}) collective-permute-start(bf16[32,768]{1,0:T(8,128)(2,1)S(1)} %get-tuple-element.76), channel_id=1, source_target_pairs={{0,1},{1,0},{2,3},{3,2},{4,5},{5,4},{6,7},{7,6},{8,9},{9,8},{10,11... | collective-permute-start | bytes 147464 | tf_op jit(solution)/shard_map/ppermute | solution.py:671
  18.3 4.2 %collective-permute-start.5 = (bf16[32,768]{1,0:T(8,128)(2,1)S(1)}, bf16[32,768]{1,0:T(8,128)(2,1)S(1)}, u32[]{:S(2)}, u32[]{:S(2)}) collective-permute-start(bf16[32,768]{1,0:T(8,128)(2,1)S(1)} %add_convert_fusion.2), channel_id=1, source_target_pairs={{0,2},{1,3},{2,0},{3,1},{4,6},{5,7},{6,4},{7,5},{8,10},{9,11},{10,... | collective-permute-start | bytes 147464 | tf_op jit(solution)/shard_map/ppermute | solution.py:671
  19.9 4.1 %collective-permute-start.6 = (bf16[32,768]{1,0:T(8,128)(2,1)S(1)}, bf16[32,768]{1,0:T(8,128)(2,1)S(1)}, u32[]{:S(2)}, u32[]{:S(2)}) collective-permute-start(bf16[32,768]{1,0:T(8,128)(2,1)S(1)} %add_convert_fusion.2), channel_id=1, source_target_pairs={{0,4},{1,5},{2,6},{3,7},{4,0},{5,1},{6,2},{7,3},{8,12},{9,13},{10,... | collective-permute-start | bytes 147464 | tf_op jit(solution)/shard_map/ppermute | solution.py:671
  20.6 5.0 %collective-permute-start.7 = (bf16[32,768]{1,0:T(8,128)(2,1)S(1)}, bf16[32,768]{1,0:T(8,128)(2,1)S(1)}, u32[]{:S(2)}, u32[]{:S(2)}) collective-permute-start(bf16[32,768]{1,0:T(8,128)(2,1)S(1)} %add_convert_fusion.2), channel_id=1, source_target_pairs={{0,6},{1,7},{2,4},{3,5},{4,2},{5,3},{6,0},{7,1},{8,14},{9,15},{10,... | collective-permute-start | bytes 147464 | tf_op jit(solution)/shard_map/ppermute | solution.py:671
  25.6 5.1 %collective-permute-start.8 = (bf16[32,768]{1,0:T(8,128)(2,1)S(1)}, bf16[32,768]{1,0:T(8,128)(2,1)S(1)}, u32[]{:S(2)}, u32[]{:S(2)}) collective-permute-start(bf16[32,768]{1,0:T(8,128)(2,1)S(1)} %add_convert_fusion.1), channel_id=1, source_target_pairs={{0,8},{1,9},{2,10},{3,11},{4,12},{5,13},{6,14},{7,15},{8,0},{9,1},... | collective-permute-start | bytes 147464 | tf_op jit(solution)/shard_map/ppermute | solution.py:671
  30.6 1.3 %collective-permute-start.9 = (bf16[32,768]{1,0:T(8,128)(2,1)S(1)}, bf16[32,768]{1,0:T(8,128)(2,1)S(1)}, u32[]{:S(2)}, u32[]{:S(2)}) collective-permute-start(bf16[32,768]{1,0:T(8,128)(2,1)S(1)} %add_convert_fusion.refs_0_), channel_id=1, source_target_pairs={{0,1},{1,0},{2,3},{3,2},{4,5},{5,4},{6,7},{7,6},{8,9},{9,8},{10,11... | collective-permute-start | bytes 147464 | tf_op jit(solution)/shard_map/ppermute | solution.py:671

commit v5 on v4

--- a/solution.py
+++ b/solution.py
@@ -233,17 +233,12 @@
         self.act_two = act.astype(bf16)
         self.grad_two = grad.astype(bf16)
 
-    def back(self):
-        grad = mm(self.spread(2), strip_taps(self.grad_two)) * self.slope
-        self.grad_one = grad.astype(bf16)
-
 
 def layers(
     rows,
     groups,
     refs,
     strips,
-    with_back,
     first,
     state_in,
     act_one,
@@ -285,8 +280,6 @@
         fed = state_in.window(r - 1, r + 3, (1,))
         grad = mm(w_out_t, fed) * (sigma + act * (1.0 - sigma))
         grad_two.put_shifted(r, grad, strips.grad_two, first)
-        if with_back and r == groups_two[0]:
-            strips.back()
         if halo <= r < halo + rows:
             bias_acc[0] += grad
             held.append((grad.astype(bf16), window, fed, act_short))
@@ -328,7 +321,6 @@
         groups,
         weight_refs,
         Strips(weight_refs, *strips),
-        False,
         low,
         state_in,
         Rows(hid, (low + 1, high - 1, act_one)),
@@ -349,7 +341,7 @@
 def outer_kernel(rows, cols, ext_ref, *refs):
     weight_refs, core_ref, refs = refs[:6], refs[6], refs[7:]
     act_one_in, slope_one_in, grad_two_in, grad_one_in, acc_mid_in, acc_small_in, bias_in, *refs = refs
-    keep_ref, send_ref, act_two, grad_one, act_two_strip, grad_one_strip, *refs = refs
+    keep_ref, send_ref, act_two, grad_one, act_two_strip, grad_two_strip, slope_strip, *refs = refs
     pay, stage, planes, state_in, act_one, slope_one, grad_two, acc_mid, acc_small, bias_acc = refs
     low, high, deep = halo, halo + rows, rows + 2 * halo
     acc_mid[...] = acc_mid_in[...]
@@ -375,7 +367,6 @@
         groups,
         weight_refs,
         strips,
-        True,
         0,
         state_in,
         both(1, act_one, act_one_in),
@@ -389,7 +380,8 @@
     )
 
     act_two_strip[...] = strips.act_two
-    grad_one_strip[...] = strips.grad_one
+    grad_two_strip[...] = strips.grad_two
+    slope_strip[...] = strips.slope
 
     for b in range(3):
         total = acc_mid[b, :hid, : 3 * hid] + acc_mid[b, hid:, hid:]
@@ -440,7 +432,9 @@
     grad_one_in,
     grad_one_edge,
     act_two_strip,
-    grad_one_strip,
+    grad_two_strip,
+    slope_strip,
+    w_mid_t_ref,
     new_ref,
     grad_ref,
     stage,
@@ -461,10 +455,10 @@
     width = stage.shape[2]
     blank = jnp.zeros((2 * slot, width - cols), f32)
 
-    def weighed(weight_ref, size, strip_ref):
+    def weighed(weight_ref, size, strip):
         weight = weight_ref[...]
         alone = [weight[2 * size * b : (2 * b + 1) * size, : 3 * hid] for b in range(3)]
-        taps = strip_taps(strip_ref[...], (0,))
+        taps = strip_taps(strip, (0,))
         ends = mm(jnp.concatenate(alone, axis=0), taps)
         ends = [ends[b * size : (b + 1) * size] for b in range(3)]
 
@@ -480,7 +474,7 @@
 
         return ends, pair
 
-    ends, pair = weighed(w_head_ref, slot, act_two_strip)
+    ends, pair = weighed(w_head_ref, slot, act_two_strip[...])
     head_strip = b_head[:slot] + ends[1] + shift(ends[0], 0, -1) + shift(ends[2], 0, 1)
     for r in range(3, deep - 3, 2):
         out = jnp.concatenate([pair(act_two, r) + b_head, blank], axis=1)
@@ -489,7 +483,9 @@
             column = [strip_column(head_strip, r + k, at, to) for k in range(2)]
             out = with_lane(out, to, jnp.concatenate(column, axis=0))
         put_rows(head, r * slot, out)
-    _, pair = weighed(w_in_t_ref, 8, grad_one_strip)
+    spread = jnp.concatenate([w_mid_t_ref[b, :hid, : 3 * hid] for b in range(3)], axis=1)
+    grad_one_strip = mm(spread, strip_taps(grad_two_strip[...])) * slope_strip[...]
+    _, pair = weighed(w_in_t_ref, 8, grad_one_strip.astype(bf16))
     for r in range(halo, halo + rows, 2):
         out = jnp.concatenate([pair(grad_one, r), blank[:16]], axis=1)
         put_rows(back, r * 8, pltpu.roll(out, halo, 1))
@@ -802,9 +798,10 @@
             jax.ShapeDtypeStruct((2, halo * hid, cols), bf16),
             strip,
             strip,
+            jax.ShapeDtypeStruct(strip.shape, f32),
         ),
         in_specs=[vmem] * 7 + [smem] + [vmem] * 7,
-        out_specs=(vmem,) * 6,
+        out_specs=(vmem,) * 7,
         scratch_shapes=[
             pltpu.VMEM((2, hid // 2, 12 * hid), bf16),
             pltpu.VMEM((4, deep, width), f32),
@@ -822,7 +819,7 @@
     new_velocity, grad_velocity = pl.pallas_call(
         lambda *refs: advance_kernel(rows, cols, *refs),
         out_shape=(jax.ShapeDtypeStruct(velocity.shape, f32),) * 2,
-        in_specs=[vmem] * 11,
+        in_specs=[vmem] * 13,
         out_specs=(vmem,) * 2,
         scratch_shapes=[
             pltpu.VMEM((4, deep, width), f32),
@@ -831,7 +828,7 @@
         ],
         compiler_params=params,
         name="advance",
-    )(ext, forcing[None, :], w_head, b_head, w_in_t, act_two_in, act_two_edge, grad_one_in, grad_one_edge, *strips)
+    )(ext, forcing[None, :], w_head, b_head, w_in_t, act_two_in, act_two_edge, grad_one_in, grad_one_edge, *strips, w_mid_t)
 
     mine, other, (new_velocity, grad_velocity) = summed(
         keep, send, (new_velocity, grad_velocity)

time: 33 us -> 32.9 us (level)
  no operation moved by 1% of the time
where the time goes in v5:
time: 32.9 us; the launch traced here: 32.7 us
  starting transfers between devices  13.4 us (41%)
  Pallas kernels  11.5 us (35%)
  waiting for transfers between devices  6.59 us (20%)
  between operations  0.78 us (2%)
  other arithmetic  0.39 us (1%)
    ppermute x6, waiting for transfers between devices, swap(): return lax.ppermute(value, ('gx', 'gy'), pairs)  6.58 us
    ppermute x6, starting transfers between devices, swap(): return lax.ppermute(value, ('gx', 'gy'), pairs)  5.86 us
    ppermute x2, starting transfers between devices, widened(): far = lax.ppermute(far, axis, far_pairs)  4.92 us
    pallas_call x1, Pallas kernels, per_device(): pl.pallas_call(lambda *refs: inner_kernel(rows, cols, *refs), out_shape=(...  3.24 us
    pallas_call x1, Pallas kernels, per_device(): pl.pallas_call(lambda *refs: outer_kernel(rows, cols, *refs), out_shape=(...  2.71 us
    ppermute x2, starting transfers between devices, widened(): near = lax.ppermute(near, axis, [(i, i ^ 1) for i in range(count)])  2.62 us
    pallas_call x1, Pallas kernels, per_device(): pl.pallas_call(lambda *refs: advance_kernel(rows, cols, *refs), out_shape...  2.37 us
    pallas_call x1, Pallas kernels, per_device(): pl.pallas_call(weights_kernel, out_shape=(jax.ShapeDtypeStruct((2 * hid,...  1.35 us
  transfers between devices with their start and end apart: 10, of which 6 were waited for; matrix products, arithmetic and copies ran while one was open for 0% of the time, Pallas kernels for 21%

profile of v5, /device:TPU:0, one launch (start us, length us, event | category | flops | bytes accessed | tf_op | source)
XLA Modules:
  0.0 32.7 jit_solution(6328681469578384567)
XLA Ops:
  0.6 0.9 %pack.1 = (f32[4,16,256]{2,1,0:T(8,128)S(1)}, bf16[4,16,4]{2,1,0:T(8,128)(2,1)S(1)}, bf16[4,16,4]{2,1,0:T(8,128)(2,1)S(1)}) custom-call(s32[1]{0:T(128)} %bitcast.even_ref, f32[2,16,256]{2,1,0:T(8,128)} %velocity_ref.1, f32[2,16,256]{2,1,0:T(8,128)} %cotangent_ref.1), custom_call_target="tpu_custom_call" | custom-call | tf_op jit(solution)/shard_map/pack/pallas_call | solution.py:750
  1.6 2.4 %collective-permute-start = (bf16[4,16,4]{2,1,0:T(8,128)(2,1)S(1)}, bf16[4,16,4]{2,1,0:T(8,128)(2,1)S(1)}, u32[]{:S(2)}, u32[]{:S(2)}) collective-permute-start(bf16[4,16,4]{2,1,0:T(8,128)(2,1)S(1)} %get-tuple-element.53), channel_id=1, source_target_pairs={{0,3},{1,2},{2,1},{3,0},{4,7},{5,6},{6,5},{7,4},{8,11},{9,10},{10,... | collective-permute-start | bytes 1544 | tf_op jit(solution)/shard_map/ppermute | solution.py:655
  4.0 0.7 %collective-permute-start.1 = (bf16[4,16,4]{2,1,0:T(8,128)(2,1)S(1)}, bf16[4,16,4]{2,1,0:T(8,128)(2,1)S(1)}, u32[]{:S(2)}, u32[]{:S(2)}) collective-permute-start(bf16[4,16,4]{2,1,0:T(8,128)(2,1)S(1)} %get-tuple-element.54), channel_id=1, source_target_pairs={{0,1},{1,0},{2,3},{3,2},{4,5},{5,4},{6,7},{7,6},{8,9},{9,8},{10,11... | collective-permute-start | bytes 1544 | tf_op jit(solution)/shard_map/ppermute | solution.py:656
  4.7 1.4 %weights.1 = (bf16[128,192]{1,0:T(8,128)(2,1)S(1)}, bf16[3,128,256]{2,1,0:T(8,128)(2,1)S(1)}, bf16[3,128,256]{2,1,0:T(8,128)(2,1)S(1)}, bf16[128,192]{1,0:T(8,12...) custom-call(bf16[9,2,64]{2,1,0:T(2,128)(2,1)} %bitcast.24, ...), custom_call_target="tpu_custom_call" | custom-call | tf_op jit(solution)/shard_map/weights/pallas_call | solution.py:712
  6.1 0.0 collective-permute-done
  6.1 0.0 collective-permute-done.1
  6.1 0.1 fusion
  6.2 1.9 %collective-permute-start.3 = (bf16[4,4,264]{2,1,0:T(4,128)(2,1)S(1)}, bf16[4,4,264]{2,1,0:T(4,128)(2,1)S(1)}, u32[]{:S(2)}, u32[]{:S(2)}) collective-permute-start(bf16[4,4,264]{2,1,0:T(4,128)(2,1)S(1)} %get-tuple-element.62), channel_id=1, source_target_pairs={{0,4},{4,0},{8,12},{12,8},{1,5},{5,1},{9,13},{13,9},{2,6},{6,2},{1... | collective-permute-start | bytes 25352 | tf_op jit(solution)/shard_map/ppermute | solution.py:656
  8.2 2.5 %collective-permute-start.2 = (bf16[4,4,264]{2,1,0:T(4,128)(2,1)S(1)}, bf16[4,4,264]{2,1,0:T(4,128)(2,1)S(1)}, u32[]{:S(2)}, u32[]{:S(2)}) collective-permute-start(bf16[4,4,264]{2,1,0:T(4,128)(2,1)S(1)} %get-tuple-element.100), channel_id=1, source_target_pairs={{0,12},{4,8},{8,4},{12,0},{1,13},{5,9},{9,5},{13,1},{2,14},{6,10},... | collective-permute-start | bytes 25352 | tf_op jit(solution)/shard_map/ppermute | solution.py:655
  10.7 3.2 %inner.1 = (bf16[3,896,256]{2,1,0:T(8,128)(2,1)S(1)}, f32[896,256]{1,0:T(8,128)S(1)}, bf16[3,768,256]{2,1,0:T(8,128)(2,1)S(1)}, bf16[768,256]{1,0:T(8,128)(2,1)S...) custom-call(f32[4,16,264]{2,1,0:T(8,128)S(1)} %get-tuple-element.99., ...), custom_call_target="tpu_custom_call" | custom-call | tf_op jit(solution)/shard_map/inner/pallas_call | solution.py:771
  13.9 0.0 collective-permute-done.3
  13.9 0.0 collective-permute-done.2
  14.0 0.1 pad_maximum_fusion.refs_0_
  14.1 2.7 %outer.1 = (bf16[32,768]{1,0:T(8,128)(2,1)S(1)}, bf16[32,768]{1,0:T(8,128)(2,1)S(1)}, bf16[2,256,256]{2,1,0:T(8,128)(2,1)S(1)}, bf16[2,256,256]{2,1,0:T(8,128)(2...) custom-call(f32[4,24,264]{2,1,0:T(8,128)S(1)} %pad_maximum_fusion.refs_0_, ...), custom_call_target="tpu_custom_call" | custom-call | tf_op jit(solution)/shard_map/outer/pallas_call | solution.py:792
  16.8 0.1 collective-permute-start.4
  16.9 1.2 %collective-permute-done.4 = bf16[32,768]{1,0:T(8,128)(2,1)S(1)} collective-permute-done((bf16[32,768]{1,0:T(8,128)(2,1)S(1)}, bf16[32,768]{1,0:T(8,128)(2,1)S(1)}, u32[]{:S(2)}, u32[]{:S(2)}) %collective-permute-start.4) | collective-permute-done | bytes 49184 | tf_op jit(solution)/shard_map/ppermute | solution.py:667
  18.1 1.6 %collective-permute-start.5 = (bf16[32,768]{1,0:T(8,128)(2,1)S(1)}, bf16[32,768]{1,0:T(8,128)(2,1)S(1)}, u32[]{:S(2)}, u32[]{:S(2)}) collective-permute-start(bf16[32,768]{1,0:T(8,128)(2,1)S(1)} %add_convert_fusion.2), channel_id=1, source_target_pairs={{0,2},{1,3},{2,0},{3,1},{4,6},{5,7},{6,4},{7,5},{8,10},{9,11},{10,... | collective-permute-start | bytes 147464 | tf_op jit(solution)/shard_map/ppermute | solution.py:667
  19.7 0.7 %collective-permute-start.6 = (bf16[32,768]{1,0:T(8,128)(2,1)S(1)}, bf16[32,768]{1,0:T(8,128)(2,1)S(1)}, u32[]{:S(2)}, u32[]{:S(2)}) collective-permute-start(bf16[32,768]{1,0:T(8,128)(2,1)S(1)} %add_convert_fusion.2), channel_id=1, source_target_pairs={{0,4},{1,5},{2,6},{3,7},{4,0},{5,1},{6,2},{7,3},{8,12},{9,13},{10,... | collective-permute-start | bytes 147464 | tf_op jit(solution)/shard_map/ppermute | solution.py:667
  20.4 1.3 %collective-permute-start.7 = (bf16[32,768]{1,0:T(8,128)(2,1)S(1)}, bf16[32,768]{1,0:T(8,128)(2,1)S(1)}, u32[]{:S(2)}, u32[]{:S(2)}) collective-permute-start(bf16[32,768]{1,0:T(8,128)(2,1)S(1)} %add_convert_fusion.2), channel_id=1, source_target_pairs={{0,6},{1,7},{2,4},{3,5},{4,2},{5,3},{6,0},{7,1},{8,14},{9,15},{10,... | collective-permute-start | bytes 147464 | tf_op jit(solution)/shard_map/ppermute | solution.py:667
  21.7 0.6 %collective-permute-done.5 = bf16[32,768]{1,0:T(8,128)(2,1)S(1)} collective-permute-done((bf16[32,768]{1,0:T(8,128)(2,1)S(1)}, bf16[32,768]{1,0:T(8,128)(2,1)S(1)}, u32[]{:S(2)}, u32[]{:S(2)}) %collective-permute-start.5) | collective-permute-done | bytes 49184 | tf_op jit(solution)/shard_map/ppermute | solution.py:667
  22.3 1.5 %collective-permute-done.6 = bf16[32,768]{1,0:T(8,128)(2,1)S(1)} collective-permute-done((bf16[32,768]{1,0:T(8,128)(2,1)S(1)}, bf16[32,768]{1,0:T(8,128)(2,1)S(1)}, u32[]{:S(2)}, u32[]{:S(2)}) %collective-permute-start.6) | collective-permute-done | bytes 49184 | tf_op jit(solution)/shard_map/ppermute | solution.py:667
  23.8 1.6 %collective-permute-done.7 = bf16[32,768]{1,0:T(8,128)(2,1)S(1)} collective-permute-done((bf16[32,768]{1,0:T(8,128)(2,1)S(1)}, bf16[32,768]{1,0:T(8,128)(2,1)S(1)}, u32[]{:S(2)}, u32[]{:S(2)}) %collective-permute-start.7) | collective-permute-done | bytes 49184 | tf_op jit(solution)/shard_map/ppermute | solution.py:667
  25.4 2.2 %collective-permute-start.8 = (bf16[32,768]{1,0:T(8,128)(2,1)S(1)}, bf16[32,768]{1,0:T(8,128)(2,1)S(1)}, u32[]{:S(2)}, u32[]{:S(2)}) collective-permute-start(bf16[32,768]{1,0:T(8,128)(2,1)S(1)} %add_convert_fusion.1), channel_id=1, source_target_pairs={{0,8},{1,9},{2,10},{3,11},{4,12},{5,13},{6,14},{7,15},{8,0},{9,1},... | collective-permute-start | bytes 147464 | tf_op jit(solution)/shard_map/ppermute | solution.py:667
  27.6 0.1 sine_multiply_fusion.refs_1_
  27.6 2.4 %advance.1 = (f32[2,16,256]{2,1,0:T(8,128)}, f32[2,16,256]{2,1,0:T(8,128)}) custom-call(f32[4,24,264]{2,1,0:T(8,128)S(1)} %pad_maximum_fusion.refs_0_, f32[1,384]{1,0:T(1,128)S(1)} %sine_multiply_fusion.refs_1_, bf16[96,256]{1,0:T(8,128)(2,1)S(1)} %get-tuple-element.78.refs_2_, f32[32,128]{1,0:T(8,128)S(1)} %get-tuple-element.79.refs_3_, ...), custom_call_target="tpu_custom_call" | custom-call | tf_op jit(solution)/shard_map/advance/pallas_call | solution.py:819
  30.0 0.5 %collective-permute-done.8 = bf16[32,768]{1,0:T(8,128)(2,1)S(1)} collective-permute-done((bf16[32,768]{1,0:T(8,128)(2,1)S(1)}, bf16[32,768]{1,0:T(8,128)(2,1)S(1)}, u32[]{:S(2)}, u32[]{:S(2)}) %collective-permute-start.8) | collective-permute-done | bytes 49184 | tf_op jit(solution)/shard_map/ppermute | solution.py:667
  30.5 0.1 collective-permute-start.9
  30.6 1.2 %collective-permute-done.9.refs_1_ = bf16[32,768]{1,0:T(8,128)(2,1)S(1)} collective-permute-done((bf16[32,768]{1,0:T(8,128)(2,1)S(1)}, bf16[32,768]{1,0:T(8,128)(2,1)S(1)}, u32[]{:S(2)}, u32[]{:S(2)}) %collective-permute-start.9) | collective-permute-done | bytes 49184 | tf_op jit(solution)/shard_map/ppermute | solution.py:667
  31.8 0.9 %finish.1 = (f32[9,2,64]{2,1,0:T(2,128)}, f32[1,64]{1,0:T(1,128)}, f32[9,64,64]{2,1,0:T(8,128)}, f32[1,64]{1,0:T(1,128)}, f32[12,3,3,64]{3,2,1,0:T(4,128)}, /*index=5*/f32[1,12]{1,0:T(1,128)}) custom-call(bf16[32,768]{1,0:T(8,128)(2,1)S(1)} %add_convert_fusion.refs_0_, bf16[32,768]{1,0:T(8,128)(2,1)S(1)} %collective-permute-done.9.refs_1_, ...), custom_call_target="tpu_custom_call" | custom-call | tf_op jit(solution)/shard_map/finish/pallas_call | solution.py:836
  (6 shorter events, 0.1 us)
Async XLA Ops:
  1.6 4.5 %collective-permute-start = (bf16[4,16,4]{2,1,0:T(8,128)(2,1)S(1)}, bf16[4,16,4]{2,1,0:T(8,128)(2,1)S(1)}, u32[]{:S(2)}, u32[]{:S(2)}) collective-permute-start(bf16[4,16,4]{2,1,0:T(8,128)(2,1)S(1)} %get-tuple-element.53), channel_id=1, source_target_pairs={{0,3},{1,2},{2,1},{3,0},{4,7},{5,6},{6,5},{7,4},{8,11},{9,10},{10,... | collective-permute-start | bytes 1544 | tf_op jit(solution)/shard_map/ppermute | solution.py:655
  4.0 2.1 %collective-permute-start.1 = (bf16[4,16,4]{2,1,0:T(8,128)(2,1)S(1)}, bf16[4,16,4]{2,1,0:T(8,128)(2,1)S(1)}, u32[]{:S(2)}, u32[]{:S(2)}) collective-permute-start(bf16[4,16,4]{2,1,0:T(8,128)(2,1)S(1)} %get-tuple-element.54), channel_id=1, source_target_pairs={{0,1},{1,0},{2,3},{3,2},{4,5},{5,4},{6,7},{7,6},{8,9},{9,8},{10,11... | collective-permute-start | bytes 1544 | tf_op jit(solution)/shard_map/ppermute | solution.py:656
  6.2 7.7 %collective-permute-start.3 = (bf16[4,4,264]{2,1,0:T(4,128)(2,1)S(1)}, bf16[4,4,264]{2,1,0:T(4,128)(2,1)S(1)}, u32[]{:S(2)}, u32[]{:S(2)}) collective-permute-start(bf16[4,4,264]{2,1,0:T(4,128)(2,1)S(1)} %get-tuple-element.62), channel_id=1, source_target_pairs={{0,4},{4,0},{8,12},{12,8},{1,5},{5,1},{9,13},{13,9},{2,6},{6,2},{1... | collective-permute-start | bytes 25352 | tf_op jit(solution)/shard_map/ppermute | solution.py:656
  8.2 5.7 %collective-permute-start.2 = (bf16[4,4,264]{2,1,0:T(4,128)(2,1)S(1)}, bf16[4,4,264]{2,1,0:T(4,128)(2,1)S(1)}, u32[]{:S(2)}, u32[]{:S(2)}) collective-permute-start(bf16[4,4,264]{2,1,0:T(4,128)(2,1)S(1)} %get-tuple-element.100), channel_id=1, source_target_pairs={{0,12},{4,8},{8,4},{12,0},{1,13},{5,9},{9,5},{13,1},{2,14},{6,10},... | collective-permute-start | bytes 25352 | tf_op jit(solution)/shard_map/ppermute | solution.py:655
  16.8 1.3 %collective-permute-start.4 = (bf16[32,768]{1,0:T(8,128)(2,1)S(1)}, bf16[32,768]{1,0:T(8,128)(2,1)S(1)}, u32[]{:S(2)}, u32[]{:S(2)}) collective-permute-start(bf16[32,768]{1,0:T(8,128)(2,1)S(1)} %get-tuple-element.77), channel_id=1, source_target_pairs={{0,1},{1,0},{2,3},{3,2},{4,5},{5,4},{6,7},{7,6},{8,9},{9,8},{10,11... | collective-permute-start | bytes 147464 | tf_op jit(solution)/shard_map/ppermute | solution.py:667
  18.1 4.2 %collective-permute-start.5 = (bf16[32,768]{1,0:T(8,128)(2,1)S(1)}, bf16[32,768]{1,0:T(8,128)(2,1)S(1)}, u32[]{:S(2)}, u32[]{:S(2)}) collective-permute-start(bf16[32,768]{1,0:T(8,128)(2,1)S(1)} %add_convert_fusion.2), channel_id=1, source_target_pairs={{0,2},{1,3},{2,0},{3,1},{4,6},{5,7},{6,4},{7,5},{8,10},{9,11},{10,... | collective-permute-start | bytes 147464 | tf_op jit(solution)/shard_map/ppermute | solution.py:667
  19.7 4.1 %collective-permute-start.6 = (bf16[32,768]{1,0:T(8,128)(2,1)S(1)}, bf16[32,768]{1,0:T(8,128)(2,1)S(1)}, u32[]{:S(2)}, u32[]{:S(2)}) collective-permute-start(bf16[32,768]{1,0:T(8,128)(2,1)S(1)} %add_convert_fusion.2), channel_id=1, source_target_pairs={{0,4},{1,5},{2,6},{3,7},{4,0},{5,1},{6,2},{7,3},{8,12},{9,13},{10,... | collective-permute-start | bytes 147464 | tf_op jit(solution)/shard_map/ppermute | solution.py:667
  20.4 5.0 %collective-permute-start.7 = (bf16[32,768]{1,0:T(8,128)(2,1)S(1)}, bf16[32,768]{1,0:T(8,128)(2,1)S(1)}, u32[]{:S(2)}, u32[]{:S(2)}) collective-permute-start(bf16[32,768]{1,0:T(8,128)(2,1)S(1)} %add_convert_fusion.2), channel_id=1, source_target_pairs={{0,6},{1,7},{2,4},{3,5},{4,2},{5,3},{6,0},{7,1},{8,14},{9,15},{10,... | collective-permute-start | bytes 147464 | tf_op jit(solution)/shard_map/ppermute | solution.py:667
  25.4 5.1 %collective-permute-start.8 = (bf16[32,768]{1,0:T(8,128)(2,1)S(1)}, bf16[32,768]{1,0:T(8,128)(2,1)S(1)}, u32[]{:S(2)}, u32[]{:S(2)}) collective-permute-start(bf16[32,768]{1,0:T(8,128)(2,1)S(1)} %add_convert_fusion.1), channel_id=1, source_target_pairs={{0,8},{1,9},{2,10},{3,11},{4,12},{5,13},{6,14},{7,15},{8,0},{9,1},... | collective-permute-start | bytes 147464 | tf_op jit(solution)/shard_map/ppermute | solution.py:667
  30.5 1.3 %collective-permute-start.9 = (bf16[32,768]{1,0:T(8,128)(2,1)S(1)}, bf16[32,768]{1,0:T(8,128)(2,1)S(1)}, u32[]{:S(2)}, u32[]{:S(2)}) collective-permute-start(bf16[32,768]{1,0:T(8,128)(2,1)S(1)} %add_convert_fusion.refs_0_), channel_id=1, source_target_pairs={{0,1},{1,0},{2,3},{3,2},{4,5},{5,4},{6,7},{7,6},{8,9},{9,8},{10,11... | collective-permute-start | bytes 147464 | tf_op jit(solution)/shard_map/ppermute | solution.py:667

commit v6 on v5

--- a/solution.py
+++ b/solution.py
@@ -283,7 +283,7 @@
         if halo <= r < halo + rows:
             bias_acc[0] += grad
             held.append((grad.astype(bf16), window, fed, act_short))
-        if held and (len(held) == 2 or r == groups_two[-1]):
+        if held and (len(held) == 3 or r == groups_two[-1]):
             grads, windows, feds, acts = zip(*held)
             held = []
             grads = jnp.concatenate(grads, axis=1)
@@ -300,8 +300,9 @@
             bias_acc[1, :hid, :] += grad[:hid, :]
         else:
             bias_acc[1] += grad
-    for r in groups_in:
-        acc_small[1] += mm_nt(state_in.window(r - 1, r + 3, (0,)), grad_one.get(r, r + 2))
+    fed = jnp.concatenate([state_in.window(r - 1, r + 3, (0,)) for r in groups_in], axis=1)
+    grads = jnp.concatenate([grad_one.get(r, r + 2) for r in groups_in], axis=1)
+    acc_small[1] += mm_nt(fed, grads)
 
 
 def inner_kernel(rows, cols, ext_ref, *refs):

time: 32.9 us -> 32.3 us (0.982)
  Pallas kernels: 11.5 us -> 11 us
    ppermute x6, waiting for transfers between devices: 6.58 us -> 6.16 us  [swap(): return lax.ppermute(value, ('gx', 'gy'), pairs)]
    pallas_call x1, Pallas kernels: 3.24 us -> 2.89 us  [per_device(): pl.pallas_call(lambda *refs: inner_kernel(rows, cols, *refs), out_shape=(...]
    ppermute x6, starting transfers between devices: 5.86 us -> 6.21 us  [swap(): return lax.ppermute(value, ('gx', 'gy'), pairs)]
  transfers between devices with their start and end apart: 10 -> 10, of which waited for: 6 -> 7; matrix products, arithmetic and copies ran while one was open for 0% -> 0% of each run, Pallas kernels for 21% -> 21%
where the time goes in v6:
time: 32.3 us; the launch traced here: 32.1 us
  starting transfers between devices  13.7 us (42%)
  Pallas kernels  11 us (34%)
  waiting for transfers between devices  6.27 us (19%)
  between operations  0.77 us (2%)
  other arithmetic  0.38 us (1%)
    ppermute x6, starting transfers between devices, swap(): return lax.ppermute(value, ('gx', 'gy'), pairs)  6.21 us
    ppermute x6, waiting for transfers between devices, swap(): return lax.ppermute(value, ('gx', 'gy'), pairs)  6.16 us
    ppermute x2, starting transfers between devices, widened(): far = lax.ppermute(far, axis, far_pairs)  4.92 us
    pallas_call x1, Pallas kernels, per_device(): pl.pallas_call(lambda *refs: inner_kernel(rows, cols, *refs), out_shape=(...  2.89 us
    ppermute x2, starting transfers between devices, widened(): near = lax.ppermute(near, axis, [(i, i ^ 1) for i in range(count)])  2.62 us
    pallas_call x1, Pallas kernels, per_device(): pl.pallas_call(lambda *refs: outer_kernel(rows, cols, *refs), out_shape=(...  2.52 us
    pallas_call x1, Pallas kernels, per_device(): pl.pallas_call(lambda *refs: advance_kernel(rows, cols, *refs), out_shape...  2.37 us
    pallas_call x1, Pallas kernels, per_device(): pl.pallas_call(weights_kernel, out_shape=(jax.ShapeDtypeStruct((2 * hid,...  1.35 us
  transfers between devices with their start and end apart: 10, of which 7 were waited for; matrix products, arithmetic and copies ran while one was open for 0% of the time, Pallas kernels for 21%

profile of v6, /device:TPU:0, one launch (start us, length us, event | category | flops | bytes accessed | tf_op | source)
XLA Modules:
  0.0 32.1 jit_solution(2401855007423170969)
XLA Ops:
  0.6 0.9 %pack.1 = (f32[4,16,256]{2,1,0:T(8,128)S(1)}, bf16[4,16,4]{2,1,0:T(8,128)(2,1)S(1)}, bf16[4,16,4]{2,1,0:T(8,128)(2,1)S(1)}) custom-call(s32[1]{0:T(128)} %bitcast.even_ref, f32[2,16,256]{2,1,0:T(8,128)} %velocity_ref.1, f32[2,16,256]{2,1,0:T(8,128)} %cotangent_ref.1), custom_call_target="tpu_custom_call" | custom-call | tf_op jit(solution)/shard_map/pack/pallas_call | solution.py:751
  1.6 2.4 %collective-permute-start = (bf16[4,16,4]{2,1,0:T(8,128)(2,1)S(1)}, bf16[4,16,4]{2,1,0:T(8,128)(2,1)S(1)}, u32[]{:S(2)}, u32[]{:S(2)}) collective-permute-start(bf16[4,16,4]{2,1,0:T(8,128)(2,1)S(1)} %get-tuple-element.53), channel_id=1, source_target_pairs={{0,3},{1,2},{2,1},{3,0},{4,7},{5,6},{6,5},{7,4},{8,11},{9,10},{10,... | collective-permute-start | bytes 1544 | tf_op jit(solution)/shard_map/ppermute | solution.py:656
  4.0 0.7 %collective-permute-start.1 = (bf16[4,16,4]{2,1,0:T(8,128)(2,1)S(1)}, bf16[4,16,4]{2,1,0:T(8,128)(2,1)S(1)}, u32[]{:S(2)}, u32[]{:S(2)}) collective-permute-start(bf16[4,16,4]{2,1,0:T(8,128)(2,1)S(1)} %get-tuple-element.54), channel_id=1, source_target_pairs={{0,1},{1,0},{2,3},{3,2},{4,5},{5,4},{6,7},{7,6},{8,9},{9,8},{10,11... | collective-permute-start | bytes 1544 | tf_op jit(solution)/shard_map/ppermute | solution.py:657
  4.7 1.4 %weights.1 = (bf16[128,192]{1,0:T(8,128)(2,1)S(1)}, bf16[3,128,256]{2,1,0:T(8,128)(2,1)S(1)}, bf16[3,128,256]{2,1,0:T(8,128)(2,1)S(1)}, bf16[128,192]{1,0:T(8,12...) custom-call(bf16[9,2,64]{2,1,0:T(2,128)(2,1)} %bitcast.24, ...), custom_call_target="tpu_custom_call" | custom-call | tf_op jit(solution)/shard_map/weights/pallas_call | solution.py:713
  6.1 0.0 collective-permute-done
  6.1 0.0 collective-permute-done.1
  6.1 0.1 fusion
  6.2 1.9 %collective-permute-start.3 = (bf16[4,4,264]{2,1,0:T(4,128)(2,1)S(1)}, bf16[4,4,264]{2,1,0:T(4,128)(2,1)S(1)}, u32[]{:S(2)}, u32[]{:S(2)}) collective-permute-start(bf16[4,4,264]{2,1,0:T(4,128)(2,1)S(1)} %get-tuple-element.62), channel_id=1, source_target_pairs={{0,4},{4,0},{8,12},{12,8},{1,5},{5,1},{9,13},{13,9},{2,6},{6,2},{1... | collective-permute-start | bytes 25352 | tf_op jit(solution)/shard_map/ppermute | solution.py:657
  8.2 2.5 %collective-permute-start.2 = (bf16[4,4,264]{2,1,0:T(4,128)(2,1)S(1)}, bf16[4,4,264]{2,1,0:T(4,128)(2,1)S(1)}, u32[]{:S(2)}, u32[]{:S(2)}) collective-permute-start(bf16[4,4,264]{2,1,0:T(4,128)(2,1)S(1)} %get-tuple-element.100), channel_id=1, source_target_pairs={{0,12},{4,8},{8,4},{12,0},{1,13},{5,9},{9,5},{13,1},{2,14},{6,10},... | collective-permute-start | bytes 25352 | tf_op jit(solution)/shard_map/ppermute | solution.py:656
  10.7 2.9 %inner.1 = (bf16[3,896,256]{2,1,0:T(8,128)(2,1)S(1)}, f32[896,256]{1,0:T(8,128)S(1)}, bf16[3,768,256]{2,1,0:T(8,128)(2,1)S(1)}, bf16[768,256]{1,0:T(8,128)(2,1)S...) custom-call(f32[4,16,264]{2,1,0:T(8,128)S(1)} %get-tuple-element.99., ...), custom_call_target="tpu_custom_call" | custom-call | tf_op jit(solution)/shard_map/inner/pallas_call | solution.py:772
  13.6 0.0 collective-permute-done.3
  13.6 0.1 collective-permute-done.2
  13.7 0.1 pad_maximum_fusion.refs_0_
  13.8 2.5 %outer.1 = (bf16[32,768]{1,0:T(8,128)(2,1)S(1)}, bf16[32,768]{1,0:T(8,128)(2,1)S(1)}, bf16[2,256,256]{2,1,0:T(8,128)(2,1)S(1)}, bf16[2,256,256]{2,1,0:T(8,128)(2...) custom-call(f32[4,24,264]{2,1,0:T(8,128)S(1)} %pad_maximum_fusion.refs_0_, ...), custom_call_target="tpu_custom_call" | custom-call | tf_op jit(solution)/shard_map/outer/pallas_call | solution.py:793
  16.4 0.1 collective-permute-start.4
  16.4 1.2 %collective-permute-done.4 = bf16[32,768]{1,0:T(8,128)(2,1)S(1)} collective-permute-done((bf16[32,768]{1,0:T(8,128)(2,1)S(1)}, bf16[32,768]{1,0:T(8,128)(2,1)S(1)}, u32[]{:S(2)}, u32[]{:S(2)}) %collective-permute-start.4) | collective-permute-done | bytes 49184 | tf_op jit(solution)/shard_map/ppermute | solution.py:668
  17.7 1.6 %collective-permute-start.5 = (bf16[32,768]{1,0:T(8,128)(2,1)S(1)}, bf16[32,768]{1,0:T(8,128)(2,1)S(1)}, u32[]{:S(2)}, u32[]{:S(2)}) collective-permute-start(bf16[32,768]{1,0:T(8,128)(2,1)S(1)} %add_convert_fusion.2), channel_id=1, source_target_pairs={{0,2},{1,3},{2,0},{3,1},{4,6},{5,7},{6,4},{7,5},{8,10},{9,11},{10,... | collective-permute-start | bytes 147464 | tf_op jit(solution)/shard_map/ppermute | solution.py:668
  19.3 0.6 %collective-permute-start.6 = (bf16[32,768]{1,0:T(8,128)(2,1)S(1)}, bf16[32,768]{1,0:T(8,128)(2,1)S(1)}, u32[]{:S(2)}, u32[]{:S(2)}) collective-permute-start(bf16[32,768]{1,0:T(8,128)(2,1)S(1)} %add_convert_fusion.2), channel_id=1, source_target_pairs={{0,4},{1,5},{2,6},{3,7},{4,0},{5,1},{6,2},{7,3},{8,12},{9,13},{10,... | collective-permute-start | bytes 147464 | tf_op jit(solution)/shard_map/ppermute | solution.py:668
  19.9 1.4 %collective-permute-start.7 = (bf16[32,768]{1,0:T(8,128)(2,1)S(1)}, bf16[32,768]{1,0:T(8,128)(2,1)S(1)}, u32[]{:S(2)}, u32[]{:S(2)}) collective-permute-start(bf16[32,768]{1,0:T(8,128)(2,1)S(1)} %add_convert_fusion.2), channel_id=1, source_target_pairs={{0,6},{1,7},{2,4},{3,5},{4,2},{5,3},{6,0},{7,1},{8,14},{9,15},{10,... | collective-permute-start | bytes 147464 | tf_op jit(solution)/shard_map/ppermute | solution.py:668
  21.2 0.6 %collective-permute-done.5 = bf16[32,768]{1,0:T(8,128)(2,1)S(1)} collective-permute-done((bf16[32,768]{1,0:T(8,128)(2,1)S(1)}, bf16[32,768]{1,0:T(8,128)(2,1)S(1)}, u32[]{:S(2)}, u32[]{:S(2)}) %collective-permute-start.5) | collective-permute-done | bytes 49184 | tf_op jit(solution)/shard_map/ppermute | solution.py:668
  21.8 1.5 %collective-permute-done.6 = bf16[32,768]{1,0:T(8,128)(2,1)S(1)} collective-permute-done((bf16[32,768]{1,0:T(8,128)(2,1)S(1)}, bf16[32,768]{1,0:T(8,128)(2,1)S(1)}, u32[]{:S(2)}, u32[]{:S(2)}) %collective-permute-start.6) | collective-permute-done | bytes 49184 | tf_op jit(solution)/shard_map/ppermute | solution.py:668
  23.4 1.5 %collective-permute-done.7 = bf16[32,768]{1,0:T(8,128)(2,1)S(1)} collective-permute-done((bf16[32,768]{1,0:T(8,128)(2,1)S(1)}, bf16[32,768]{1,0:T(8,128)(2,1)S(1)}, u32[]{:S(2)}, u32[]{:S(2)}) %collective-permute-start.7) | collective-permute-done | bytes 49184 | tf_op jit(solution)/shard_map/ppermute | solution.py:668
  24.9 2.5 %collective-permute-start.8 = (bf16[32,768]{1,0:T(8,128)(2,1)S(1)}, bf16[32,768]{1,0:T(8,128)(2,1)S(1)}, u32[]{:S(2)}, u32[]{:S(2)}) collective-permute-start(bf16[32,768]{1,0:T(8,128)(2,1)S(1)} %add_convert_fusion.1), channel_id=1, source_target_pairs={{0,8},{1,9},{2,10},{3,11},{4,12},{5,13},{6,14},{7,15},{8,0},{9,1},... | collective-permute-start | bytes 147464 | tf_op jit(solution)/shard_map/ppermute | solution.py:668
  27.4 0.1 sine_multiply_fusion.refs_1_
  27.5 2.4 %advance.1 = (f32[2,16,256]{2,1,0:T(8,128)}, f32[2,16,256]{2,1,0:T(8,128)}) custom-call(f32[4,24,264]{2,1,0:T(8,128)S(1)} %pad_maximum_fusion.refs_0_, f32[1,384]{1,0:T(1,128)S(1)} %sine_multiply_fusion.refs_1_, bf16[96,256]{1,0:T(8,128)(2,1)S(1)} %get-tuple-element.78.refs_2_, f32[32,128]{1,0:T(8,128)S(1)} %get-tuple-element.79.refs_3_, ...), custom_call_target="tpu_custom_call" | custom-call | tf_op jit(solution)/shard_map/advance/pallas_call | solution.py:820
  29.8 0.1 collective-permute-done.8
  29.9 0.1 collective-permute-start.9
  30.0 1.2 %collective-permute-done.9.refs_1_ = bf16[32,768]{1,0:T(8,128)(2,1)S(1)} collective-permute-done((bf16[32,768]{1,0:T(8,128)(2,1)S(1)}, bf16[32,768]{1,0:T(8,128)(2,1)S(1)}, u32[]{:S(2)}, u32[]{:S(2)}) %collective-permute-start.9) | collective-permute-done | bytes 49184 | tf_op jit(solution)/shard_map/ppermute | solution.py:668
  31.2 0.9 %finish.1 = (f32[9,2,64]{2,1,0:T(2,128)}, f32[1,64]{1,0:T(1,128)}, f32[9,64,64]{2,1,0:T(8,128)}, f32[1,64]{1,0:T(1,128)}, f32[12,3,3,64]{3,2,1,0:T(4,128)}, /*index=5*/f32[1,12]{1,0:T(1,128)}) custom-call(bf16[32,768]{1,0:T(8,128)(2,1)S(1)} %add_convert_fusion.refs_0_, bf16[32,768]{1,0:T(8,128)(2,1)S(1)} %collective-permute-done.9.refs_1_, ...), custom_call_target="tpu_custom_call" | custom-call | tf_op jit(solution)/shard_map/finish/pallas_call | solution.py:837
  (6 shorter events, 0.1 us)
Async XLA Ops:
  1.6 4.5 %collective-permute-start = (bf16[4,16,4]{2,1,0:T(8,128)(2,1)S(1)}, bf16[4,16,4]{2,1,0:T(8,128)(2,1)S(1)}, u32[]{:S(2)}, u32[]{:S(2)}) collective-permute-start(bf16[4,16,4]{2,1,0:T(8,128)(2,1)S(1)} %get-tuple-element.53), channel_id=1, source_target_pairs={{0,3},{1,2},{2,1},{3,0},{4,7},{5,6},{6,5},{7,4},{8,11},{9,10},{10,... | collective-permute-start | bytes 1544 | tf_op jit(solution)/shard_map/ppermute | solution.py:656
  4.0 2.1 %collective-permute-start.1 = (bf16[4,16,4]{2,1,0:T(8,128)(2,1)S(1)}, bf16[4,16,4]{2,1,0:T(8,128)(2,1)S(1)}, u32[]{:S(2)}, u32[]{:S(2)}) collective-permute-start(bf16[4,16,4]{2,1,0:T(8,128)(2,1)S(1)} %get-tuple-element.54), channel_id=1, source_target_pairs={{0,1},{1,0},{2,3},{3,2},{4,5},{5,4},{6,7},{7,6},{8,9},{9,8},{10,11... | collective-permute-start | bytes 1544 | tf_op jit(solution)/shard_map/ppermute | solution.py:657
  6.2 7.3 %collective-permute-start.3 = (bf16[4,4,264]{2,1,0:T(4,128)(2,1)S(1)}, bf16[4,4,264]{2,1,0:T(4,128)(2,1)S(1)}, u32[]{:S(2)}, u32[]{:S(2)}) collective-permute-start(bf16[4,4,264]{2,1,0:T(4,128)(2,1)S(1)} %get-tuple-element.62), channel_id=1, source_target_pairs={{0,4},{4,0},{8,12},{12,8},{1,5},{5,1},{9,13},{13,9},{2,6},{6,2},{1... | collective-permute-start | bytes 25352 | tf_op jit(solution)/shard_map/ppermute | solution.py:657
  8.2 5.5 %collective-permute-start.2 = (bf16[4,4,264]{2,1,0:T(4,128)(2,1)S(1)}, bf16[4,4,264]{2,1,0:T(4,128)(2,1)S(1)}, u32[]{:S(2)}, u32[]{:S(2)}) collective-permute-start(bf16[4,4,264]{2,1,0:T(4,128)(2,1)S(1)} %get-tuple-element.100), channel_id=1, source_target_pairs={{0,12},{4,8},{8,4},{12,0},{1,13},{5,9},{9,5},{13,1},{2,14},{6,10},... | collective-permute-start | bytes 25352 | tf_op jit(solution)/shard_map/ppermute | solution.py:656
  16.4 1.3 %collective-permute-start.4 = (bf16[32,768]{1,0:T(8,128)(2,1)S(1)}, bf16[32,768]{1,0:T(8,128)(2,1)S(1)}, u32[]{:S(2)}, u32[]{:S(2)}) collective-permute-start(bf16[32,768]{1,0:T(8,128)(2,1)S(1)} %get-tuple-element.77), channel_id=1, source_target_pairs={{0,1},{1,0},{2,3},{3,2},{4,5},{5,4},{6,7},{7,6},{8,9},{9,8},{10,11... | collective-permute-start | bytes 147464 | tf_op jit(solution)/shard_map/ppermute | solution.py:668
  17.7 4.2 %collective-permute-start.5 = (bf16[32,768]{1,0:T(8,128)(2,1)S(1)}, bf16[32,768]{1,0:T(8,128)(2,1)S(1)}, u32[]{:S(2)}, u32[]{:S(2)}) collective-permute-start(bf16[32,768]{1,0:T(8,128)(2,1)S(1)} %add_convert_fusion.2), channel_id=1, source_target_pairs={{0,2},{1,3},{2,0},{3,1},{4,6},{5,7},{6,4},{7,5},{8,10},{9,11},{10,... | collective-permute-start | bytes 147464 | tf_op jit(solution)/shard_map/ppermute | solution.py:668
  19.3 4.1 %collective-permute-start.6 = (bf16[32,768]{1,0:T(8,128)(2,1)S(1)}, bf16[32,768]{1,0:T(8,128)(2,1)S(1)}, u32[]{:S(2)}, u32[]{:S(2)}) collective-permute-start(bf16[32,768]{1,0:T(8,128)(2,1)S(1)} %add_convert_fusion.2), channel_id=1, source_target_pairs={{0,4},{1,5},{2,6},{3,7},{4,0},{5,1},{6,2},{7,3},{8,12},{9,13},{10,... | collective-permute-start | bytes 147464 | tf_op jit(solution)/shard_map/ppermute | solution.py:668
  19.9 5.0 %collective-permute-start.7 = (bf16[32,768]{1,0:T(8,128)(2,1)S(1)}, bf16[32,768]{1,0:T(8,128)(2,1)S(1)}, u32[]{:S(2)}, u32[]{:S(2)}) collective-permute-start(bf16[32,768]{1,0:T(8,128)(2,1)S(1)} %add_convert_fusion.2), channel_id=1, source_target_pairs={{0,6},{1,7},{2,4},{3,5},{4,2},{5,3},{6,0},{7,1},{8,14},{9,15},{10,... | collective-permute-start | bytes 147464 | tf_op jit(solution)/shard_map/ppermute | solution.py:668
  24.9 5.1 %collective-permute-start.8 = (bf16[32,768]{1,0:T(8,128)(2,1)S(1)}, bf16[32,768]{1,0:T(8,128)(2,1)S(1)}, u32[]{:S(2)}, u32[]{:S(2)}) collective-permute-start(bf16[32,768]{1,0:T(8,128)(2,1)S(1)} %add_convert_fusion.1), channel_id=1, source_target_pairs={{0,8},{1,9},{2,10},{3,11},{4,12},{5,13},{6,14},{7,15},{8,0},{9,1},... | collective-permute-start | bytes 147464 | tf_op jit(solution)/shard_map/ppermute | solution.py:668
  29.9 1.3 %collective-permute-start.9 = (bf16[32,768]{1,0:T(8,128)(2,1)S(1)}, bf16[32,768]{1,0:T(8,128)(2,1)S(1)}, u32[]{:S(2)}, u32[]{:S(2)}) collective-permute-start(bf16[32,768]{1,0:T(8,128)(2,1)S(1)} %add_convert_fusion.refs_0_), channel_id=1, source_target_pairs={{0,1},{1,0},{2,3},{3,2},{4,5},{5,4},{6,7},{7,6},{8,9},{9,8},{10,11... | collective-permute-start | bytes 147464 | tf_op jit(solution)/shard_map/ppermute | solution.py:668

commit v7 on v6

--- a/solution.py
+++ b/solution.py
@@ -108,10 +108,10 @@
                 rows = slice((lo - start) * self.size, (lo - start) * self.size + value.shape[0])
                 ref[(*lead, rows, slice(None))] = value
 
-    def put_shifted(self, lo, value, strip, first):
+    def put_shifted(self, lo, value, strip, place):
         value = value.astype(bf16)
         ends = [
-            jnp.concatenate([strip_column(strip, lo + k - first, at, to) for k in range(2)], axis=0)
+            jnp.concatenate([strip_column(strip, place(lo + k), at, to) for k in range(2)], axis=0)
             for at, to in ((left_of, 0), (right_of, value.shape[1] - 1))
         ]
         for b, shifted in enumerate(beside(value, value, value, *ends)):
@@ -169,18 +169,23 @@
     return jnp.sum(part.T, axis=0, keepdims=True)
 
 
-def prepare(first, rows, cols, ext_ref, stage, planes, state_in, state_rows, head_rows):
-    count = ext_ref.shape[1]
+def fill(stage, parts):
+    stage[...] = jnp.zeros(stage.shape, f32)
+    for at, part in parts:
+        stage[:, at : at + part.shape[1], 0 : part.shape[2]] = part.astype(f32)
+
+
+def prepare(place, cols, parts, stage, planes, state_in, state_rows, head_rows, sum_rows):
     height, width = stage.shape[1], stage.shape[2]
-    stage[...] = jnp.zeros(stage.shape, f32)
-    stage[:, 0:count, 0 : cols + 2 * halo] = ext_ref[...]
+    count = height
+    fill(stage, parts)
     w0, w1, c0, c1 = stage[0], stage[1], stage[2], stage[3]
 
     planes[...] = jnp.zeros(planes.shape, f32)
     put_plane(planes, 0, slot, w0)
     put_plane(planes, 1, slot, w1)
     for r in state_rows:
-        state_in.put_cut(r, take_rows(planes, (r - first) * slot, 2 * slot), (0,))
+        state_in.put_cut(r, take_rows(planes, place(r) * slot, 2 * slot), (0,))
     strips = [strip_of(planes, count, cols)]
 
     normal_x, normal_y = faces(w0, w1)
@@ -190,8 +195,12 @@
     fy0 = -advection * (c0 - shift(c0, 0, 1)) * normal_y
     fy1 = -advection * (c1 - shift(c1, 0, 1)) * normal_y
     lane = lax.broadcasted_iota(jnp.int32, (height, width), 1)
-    row_id = lax.broadcasted_iota(jnp.int32, (height, width), 0) + first
-    own = (lane >= halo) & (lane < halo + cols) & (row_id >= halo) & (row_id < halo + rows)
+    row_id = lax.broadcasted_iota(jnp.int32, (height, width), 0)
+    own = (lane >= halo) & (lane < halo + cols)
+    inside = row_id < 0
+    for lo, hi in sum_rows:
+        inside = inside | ((row_id >= place(lo)) & (row_id <= place(hi - 1)))
+    own = own & inside
     sums = []
     for at, taps, g0, g1 in ((0, taps_x, fx0, fx1), (6, taps_y, fy0, fy1)):
         raw = [g0 * t0[tap] + g1 * t1[tap] for tap in taps]
@@ -201,8 +210,9 @@
             put_plane(planes, at + k, slot, value)
             sums.append(jnp.sum(jnp.where(own, value, 0.0), axis=0, keepdims=True))
     for r in head_rows:
-        state_in.put_cut(r, take_rows(planes, (r - first) * slot, 2 * slot), (1,))
+        state_in.put_cut(r, take_rows(planes, place(r) * slot, 2 * slot), (1,))
     strips.append(strip_of(planes, count, cols))
+    sums = jnp.concatenate(sums + [jnp.zeros((slot - coef, width), f32)], axis=0)
     return sums, strips
 
 
@@ -233,13 +243,17 @@
         self.act_two = act.astype(bf16)
         self.grad_two = grad.astype(bf16)
 
+    def put(self, refs):
+        for ref, value in zip(refs, (self.act_two, self.grad_two, self.slope), strict=True):
+            ref[...] = value
+
 
 def layers(
     rows,
     groups,
     refs,
     strips,
-    first,
+    place,
     state_in,
     act_one,
     slope_one,
@@ -260,7 +274,7 @@
         linear = mm(w_in, state_in.window(r - 1, r + 3, (0,))) + b_in
         sigma = sigma_of(linear)
         act = linear * sigma
-        act_one.put_shifted(r, act, strips.act_one, first)
+        act_one.put_shifted(r, act, strips.act_one, place)
         slope_one.put(r, sigma + act * (1.0 - sigma))
         if r == groups_one[0]:
             strips.second()
@@ -279,7 +293,7 @@
         act_two.put(r, act_short)
         fed = state_in.window(r - 1, r + 3, (1,))
         grad = mm(w_out_t, fed) * (sigma + act * (1.0 - sigma))
-        grad_two.put_shifted(r, grad, strips.grad_two, first)
+        grad_two.put_shifted(r, grad, strips.grad_two, place)
         if halo <= r < halo + rows:
             bias_acc[0] += grad
             held.append((grad.astype(bf16), window, fed, act_short))
@@ -305,24 +319,34 @@
     acc_small[1] += mm_nt(fed, grads)
 
 
-def inner_kernel(rows, cols, ext_ref, *refs):
+def inner_kernel(rows, cols, wide_ref, *refs):
     weight_refs, refs = refs[:6], refs[6:]
-    act_one, slope_one, grad_two, act_two, grad_one, acc_mid, acc_small, bias_acc, *refs = refs
-    stage, planes, state_in = refs
+    act_one, slope_one, grad_two, act_two, grad_one, *refs = refs
+    acc_mid, acc_small, bias_acc, state_ref, sums_ref, *strip_refs, stage, planes = refs
     low, high = halo, halo + rows
-    state_in = Rows(slot, (low, high, state_in))
+    state_in = Rows(slot, (low, high, state_ref))
     acc_mid[...] = jnp.zeros(acc_mid.shape, f32)
     acc_small[...] = jnp.zeros(acc_small.shape, f32)
     bias_acc[...] = jnp.zeros(bias_acc.shape, f32)
     pairs = range(low, high, 2)
-    _, strips = prepare(low, rows, cols, ext_ref, stage, planes, state_in, pairs, pairs)
-    groups = [range(low + k, high - k, 2) for k in (1, 2, 3, 4)]
+    sums_ref[...], strips = prepare(
+        lambda r: r - low,
+        cols,
+        [(0, wide_ref[...])],
+        stage,
+        planes,
+        state_in,
+        pairs,
+        pairs,
+        [(low + 2, high - 2)],
+    )
+    strips = Strips(weight_refs, *strips)
     layers(
         rows,
-        groups,
+        [range(low + k, high - k, 2) for k in (1, 2, 3, 4)],
         weight_refs,
-        Strips(weight_refs, *strips),
-        low,
+        strips,
+        lambda r: r - low,
         state_in,
         Rows(hid, (low + 1, high - 1, act_one)),
         Rows(hid, (low + 1, high - 1, slope_one)),
@@ -333,42 +357,72 @@
         acc_small,
         bias_acc,
     )
-
-
-def split_rows(size, first, low, high, last, lower_ref, inner_ref, upper_ref):
-    return Rows(size, (first, low, lower_ref), (low, high, inner_ref), (high, last, upper_ref))
-
-
-def outer_kernel(rows, cols, ext_ref, *refs):
-    weight_refs, core_ref, refs = refs[:6], refs[6], refs[7:]
-    act_one_in, slope_one_in, grad_two_in, grad_one_in, acc_mid_in, acc_small_in, bias_in, *refs = refs
-    keep_ref, send_ref, act_two, grad_one, act_two_strip, grad_two_strip, slope_strip, *refs = refs
-    pay, stage, planes, state_in, act_one, slope_one, grad_two, acc_mid, acc_small, bias_acc = refs
+    strips.put(strip_refs)
+
+
+def sides(far_ref, near_ref, even_ref):
+    far, near = far_ref[...].astype(f32), near_ref[...].astype(f32)
+    even = even_ref[0] == 1
+    return jnp.where(even, far, near), jnp.where(even, near, far)
+
+
+def outer_kernel(rows, cols, wide_ref, far_ref, near_ref, even_ref, core_ref, *refs):
+    weight_refs, refs = refs[:6], refs[6:]
+    act_one_in, slope_one_in, grad_two_in, grad_one_in, state_inner, *refs = refs
+    acc_mid_in, acc_small_in, bias_in, sums_in, *refs = refs
+    keep_ref, send_ref, act_two, grad_one, *refs = refs
+    strip_refs, refs = refs[:3], refs[3:]
+    acc_mid, acc_small, bias_acc, pay, stage, planes, state_edge, act_one, slope_one, grad_two = refs
     low, high, deep = halo, halo + rows, rows + 2 * halo
     acc_mid[...] = acc_mid_in[...]
     acc_small[...] = acc_small_in[...]
     bias_acc[...] = bias_in[...]
-    state_in = Rows(slot, (0, deep, state_in))
-    state_rows = [r for r in range(0, deep, 2) if r < low + 6 or r + 2 > high - 6]
-    head_rows = [r for r in range(0, deep, 2) if r < low + 4 or r + 2 > high - 4]
-    sums, strips = prepare(0, rows, cols, ext_ref, stage, planes, state_in, state_rows, head_rows)
-    bias_out = jnp.concatenate(sums + [jnp.zeros((128 - coef, stage.shape[2]), f32)], axis=0)
-    groups = [
-        [*range(k, low + k, 2), *range(high - k, deep - k, 2)] for k in (1, 2, 3)
-    ]
-    groups.append([low, low + 2, high - 4, high - 2])
-
-    def both(k, edge, inner):
-        edges = [edge.at[i] for i in range(2)]
-        return split_rows(hid, k, low + k, high - k, deep - k, edges[0], inner, edges[1])
-
+    edge, used = 2 * halo, 2 * halo - 2
+
+    def place(r):
+        return r if r < edge else r - (deep - 2 * edge)
+
+    def both(k, edge_ref, inner_ref):
+        return split_rows(
+            hid, k, low + k, high - k, deep - k, edge_ref.at[0], inner_ref, edge_ref.at[1]
+        )
+
+    state_in = split_rows(
+        slot,
+        0,
+        used,
+        deep - used,
+        deep,
+        state_edge.at[:, :, 0 : used * slot, :],
+        state_inner.at[:, :, 2 * slot : (rows - 2) * slot, :],
+        state_edge.at[:, :, (2 * edge - used) * slot : 2 * edge * slot, :],
+    )
+    lower, upper = sides(far_ref, near_ref, even_ref)
+    pairs = [*range(0, used, 2), *range(deep - used, deep, 2)]
+    sums, strips = prepare(
+        place,
+        cols,
+        [
+            (0, lower),
+            (halo, wide_ref[:, 0:halo, :]),
+            (edge, wide_ref[:, rows - halo : rows, :]),
+            (edge + halo, upper),
+        ],
+        stage,
+        planes,
+        state_in,
+        pairs,
+        pairs,
+        [(low, low + 2), (high - 2, high)],
+    )
     strips = Strips(weight_refs, *strips)
     layers(
         rows,
-        groups,
+        [[*range(k, low + k, 2), *range(high - k, deep - k, 2)] for k in (1, 2, 3)]
+        + [[low, low + 2, high - 4, high - 2]],
         weight_refs,
         strips,
-        0,
+        place,
         state_in,
         both(1, act_one, act_one_in),
         both(1, slope_one, slope_one_in),
@@ -379,10 +433,9 @@
         acc_small,
         bias_acc,
     )
-
-    act_two_strip[...] = strips.act_two
-    grad_two_strip[...] = strips.grad_two
-    slope_strip[...] = strips.slope
+    strips.put(strip_refs)
+    sums = sums + sums_in[...]
+    bias_out = jnp.concatenate([sums, jnp.zeros((128 - slot, sums.shape[1]), f32)], axis=0)
 
     for b in range(3):
         total = acc_mid[b, :hid, : 3 * hid] + acc_mid[b, hid:, hid:]
@@ -420,35 +473,45 @@
     send_ref[...] = pay[1 - core]
 
 
+def split_rows(size, first, low, high, last, lower_ref, inner_ref, upper_ref):
+    return Rows(size, (first, low, lower_ref), (low, high, inner_ref), (high, last, upper_ref))
+
+
 def advance_kernel(
     rows,
     cols,
-    ext_ref,
+    wide_ref,
+    far_ref,
+    near_ref,
+    even_ref,
     forcing_ref,
     w_head_ref,
     b_head_ref,
     w_in_t_ref,
-    act_two_in,
-    act_two_edge,
-    grad_one_in,
-    grad_one_edge,
-    act_two_strip,
-    grad_two_strip,
-    slope_strip,
     w_mid_t_ref,
-    new_ref,
-    grad_ref,
-    stage,
-    head,
-    back,
+    *refs,
 ):
+    inner, outer, (new_ref, grad_ref, stage, head, back) = refs[0:5], refs[5:10], refs[10:]
+    act_two_in, grad_one_in = inner[:2]
+    act_two_edge, grad_one_edge = outer[:2]
+    edge = 2 * halo
+
+    def whole(k):
+        skip = 2 * pitch
+        parts = [
+            outer[k][:, : edge * pitch - skip],
+            inner[k][:, skip : rows * pitch - skip],
+            outer[k][:, edge * pitch + skip :],
+        ]
+        return jnp.concatenate(parts, axis=1)
+
     low, high, deep = halo, halo + rows, rows + 2 * halo
     act_two, grad_one = (
         split_rows(hid, k, low + k, high - k, deep - k, edge.at[0], inner, edge.at[1])
         for k, inner, edge in ((2, act_two_in, act_two_edge), (3, grad_one_in, grad_one_edge))
     )
-    stage[...] = jnp.zeros(stage.shape, f32)
-    stage[:, 0:deep, 0 : cols + 2 * halo] = ext_ref[...]
+    lower, upper = sides(far_ref, near_ref, even_ref)
+    fill(stage, [(0, lower), (halo, wide_ref[...]), (halo + rows, upper)])
     w0, w1, c0, c1 = stage[0], stage[1], stage[2], stage[3]
     head[...] = jnp.zeros(head.shape, f32)
     back[...] = jnp.zeros(back.shape, f32)
@@ -475,7 +538,7 @@
 
         return ends, pair
 
-    ends, pair = weighed(w_head_ref, slot, act_two_strip[...])
+    ends, pair = weighed(w_head_ref, slot, whole(2))
     head_strip = b_head[:slot] + ends[1] + shift(ends[0], 0, -1) + shift(ends[2], 0, 1)
     for r in range(3, deep - 3, 2):
         out = jnp.concatenate([pair(act_two, r) + b_head, blank], axis=1)
@@ -485,7 +548,7 @@
             out = with_lane(out, to, jnp.concatenate(column, axis=0))
         put_rows(head, r * slot, out)
     spread = jnp.concatenate([w_mid_t_ref[b, :hid, : 3 * hid] for b in range(3)], axis=1)
-    grad_one_strip = mm(spread, strip_taps(grad_two_strip[...])) * slope_strip[...]
+    grad_one_strip = mm(spread, strip_taps(whole(3))) * whole(4)
     _, pair = weighed(w_in_t_ref, 8, grad_one_strip.astype(bf16))
     for r in range(halo, halo + rows, 2):
         out = jnp.concatenate([pair(grad_one, r), blank[:16]], axis=1)
@@ -641,23 +704,16 @@
     c_head_ref[...] = jnp.broadcast_to(bias, (128, 128)).T[: 2 * slot]
 
 
-def edges(fields, axis, dim):
-    size = fields.shape[dim]
+def paired(axis, first, last):
     even = lax.axis_index(axis) % 2 == 0
-    first = lax.slice_in_dim(fields, 0, halo, axis=dim).astype(bf16)
-    last = lax.slice_in_dim(fields, size - halo, size, axis=dim).astype(bf16)
     return jnp.where(even, first, last), jnp.where(even, last, first)
 
 
-def widened(fields, far, near, axis, dim):
+def met(far, near, axis):
     count = lax.axis_size(axis)
-    even = lax.axis_index(axis) % 2 == 0
     far_pairs = [(i, (i + 1 if i % 2 else i - 1) % count) for i in range(count)]
-    far = lax.ppermute(far, axis, far_pairs)
-    near = lax.ppermute(near, axis, [(i, i ^ 1) for i in range(count)])
-    low = jnp.where(even, far, near).astype(f32)
-    high = jnp.where(even, near, far).astype(f32)
-    return jnp.concatenate([low, fields, high], axis=dim)
+    near_pairs = [(i, i ^ 1) for i in range(count)]
+    return lax.ppermute(far, axis, far_pairs), lax.ppermute(near, axis, near_pairs)
 
 
 def swap(value, rows, cols):
@@ -757,19 +813,32 @@
         compiler_params=params,
         name="pack",
     )(even, in_hbm(velocity), in_hbm(cotangent))
-    wide = widened(fields, far, near, "gy", 2)
+    far, near = met(far, near, "gy")
+    low, high = paired("gy", far, near)[0], paired("gy", near, far)[0]
+    wide = jnp.concatenate([low.astype(f32), fields, high.astype(f32)], axis=2)
+    first, last = (
+        jnp.concatenate([low[:, at], fields[:, at].astype(bf16), high[:, at]], axis=2)
+        for at in (slice(0, halo), slice(rows - halo, rows))
+    )
     maps = (w_in, w_mid, w_mid_t, w_out_t, b_in, b_mid)
-    far, near = edges(wide, "gx", 1)
+    far, near = paired("gx", first, last)
     near, maps = lax.optimization_barrier((near, maps))
-    ext = widened(wide, far, near, "gx", 1)
+    far, near = met(far, near, "gx")
+    row_even = (lax.axis_index("gx") % 2 == 0).astype(jnp.int32).reshape(1)
 
     accs = (
         jax.ShapeDtypeStruct((3, 2 * hid, 4 * hid), f32),
         jax.ShapeDtypeStruct((2, 12 * slot, 2 * hid), f32),
         jax.ShapeDtypeStruct((2, 2 * hid, cols), f32),
     )
-    strip = jax.ShapeDtypeStruct((hid, deep * pitch), bf16)
-    act_one, slope_one, grad_two, act_two_in, grad_one_in, *totals = pl.pallas_call(
+    edge = 2 * halo
+    state = jax.ShapeDtypeStruct((2, 3, rows * slot, cols), bf16)
+    sums = jax.ShapeDtypeStruct((slot, width), f32)
+
+    def strips(count):
+        return [jax.ShapeDtypeStruct((hid, count * pitch), kind) for kind in (bf16, bf16, f32)]
+
+    act_one, slope_one, grad_two, act_two, grad_one, *totals = pl.pallas_call(
         lambda *refs: inner_kernel(rows, cols, *refs),
         out_shape=(
             jax.ShapeDtypeStruct((3, (rows - 2) * hid, cols), bf16),
@@ -778,49 +847,60 @@
             jax.ShapeDtypeStruct(((rows - 4) * hid, cols), bf16),
             jax.ShapeDtypeStruct(((rows - 6) * hid, cols), bf16),
             *accs,
+            state,
+            sums,
+            *strips(rows),
         ),
         in_specs=[vmem] * 7,
-        out_specs=(vmem,) * 8,
+        out_specs=(vmem,) * 13,
         scratch_shapes=[
             pltpu.VMEM((4, rows, width), f32),
             pltpu.VMEM((width // 128, rows * slot, 128), f32),
-            pltpu.VMEM((2, 3, rows * slot, cols), bf16),
         ],
         compiler_params=params,
         name="inner",
     )(wide, *maps)
-
-    keep, send, act_two_edge, grad_one_edge, *strips = pl.pallas_call(
+    *totals, state_in, sums_in, strip_a, strip_b, strip_c = totals
+    inner = (act_two, grad_one, strip_a, strip_b, strip_c)
+    short = jax.ShapeDtypeStruct((hid // 2, 12 * hid), bf16)
+    ends = jax.ShapeDtypeStruct((2, halo * hid, cols), bf16)
+    keep, send, *outer = pl.pallas_call(
         lambda *refs: outer_kernel(rows, cols, *refs),
-        out_shape=(
-            jax.ShapeDtypeStruct((hid // 2, 12 * hid), bf16),
-            jax.ShapeDtypeStruct((hid // 2, 12 * hid), bf16),
-            jax.ShapeDtypeStruct((2, halo * hid, cols), bf16),
-            jax.ShapeDtypeStruct((2, halo * hid, cols), bf16),
-            strip,
-            strip,
-            jax.ShapeDtypeStruct(strip.shape, f32),
-        ),
-        in_specs=[vmem] * 7 + [smem] + [vmem] * 7,
+        out_shape=(short, short, ends, ends, *strips(2 * edge)),
+        in_specs=[vmem] * 3 + [smem] * 2 + [vmem] * 15,
         out_specs=(vmem,) * 7,
         scratch_shapes=[
-            pltpu.VMEM((2, hid // 2, 12 * hid), bf16),
-            pltpu.VMEM((4, deep, width), f32),
-            pltpu.VMEM((width // 128, deep * slot, 128), f32),
-            pltpu.VMEM((2, 3, deep * slot, cols), bf16),
+            *(pltpu.VMEM(acc.shape, f32) for acc in accs),
+            pltpu.VMEM((2, *short.shape), bf16),
+            pltpu.VMEM((4, 2 * edge, width), f32),
+            pltpu.VMEM((width // 128, 2 * edge * slot, 128), f32),
+            pltpu.VMEM((2, 3, 2 * edge * slot, cols), bf16),
             pltpu.VMEM((2, 3, halo * hid, cols), bf16),
             pltpu.VMEM((2, halo * hid, cols), f32),
             pltpu.VMEM((2, 3, halo * hid, cols), bf16),
-            *(pltpu.VMEM(acc.shape, f32) for acc in accs),
         ],
         compiler_params=params,
         name="outer",
-    )(ext, *maps, core, act_one, slope_one, grad_two, grad_one_in, *totals)
+    )(
+        wide,
+        far,
+        near,
+        row_even,
+        core,
+        *maps,
+        act_one,
+        slope_one,
+        grad_two,
+        grad_one,
+        state_in,
+        *totals,
+        sums_in,
+    )
 
     new_velocity, grad_velocity = pl.pallas_call(
         lambda *refs: advance_kernel(rows, cols, *refs),
         out_shape=(jax.ShapeDtypeStruct(velocity.shape, f32),) * 2,
-        in_specs=[vmem] * 13,
+        in_specs=[vmem] * 3 + [smem] + [vmem] * 15,
         out_specs=(vmem,) * 2,
         scratch_shapes=[
             pltpu.VMEM((4, deep, width), f32),
@@ -829,7 +909,19 @@
         ],
         compiler_params=params,
         name="advance",
-    )(ext, forcing[None, :], w_head, b_head, w_in_t, act_two_in, act_two_edge, grad_one_in, grad_one_edge, *strips, w_mid_t)
+    )(
+        wide,
+        far,
+        near,
+        row_even,
+        forcing[None, :],
+        w_head,
+        b_head,
+        w_in_t,
+        w_mid_t,
+        *inner,
+        *outer,
+    )
 
     mine, other, (new_velocity, grad_velocity) = summed(
         keep, send, (new_velocity, grad_velocity)

time: 32.3 us -> 32 us (level)
  transfers between devices with their start and end apart: 10 -> 10, of which waited for: 7 -> 6; matrix products, arithmetic and copies ran while one was open for 0% -> 1% of each run, Pallas kernels for 21% -> 21%
where the time goes in v7:
time: 32 us; the launch traced here: 31.8 us
  starting transfers between devices  13.6 us (42%)
  Pallas kernels  10.8 us (34%)
  waiting for transfers between devices  6.33 us (20%)
  between operations  0.78 us (2%)
  other arithmetic  0.33 us (1%)
    ppermute x6, waiting for transfers between devices, swap(): return lax.ppermute(value, ('gx', 'gy'), pairs)  6.32 us
    ppermute x6, starting transfers between devices, swap(): return lax.ppermute(value, ('gx', 'gy'), pairs)  6.07 us
    ppermute x2, starting transfers between devices, met(): lax.ppermute(far, axis, far_pairs)  4.92 us
    pallas_call x1, Pallas kernels, per_device(): pl.pallas_call(lambda *refs: inner_kernel(rows, cols, *refs), out_shape=(...  2.94 us
    ppermute x2, starting transfers between devices, met(): lax.ppermute(near, axis, near_pairs)  2.58 us
    pallas_call x1, Pallas kernels, per_device(): pl.pallas_call(lambda *refs: advance_kernel(rows, cols, *refs), out_shape...  2.43 us
    pallas_call x1, Pallas kernels, per_device(): pl.pallas_call(lambda *refs: outer_kernel(rows, cols, *refs), out_shape=(...  2.2 us
    pallas_call x1, Pallas kernels, per_device(): pl.pallas_call(weights_kernel, out_shape=(jax.ShapeDtypeStruct((2 * hid,...  1.36 us
  transfers between devices with their start and end apart: 10, of which 6 were waited for; matrix products, arithmetic and copies ran while one was open for 1% of the time, Pallas kernels for 21%

profile of v7, /device:TPU:0, one launch (start us, length us, event | category | flops | bytes accessed | tf_op | source)
XLA Modules:
  0.0 31.8 jit_solution(1639025494875648394)
XLA Ops:
  0.6 0.9 %pack.1 = (f32[4,16,256]{2,1,0:T(8,128)S(1)}, bf16[4,16,4]{2,1,0:T(8,128)(2,1)S(1)}, bf16[4,16,4]{2,1,0:T(8,128)(2,1)S(1)}) custom-call(s32[1]{0:T(128)} %bitcast.even_ref, f32[2,16,256]{2,1,0:T(8,128)} %velocity_ref.1, f32[2,16,256]{2,1,0:T(8,128)} %cotangent_ref.1), custom_call_target="tpu_custom_call" | custom-call | tf_op jit(solution)/shard_map/pack/pallas_call | solution.py:807
  1.6 2.4 %collective-permute-start = (bf16[4,16,4]{2,1,0:T(8,128)(2,1)S(1)}, bf16[4,16,4]{2,1,0:T(8,128)(2,1)S(1)}, u32[]{:S(2)}, u32[]{:S(2)}) collective-permute-start(bf16[4,16,4]{2,1,0:T(8,128)(2,1)S(1)} %get-tuple-element.58), channel_id=1, source_target_pairs={{0,3},{1,2},{2,1},{3,0},{4,7},{5,6},{6,5},{7,4},{8,11},{9,10},{10,... | collective-permute-start | bytes 1544 | tf_op jit(solution)/shard_map/ppermute | solution.py:716
  4.0 0.7 %collective-permute-start.1 = (bf16[4,16,4]{2,1,0:T(8,128)(2,1)S(1)}, bf16[4,16,4]{2,1,0:T(8,128)(2,1)S(1)}, u32[]{:S(2)}, u32[]{:S(2)}) collective-permute-start(bf16[4,16,4]{2,1,0:T(8,128)(2,1)S(1)} %get-tuple-element.59), channel_id=1, source_target_pairs={{0,1},{1,0},{2,3},{3,2},{4,5},{5,4},{6,7},{7,6},{8,9},{9,8},{10,11... | collective-permute-start | bytes 1544 | tf_op jit(solution)/shard_map/ppermute | solution.py:716
  4.7 1.4 %weights.1 = (bf16[128,192]{1,0:T(8,128)(2,1)S(1)}, bf16[3,128,256]{2,1,0:T(8,128)(2,1)S(1)}, bf16[3,128,256]{2,1,0:T(8,128)(2,1)S(1)}, bf16[128,192]{1,0:T(8,12...) custom-call(bf16[9,2,64]{2,1,0:T(2,128)(2,1)} %bitcast.25, ...), custom_call_target="tpu_custom_call" | custom-call | tf_op jit(solution)/shard_map/weights/pallas_call | solution.py:769
  6.1 0.0 collective-permute-done
  6.1 0.0 collective-permute-done.1
  6.2 0.1 broadcast_select_fusion.2
  6.3 1.9 %collective-permute-start.3 = (bf16[4,4,264]{2,1,0:T(4,128)(2,1)S(1)}, bf16[4,4,264]{2,1,0:T(4,128)(2,1)S(1)}, u32[]{:S(2)}, u32[]{:S(2)}) collective-permute-start(bf16[4,4,264]{2,1,0:T(4,128)(2,1)S(1)} %get-tuple-element.67), channel_id=1, source_target_pairs={{0,4},{4,0},{8,12},{12,8},{1,5},{5,1},{9,13},{13,9},{2,6},{6,2},{1... | collective-permute-start | bytes 25352 | tf_op jit(solution)/shard_map/ppermute | solution.py:716
  8.2 2.5 %collective-permute-start.2 = (bf16[4,4,264]{2,1,0:T(4,128)(2,1)S(1)}, bf16[4,4,264]{2,1,0:T(4,128)(2,1)S(1)}, u32[]{:S(2)}, u32[]{:S(2)}) collective-permute-start(bf16[4,4,264]{2,1,0:T(4,128)(2,1)S(1)} %get-tuple-element.113), channel_id=1, source_target_pairs={{0,12},{4,8},{8,4},{12,0},{1,13},{5,9},{9,5},{13,1},{2,14},{6,10},... | collective-permute-start | bytes 25352 | tf_op jit(solution)/shard_map/ppermute | solution.py:716
  10.6 0.1 pad_maximum_fusion.refs_0_
  10.8 2.9 %inner.1 = (bf16[3,896,256]{2,1,0:T(8,128)(2,1)S(1)}, f32[896,256]{1,0:T(8,128)S(1)}, bf16[3,768,256]{2,1,0:T(8,128)(2,1)S(1)}, bf16[768,256]{1,0:T(8,128)(2,1)S...) custom-call(f32[4,16,264]{2,1,0:T(8,128)S(1)} %pad_maximum_fusion.re, ...), custom_call_target="tpu_custom_call" | custom-call | tf_op jit(solution)/shard_map/inner/pallas_call | solution.py:841
  13.7 0.0 collective-permute-done.3.refs_2_
  13.7 0.0 collective-permute-done.2.refs_1_
  13.7 2.2 %outer.1 = (bf16[32,768]{1,0:T(8,128)(2,1)S(1)}, bf16[32,768]{1,0:T(8,128)(2,1)S(1)}, bf16[2,256,256]{2,1,0:T(8,128)(2,1)S(1)}, bf16[2,256,256]{2,1,0:T(8,128)(2...) custom-call(f32[4,16,264]{2,1,0:T(8,128)S(1)} %pad_maximum_fusion.refs_0_, ...), custom_call_target="tpu_custom_call" | custom-call | tf_op jit(solution)/shard_map/outer/pallas_call | solution.py:867
  15.9 0.1 collective-permute-start.4
  16.0 1.2 %collective-permute-done.4 = bf16[32,768]{1,0:T(8,128)(2,1)S(1)} collective-permute-done((bf16[32,768]{1,0:T(8,128)(2,1)S(1)}, bf16[32,768]{1,0:T(8,128)(2,1)S(1)}, u32[]{:S(2)}, u32[]{:S(2)}) %collective-permute-start.4) | collective-permute-done | bytes 49184 | tf_op jit(solution)/shard_map/ppermute | solution.py:724
  17.2 1.6 %collective-permute-start.5 = (bf16[32,768]{1,0:T(8,128)(2,1)S(1)}, bf16[32,768]{1,0:T(8,128)(2,1)S(1)}, u32[]{:S(2)}, u32[]{:S(2)}) collective-permute-start(bf16[32,768]{1,0:T(8,128)(2,1)S(1)} %add_convert_fusion.2), channel_id=1, source_target_pairs={{0,2},{1,3},{2,0},{3,1},{4,6},{5,7},{6,4},{7,5},{8,10},{9,11},{10,... | collective-permute-start | bytes 147464 | tf_op jit(solution)/shard_map/ppermute | solution.py:724
  18.8 0.7 %collective-permute-start.6 = (bf16[32,768]{1,0:T(8,128)(2,1)S(1)}, bf16[32,768]{1,0:T(8,128)(2,1)S(1)}, u32[]{:S(2)}, u32[]{:S(2)}) collective-permute-start(bf16[32,768]{1,0:T(8,128)(2,1)S(1)} %add_convert_fusion.2), channel_id=1, source_target_pairs={{0,4},{1,5},{2,6},{3,7},{4,0},{5,1},{6,2},{7,3},{8,12},{9,13},{10,... | collective-permute-start | bytes 147464 | tf_op jit(solution)/shard_map/ppermute | solution.py:724
  19.5 1.3 %collective-permute-start.7 = (bf16[32,768]{1,0:T(8,128)(2,1)S(1)}, bf16[32,768]{1,0:T(8,128)(2,1)S(1)}, u32[]{:S(2)}, u32[]{:S(2)}) collective-permute-start(bf16[32,768]{1,0:T(8,128)(2,1)S(1)} %add_convert_fusion.2), channel_id=1, source_target_pairs={{0,6},{1,7},{2,4},{3,5},{4,2},{5,3},{6,0},{7,1},{8,14},{9,15},{10,... | collective-permute-start | bytes 147464 | tf_op jit(solution)/shard_map/ppermute | solution.py:724
  20.8 0.6 %collective-permute-done.5 = bf16[32,768]{1,0:T(8,128)(2,1)S(1)} collective-permute-done((bf16[32,768]{1,0:T(8,128)(2,1)S(1)}, bf16[32,768]{1,0:T(8,128)(2,1)S(1)}, u32[]{:S(2)}, u32[]{:S(2)}) %collective-permute-start.5) | collective-permute-done | bytes 49184 | tf_op jit(solution)/shard_map/ppermute | solution.py:724
  21.4 1.5 %collective-permute-done.6 = bf16[32,768]{1,0:T(8,128)(2,1)S(1)} collective-permute-done((bf16[32,768]{1,0:T(8,128)(2,1)S(1)}, bf16[32,768]{1,0:T(8,128)(2,1)S(1)}, u32[]{:S(2)}, u32[]{:S(2)}) %collective-permute-start.6) | collective-permute-done | bytes 49184 | tf_op jit(solution)/shard_map/ppermute | solution.py:724
  22.9 1.6 %collective-permute-done.7 = bf16[32,768]{1,0:T(8,128)(2,1)S(1)} collective-permute-done((bf16[32,768]{1,0:T(8,128)(2,1)S(1)}, bf16[32,768]{1,0:T(8,128)(2,1)S(1)}, u32[]{:S(2)}, u32[]{:S(2)}) %collective-permute-start.7) | collective-permute-done | bytes 49184 | tf_op jit(solution)/shard_map/ppermute | solution.py:724
  24.5 2.4 %collective-permute-start.8 = (bf16[32,768]{1,0:T(8,128)(2,1)S(1)}, bf16[32,768]{1,0:T(8,128)(2,1)S(1)}, u32[]{:S(2)}, u32[]{:S(2)}) collective-permute-start(bf16[32,768]{1,0:T(8,128)(2,1)S(1)} %add_convert_fusion.1), channel_id=1, source_target_pairs={{0,8},{1,9},{2,10},{3,11},{4,12},{5,13},{6,14},{7,15},{8,0},{9,1},... | collective-permute-start | bytes 147464 | tf_op jit(solution)/shard_map/ppermute | solution.py:724
  26.9 0.1 sine_multiply_fusion.refs_4_
  27.0 2.4 %advance.1 = (f32[2,16,256]{2,1,0:T(8,128)}, f32[2,16,256]{2,1,0:T(8,128)}) custom-call(f32[4,16,264]{2,1,0:T(8,128)S(1)} %pad_maximum_fusion.refs_0_, bf16[4,4,264]{2,1,0:T(4,128)(2,1)S(1)} %collective-permute-done.2.refs_1_, bf16[4,4,264]{2,1,0:T(4,128)(2,1)S(1)} %collective-permute-done.3.refs_2_, s32[1]{0:T(128)} %bitcast.9.refs_3_, ...), custom_call_target="tpu_custom_call" | custom-call | tf_op jit(solution)/shard_map/advance/pallas_call | solution.py:900
  29.4 0.2 collective-permute-done.8
  29.6 0.1 collective-permute-start.9
  29.7 1.2 %collective-permute-done.9.refs_1_ = bf16[32,768]{1,0:T(8,128)(2,1)S(1)} collective-permute-done((bf16[32,768]{1,0:T(8,128)(2,1)S(1)}, bf16[32,768]{1,0:T(8,128)(2,1)S(1)}, u32[]{:S(2)}, u32[]{:S(2)}) %collective-permute-start.9) | collective-permute-done | bytes 49184 | tf_op jit(solution)/shard_map/ppermute | solution.py:724
  30.9 0.9 %finish.1 = (f32[9,2,64]{2,1,0:T(2,128)}, f32[1,64]{1,0:T(1,128)}, f32[9,64,64]{2,1,0:T(8,128)}, f32[1,64]{1,0:T(1,128)}, f32[12,3,3,64]{3,2,1,0:T(4,128)}, /*index=5*/f32[1,12]{1,0:T(1,128)}) custom-call(bf16[32,768]{1,0:T(8,128)(2,1)S(1)} %add_convert_fusion.refs_0_, bf16[32,768]{1,0:T(8,128)(2,1)S(1)} %collective-permute-done.9.refs_1_, ...), custom_call_target="tpu_custom_call" | custom-call | tf_op jit(solution)/shard_map/finish/pallas_call | solution.py:929
  (7 shorter events, 0.1 us)
Async XLA Ops:
  1.6 4.5 %collective-permute-start = (bf16[4,16,4]{2,1,0:T(8,128)(2,1)S(1)}, bf16[4,16,4]{2,1,0:T(8,128)(2,1)S(1)}, u32[]{:S(2)}, u32[]{:S(2)}) collective-permute-start(bf16[4,16,4]{2,1,0:T(8,128)(2,1)S(1)} %get-tuple-element.58), channel_id=1, source_target_pairs={{0,3},{1,2},{2,1},{3,0},{4,7},{5,6},{6,5},{7,4},{8,11},{9,10},{10,... | collective-permute-start | bytes 1544 | tf_op jit(solution)/shard_map/ppermute | solution.py:716
  4.0 2.1 %collective-permute-start.1 = (bf16[4,16,4]{2,1,0:T(8,128)(2,1)S(1)}, bf16[4,16,4]{2,1,0:T(8,128)(2,1)S(1)}, u32[]{:S(2)}, u32[]{:S(2)}) collective-permute-start(bf16[4,16,4]{2,1,0:T(8,128)(2,1)S(1)} %get-tuple-element.59), channel_id=1, source_target_pairs={{0,1},{1,0},{2,3},{3,2},{4,5},{5,4},{6,7},{7,6},{8,9},{9,8},{10,11... | collective-permute-start | bytes 1544 | tf_op jit(solution)/shard_map/ppermute | solution.py:716
  6.3 7.4 %collective-permute-start.3 = (bf16[4,4,264]{2,1,0:T(4,128)(2,1)S(1)}, bf16[4,4,264]{2,1,0:T(4,128)(2,1)S(1)}, u32[]{:S(2)}, u32[]{:S(2)}) collective-permute-start(bf16[4,4,264]{2,1,0:T(4,128)(2,1)S(1)} %get-tuple-element.67), channel_id=1, source_target_pairs={{0,4},{4,0},{8,12},{12,8},{1,5},{5,1},{9,13},{13,9},{2,6},{6,2},{1... | collective-permute-start | bytes 25352 | tf_op jit(solution)/shard_map/ppermute | solution.py:716
  8.2 5.5 %collective-permute-start.2 = (bf16[4,4,264]{2,1,0:T(4,128)(2,1)S(1)}, bf16[4,4,264]{2,1,0:T(4,128)(2,1)S(1)}, u32[]{:S(2)}, u32[]{:S(2)}) collective-permute-start(bf16[4,4,264]{2,1,0:T(4,128)(2,1)S(1)} %get-tuple-element.113), channel_id=1, source_target_pairs={{0,12},{4,8},{8,4},{12,0},{1,13},{5,9},{9,5},{13,1},{2,14},{6,10},... | collective-permute-start | bytes 25352 | tf_op jit(solution)/shard_map/ppermute | solution.py:716
  15.9 1.3 %collective-permute-start.4 = (bf16[32,768]{1,0:T(8,128)(2,1)S(1)}, bf16[32,768]{1,0:T(8,128)(2,1)S(1)}, u32[]{:S(2)}, u32[]{:S(2)}) collective-permute-start(bf16[32,768]{1,0:T(8,128)(2,1)S(1)} %get-tuple-element.84), channel_id=1, source_target_pairs={{0,1},{1,0},{2,3},{3,2},{4,5},{5,4},{6,7},{7,6},{8,9},{9,8},{10,11... | collective-permute-start | bytes 147464 | tf_op jit(solution)/shard_map/ppermute | solution.py:724
  17.2 4.2 %collective-permute-start.5 = (bf16[32,768]{1,0:T(8,128)(2,1)S(1)}, bf16[32,768]{1,0:T(8,128)(2,1)S(1)}, u32[]{:S(2)}, u32[]{:S(2)}) collective-permute-start(bf16[32,768]{1,0:T(8,128)(2,1)S(1)} %add_convert_fusion.2), channel_id=1, source_target_pairs={{0,2},{1,3},{2,0},{3,1},{4,6},{5,7},{6,4},{7,5},{8,10},{9,11},{10,... | collective-permute-start | bytes 147464 | tf_op jit(solution)/shard_map/ppermute | solution.py:724
  18.8 4.1 %collective-permute-start.6 = (bf16[32,768]{1,0:T(8,128)(2,1)S(1)}, bf16[32,768]{1,0:T(8,128)(2,1)S(1)}, u32[]{:S(2)}, u32[]{:S(2)}) collective-permute-start(bf16[32,768]{1,0:T(8,128)(2,1)S(1)} %add_convert_fusion.2), channel_id=1, source_target_pairs={{0,4},{1,5},{2,6},{3,7},{4,0},{5,1},{6,2},{7,3},{8,12},{9,13},{10,... | collective-permute-start | bytes 147464 | tf_op jit(solution)/shard_map/ppermute | solution.py:724
  19.5 5.0 %collective-permute-start.7 = (bf16[32,768]{1,0:T(8,128)(2,1)S(1)}, bf16[32,768]{1,0:T(8,128)(2,1)S(1)}, u32[]{:S(2)}, u32[]{:S(2)}) collective-permute-start(bf16[32,768]{1,0:T(8,128)(2,1)S(1)} %add_convert_fusion.2), channel_id=1, source_target_pairs={{0,6},{1,7},{2,4},{3,5},{4,2},{5,3},{6,0},{7,1},{8,14},{9,15},{10,... | collective-permute-start | bytes 147464 | tf_op jit(solution)/shard_map/ppermute | solution.py:724
  24.5 5.1 %collective-permute-start.8 = (bf16[32,768]{1,0:T(8,128)(2,1)S(1)}, bf16[32,768]{1,0:T(8,128)(2,1)S(1)}, u32[]{:S(2)}, u32[]{:S(2)}) collective-permute-start(bf16[32,768]{1,0:T(8,128)(2,1)S(1)} %add_convert_fusion.1), channel_id=1, source_target_pairs={{0,8},{1,9},{2,10},{3,11},{4,12},{5,13},{6,14},{7,15},{8,0},{9,1},... | collective-permute-start | bytes 147464 | tf_op jit(solution)/shard_map/ppermute | solution.py:724
  29.6 1.3 %collective-permute-start.9 = (bf16[32,768]{1,0:T(8,128)(2,1)S(1)}, bf16[32,768]{1,0:T(8,128)(2,1)S(1)}, u32[]{:S(2)}, u32[]{:S(2)}) collective-permute-start(bf16[32,768]{1,0:T(8,128)(2,1)S(1)} %add_convert_fusion.refs_0_), channel_id=1, source_target_pairs={{0,1},{1,0},{2,3},{3,2},{4,5},{5,4},{6,7},{7,6},{8,9},{9,8},{10,11... | collective-permute-start | bytes 147464 | tf_op jit(solution)/shard_map/ppermute | solution.py:724

commit v8 on v7

--- a/solution.py
+++ b/solution.py
@@ -738,11 +738,12 @@
     while steps:
         if len(steps) >= 2 and steps[0][0] == 0 and steps[1][1] == 0:
             (_, cols), (rows, _) = steps[:2]
+            tied, keep = lax.optimization_barrier((half, keep))
             half = added(
                 half,
                 swap(half, 0, cols),
                 swap(half, rows, 0),
-                swap(half, rows, cols),
+                swap(tied, rows, cols),
             )
             steps = steps[2:]
         else:
@@ -813,6 +814,7 @@
         compiler_params=params,
         name="pack",
     )(even, in_hbm(velocity), in_hbm(cotangent))
+    near, even = lax.optimization_barrier((near, even))
     far, near = met(far, near, "gy")
     low, high = paired("gy", far, near)[0], paired("gy", near, far)[0]
     wide = jnp.concatenate([low.astype(f32), fields, high.astype(f32)], axis=2)
@@ -821,10 +823,11 @@
         for at in (slice(0, halo), slice(rows - halo, rows))
     )
     maps = (w_in, w_mid, w_mid_t, w_out_t, b_in, b_mid)
-    far, near = paired("gx", first, last)
-    near, maps = lax.optimization_barrier((near, maps))
-    far, near = met(far, near, "gx")
-    row_even = (lax.axis_index("gx") % 2 == 0).astype(jnp.int32).reshape(1)
+    count = lax.axis_size("gx")
+    last, maps = lax.optimization_barrier((last, maps))
+    far = lax.ppermute(last, "gx", [(i, (i + 1) % count) for i in range(count)])
+    near = lax.ppermute(first, "gx", [(i, (i - 1) % count) for i in range(count)])
+    row_even = jnp.ones((1,), jnp.int32)
 
     accs = (
         jax.ShapeDtypeStruct((3, 2 * hid, 4 * hid), f32),

time: 32 us -> 30.5 us (0.953)
  waiting for transfers between devices: 6.33 us -> 4.83 us
    ppermute x0 -> x2, starting transfers between devices: none -> 3.93 us  [the longest x1 2.12 us: per_device(): lax.ppermute(first, 'gx', [(i, (i - 1) % count) for i in range(count)])]
    ppermute x2 -> x1, starting transfers between devices: 4.92 us -> 2.61 us  [met(): lax.ppermute(far, axis, far_pairs)]
    ppermute x2 -> x1, starting transfers between devices: 2.58 us -> 0.52 us  [met(): lax.ppermute(near, axis, near_pairs)]
    ppermute x6, waiting for transfers between devices: 6.32 us -> 4.77 us  [swap(): return lax.ppermute(value, ('gx', 'gy'), pairs)]
    ppermute x6, starting transfers between devices: 6.07 us -> 6.48 us  [swap(): return lax.ppermute(value, ('gx', 'gy'), pairs)]
  transfers between devices with their start and end apart: 10 -> 10, of which waited for: 6 -> 5; matrix products, arithmetic and copies ran while one was open for 1% -> 1% of each run, Pallas kernels for 21% -> 22%
where the time goes in v8:
time: 30.5 us; the launch traced here: 30.3 us
  starting transfers between devices  13.5 us (44%)
  Pallas kernels  10.8 us (35%)
  waiting for transfers between devices  4.83 us (16%)
  between operations  0.76 us (2%)
  other arithmetic  0.4 us (1%)
    ppermute x6, starting transfers between devices, swap(): return lax.ppermute(value, ('gx', 'gy'), pairs)  6.48 us
    ppermute x6, waiting for transfers between devices, swap(): return lax.ppermute(value, ('gx', 'gy'), pairs)  4.77 us
    pallas_call x1, Pallas kernels, per_device(): pl.pallas_call(lambda *refs: inner_kernel(rows, cols, *refs), out_shape=(...  2.93 us
    ppermute x1, starting transfers between devices, met(): lax.ppermute(far, axis, far_pairs)  2.61 us
    pallas_call x1, Pallas kernels, per_device(): pl.pallas_call(lambda *refs: advance_kernel(rows, cols, *refs), out_shape...  2.43 us
    pallas_call x1, Pallas kernels, per_device(): pl.pallas_call(lambda *refs: outer_kernel(rows, cols, *refs), out_shape=(...  2.2 us
    ppermute x1, starting transfers between devices, per_device(): lax.ppermute(first, 'gx', [(i, (i - 1) % count) for i in range(count)])  2.12 us
    ppermute x1, starting transfers between devices, per_device(): far = lax.ppermute(last, 'gx', [(i, (i + 1) % count) for i in range(count)])  1.81 us
  transfers between devices with their start and end apart: 10, of which 5 were waited for; matrix products, arithmetic and copies ran while one was open for 1% of the time, Pallas kernels for 22%

profile of v8, /device:TPU:0, one launch (start us, length us, event | category | flops | bytes accessed | tf_op | source)
XLA Modules:
  0.0 30.3 jit_solution(5466575465171686839)
XLA Ops:
  0.6 0.9 %pack.1 = (f32[4,16,256]{2,1,0:T(8,128)S(1)}, bf16[4,16,4]{2,1,0:T(8,128)(2,1)S(1)}, bf16[4,16,4]{2,1,0:T(8,128)(2,1)S(1)}) custom-call(s32[1]{0:T(128)} %bitcast.even_ref, f32[2,16,256]{2,1,0:T(8,128)} %velocity_ref.1, f32[2,16,256]{2,1,0:T(8,128)} %cotangent_ref.1), custom_call_target="tpu_custom_call" | custom-call | tf_op jit(solution)/shard_map/pack/pallas_call | solution.py:808
  1.6 0.5 %collective-permute-start.1 = (bf16[4,16,4]{2,1,0:T(8,128)(2,1)S(1)}, bf16[4,16,4]{2,1,0:T(8,128)(2,1)S(1)}, u32[]{:S(2)}, u32[]{:S(2)}) collective-permute-start(bf16[4,16,4]{2,1,0:T(8,128)(2,1)S(1)} %get-tuple-element.62), channel_id=1, source_target_pairs={{0,1},{1,0},{2,3},{3,2},{4,5},{5,4},{6,7},{7,6},{8,9},{9,8},{10,11... | collective-permute-start | bytes 1544 | tf_op jit(solution)/shard_map/ppermute | solution.py:716
  2.1 2.6 %collective-permute-start = (bf16[4,16,4]{2,1,0:T(8,128)(2,1)S(1)}, bf16[4,16,4]{2,1,0:T(8,128)(2,1)S(1)}, u32[]{:S(2)}, u32[]{:S(2)}) collective-permute-start(bf16[4,16,4]{2,1,0:T(8,128)(2,1)S(1)} %get-tuple-element.60), channel_id=1, source_target_pairs={{0,3},{1,2},{2,1},{3,0},{4,7},{5,6},{6,5},{7,4},{8,11},{9,10},{10,... | collective-permute-start | bytes 1544 | tf_op jit(solution)/shard_map/ppermute | solution.py:716
  4.7 1.4 %weights.1 = (bf16[128,192]{1,0:T(8,128)(2,1)S(1)}, bf16[3,128,256]{2,1,0:T(8,128)(2,1)S(1)}, bf16[3,128,256]{2,1,0:T(8,128)(2,1)S(1)}, bf16[128,192]{1,0:T(8,12...) custom-call(bf16[9,2,64]{2,1,0:T(2,128)(2,1)} %bitcast.24, ...), custom_call_target="tpu_custom_call" | custom-call | tf_op jit(solution)/shard_map/weights/pallas_call | solution.py:770
  6.1 0.0 collective-permute-done.1
  6.1 0.0 collective-permute-done
  6.2 0.1 pad_maximum_fusion.1
  6.3 1.8 %collective-permute-start.2 = (bf16[4,4,264]{2,1,0:T(4,128)(2,1)S(1)}, bf16[4,4,264]{2,1,0:T(4,128)(2,1)S(1)}, u32[]{:S(2)}, u32[]{:S(2)}) collective-permute-start(bf16[4,4,264]{2,1,0:T(4,128)(2,1)S(1)} %pad_maximum_fusion.1), channel_id=1, source_target_pairs={{0,4},{4,8},{8,12},{12,0},{1,5},{5,9},{9,13},{13,1},{2,6},{6,10},{... | collective-permute-start | bytes 25352 | tf_op jit(solution)/shard_map/ppermute | solution.py:828
  8.1 0.1 pad_maximum_fusion.2
  8.2 2.1 %collective-permute-start.3 = (bf16[4,4,264]{2,1,0:T(4,128)(2,1)S(1)}, bf16[4,4,264]{2,1,0:T(4,128)(2,1)S(1)}, u32[]{:S(2)}, u32[]{:S(2)}) collective-permute-start(bf16[4,4,264]{2,1,0:T(4,128)(2,1)S(1)} %pad_maximum_fusion.2), channel_id=1, source_target_pairs={{0,12},{4,0},{8,4},{12,8},{1,13},{5,1},{9,5},{13,9},{2,14},{6,2},{... | collective-permute-start | bytes 25352 | tf_op jit(solution)/shard_map/ppermute | solution.py:829
  10.3 0.1 pad_maximum_fusion.refs_0_
  10.4 2.9 %inner.1 = (bf16[3,896,256]{2,1,0:T(8,128)(2,1)S(1)}, f32[896,256]{1,0:T(8,128)S(1)}, bf16[3,768,256]{2,1,0:T(8,128)(2,1)S(1)}, bf16[768,256]{1,0:T(8,128)(2,1)S...) custom-call(f32[4,16,264]{2,1,0:T(8,128)S(1)} %pad_maximum_fusion.re, ...), custom_call_target="tpu_custom_call" | custom-call | tf_op jit(solution)/shard_map/inner/pallas_call | solution.py:844
  13.3 0.0 collective-permute-done.2.refs_1_
  13.4 0.0 collective-permute-done.3.refs_2_
  13.4 2.2 %outer.1 = (bf16[32,768]{1,0:T(8,128)(2,1)S(1)}, bf16[32,768]{1,0:T(8,128)(2,1)S(1)}, bf16[2,256,256]{2,1,0:T(8,128)(2,1)S(1)}, bf16[2,256,256]{2,1,0:T(8,128)(2...) custom-call(f32[4,16,264]{2,1,0:T(8,128)S(1)} %pad_maximum_fusion.refs_0_, ...), custom_call_target="tpu_custom_call" | custom-call | tf_op jit(solution)/shard_map/outer/pallas_call | solution.py:870
  15.6 0.2 collective-permute-start.4
  15.8 1.1 %collective-permute-done.4 = bf16[32,768]{1,0:T(8,128)(2,1)S(1)} collective-permute-done((bf16[32,768]{1,0:T(8,128)(2,1)S(1)}, bf16[32,768]{1,0:T(8,128)(2,1)S(1)}, u32[]{:S(2)}, u32[]{:S(2)}) %collective-permute-start.4) | collective-permute-done | bytes 49184 | tf_op jit(solution)/shard_map/ppermute | solution.py:724
  16.9 1.1 %collective-permute-start.7 = (bf16[32,768]{1,0:T(8,128)(2,1)S(1)}, bf16[32,768]{1,0:T(8,128)(2,1)S(1)}, u32[]{:S(2)}, u32[]{:S(2)}) collective-permute-start(bf16[32,768]{1,0:T(8,128)(2,1)S(1)} %add_convert_fusion.2), channel_id=1, source_target_pairs={{0,6},{1,7},{2,4},{3,5},{4,2},{5,3},{6,0},{7,1},{8,14},{9,15},{10,... | collective-permute-start | bytes 147464 | tf_op jit(solution)/shard_map/ppermute | solution.py:724
  18.0 0.7 %collective-permute-start.5 = (bf16[32,768]{1,0:T(8,128)(2,1)S(1)}, bf16[32,768]{1,0:T(8,128)(2,1)S(1)}, u32[]{:S(2)}, u32[]{:S(2)}) collective-permute-start(bf16[32,768]{1,0:T(8,128)(2,1)S(1)} %add_convert_fusion.2), channel_id=1, source_target_pairs={{0,2},{1,3},{2,0},{3,1},{4,6},{5,7},{6,4},{7,5},{8,10},{9,11},{10,... | collective-permute-start | bytes 147464 | tf_op jit(solution)/shard_map/ppermute | solution.py:724
  18.7 1.7 %collective-permute-start.6 = (bf16[32,768]{1,0:T(8,128)(2,1)S(1)}, bf16[32,768]{1,0:T(8,128)(2,1)S(1)}, u32[]{:S(2)}, u32[]{:S(2)}) collective-permute-start(bf16[32,768]{1,0:T(8,128)(2,1)S(1)} %add_convert_fusion.2), channel_id=1, source_target_pairs={{0,4},{1,5},{2,6},{3,7},{4,0},{5,1},{6,2},{7,3},{8,12},{9,13},{10,... | collective-permute-start | bytes 147464 | tf_op jit(solution)/shard_map/ppermute | solution.py:724
  20.4 1.6 %collective-permute-done.7 = bf16[32,768]{1,0:T(8,128)(2,1)S(1)} collective-permute-done((bf16[32,768]{1,0:T(8,128)(2,1)S(1)}, bf16[32,768]{1,0:T(8,128)(2,1)S(1)}, u32[]{:S(2)}, u32[]{:S(2)}) %collective-permute-start.7) | collective-permute-done | bytes 49184 | tf_op jit(solution)/shard_map/ppermute | solution.py:724
  22.0 0.6 %collective-permute-done.5 = bf16[32,768]{1,0:T(8,128)(2,1)S(1)} collective-permute-done((bf16[32,768]{1,0:T(8,128)(2,1)S(1)}, bf16[32,768]{1,0:T(8,128)(2,1)S(1)}, u32[]{:S(2)}, u32[]{:S(2)}) %collective-permute-start.5) | collective-permute-done | bytes 49184 | tf_op jit(solution)/shard_map/ppermute | solution.py:724
  22.6 0.3 %collective-permute-done.6 = bf16[32,768]{1,0:T(8,128)(2,1)S(1)} collective-permute-done((bf16[32,768]{1,0:T(8,128)(2,1)S(1)}, bf16[32,768]{1,0:T(8,128)(2,1)S(1)}, u32[]{:S(2)}, u32[]{:S(2)}) %collective-permute-start.6) | collective-permute-done | bytes 49184 | tf_op jit(solution)/shard_map/ppermute | solution.py:724
  23.0 2.6 %collective-permute-start.8 = (bf16[32,768]{1,0:T(8,128)(2,1)S(1)}, bf16[32,768]{1,0:T(8,128)(2,1)S(1)}, u32[]{:S(2)}, u32[]{:S(2)}) collective-permute-start(bf16[32,768]{1,0:T(8,128)(2,1)S(1)} %add_convert_fusion.1), channel_id=1, source_target_pairs={{0,8},{1,9},{2,10},{3,11},{4,12},{5,13},{6,14},{7,15},{8,0},{9,1},... | collective-permute-start | bytes 147464 | tf_op jit(solution)/shard_map/ppermute | solution.py:724
  25.6 0.1 sine_multiply_fusion.refs_4_
  25.7 2.4 %advance.1 = (f32[2,16,256]{2,1,0:T(8,128)}, f32[2,16,256]{2,1,0:T(8,128)}) custom-call(f32[4,16,264]{2,1,0:T(8,128)S(1)} %pad_maximum_fusion.refs_0_, bf16[4,4,264]{2,1,0:T(4,128)(2,1)S(1)} %collective-permute-done.2.refs_1_, bf16[4,4,264]{2,1,0:T(4,128)(2,1)S(1)} %collective-permute-done.3.refs_2_, s32[1]{0:T(128)} %constant.33.clone.1.refs_3_, ...), custom_call_target="tpu_custom_call" | custom-call | tf_op jit(solution)/shard_map/advance/pallas_call | solution.py:903
  28.1 0.0 collective-permute-done.8
  28.1 0.1 collective-permute-start.9
  28.2 1.2 %collective-permute-done.9.refs_1_ = bf16[32,768]{1,0:T(8,128)(2,1)S(1)} collective-permute-done((bf16[32,768]{1,0:T(8,128)(2,1)S(1)}, bf16[32,768]{1,0:T(8,128)(2,1)S(1)}, u32[]{:S(2)}, u32[]{:S(2)}) %collective-permute-start.9) | collective-permute-done | bytes 49184 | tf_op jit(solution)/shard_map/ppermute | solution.py:724
  29.4 0.9 %finish.1 = (f32[9,2,64]{2,1,0:T(2,128)}, f32[1,64]{1,0:T(1,128)}, f32[9,64,64]{2,1,0:T(8,128)}, f32[1,64]{1,0:T(1,128)}, f32[12,3,3,64]{3,2,1,0:T(4,128)}, /*index=5*/f32[1,12]{1,0:T(1,128)}) custom-call(bf16[32,768]{1,0:T(8,128)(2,1)S(1)} %add_convert_fusion.refs_0_, bf16[32,768]{1,0:T(8,128)(2,1)S(1)} %collective-permute-done.9.refs_1_, ...), custom_call_target="tpu_custom_call" | custom-call | tf_op jit(solution)/shard_map/finish/pallas_call | solution.py:932
  (7 shorter events, 0.1 us)
Async XLA Ops:
  1.6 4.5 %collective-permute-start.1 = (bf16[4,16,4]{2,1,0:T(8,128)(2,1)S(1)}, bf16[4,16,4]{2,1,0:T(8,128)(2,1)S(1)}, u32[]{:S(2)}, u32[]{:S(2)}) collective-permute-start(bf16[4,16,4]{2,1,0:T(8,128)(2,1)S(1)} %get-tuple-element.62), channel_id=1, source_target_pairs={{0,1},{1,0},{2,3},{3,2},{4,5},{5,4},{6,7},{7,6},{8,9},{9,8},{10,11... | collective-permute-start | bytes 1544 | tf_op jit(solution)/shard_map/ppermute | solution.py:716
  2.1 4.1 %collective-permute-start = (bf16[4,16,4]{2,1,0:T(8,128)(2,1)S(1)}, bf16[4,16,4]{2,1,0:T(8,128)(2,1)S(1)}, u32[]{:S(2)}, u32[]{:S(2)}) collective-permute-start(bf16[4,16,4]{2,1,0:T(8,128)(2,1)S(1)} %get-tuple-element.60), channel_id=1, source_target_pairs={{0,3},{1,2},{2,1},{3,0},{4,7},{5,6},{6,5},{7,4},{8,11},{9,10},{10,... | collective-permute-start | bytes 1544 | tf_op jit(solution)/shard_map/ppermute | solution.py:716
  6.3 7.1 %collective-permute-start.2 = (bf16[4,4,264]{2,1,0:T(4,128)(2,1)S(1)}, bf16[4,4,264]{2,1,0:T(4,128)(2,1)S(1)}, u32[]{:S(2)}, u32[]{:S(2)}) collective-permute-start(bf16[4,4,264]{2,1,0:T(4,128)(2,1)S(1)} %pad_maximum_fusion.1), channel_id=1, source_target_pairs={{0,4},{4,8},{8,12},{12,0},{1,5},{5,9},{9,13},{13,1},{2,6},{6,10},{... | collective-permute-start | bytes 25352 | tf_op jit(solution)/shard_map/ppermute | solution.py:828
  8.2 5.2 %collective-permute-start.3 = (bf16[4,4,264]{2,1,0:T(4,128)(2,1)S(1)}, bf16[4,4,264]{2,1,0:T(4,128)(2,1)S(1)}, u32[]{:S(2)}, u32[]{:S(2)}) collective-permute-start(bf16[4,4,264]{2,1,0:T(4,128)(2,1)S(1)} %pad_maximum_fusion.2), channel_id=1, source_target_pairs={{0,12},{4,0},{8,4},{12,8},{1,13},{5,1},{9,5},{13,9},{2,14},{6,2},{... | collective-permute-start | bytes 25352 | tf_op jit(solution)/shard_map/ppermute | solution.py:829
  15.6 1.3 %collective-permute-start.4 = (bf16[32,768]{1,0:T(8,128)(2,1)S(1)}, bf16[32,768]{1,0:T(8,128)(2,1)S(1)}, u32[]{:S(2)}, u32[]{:S(2)}) collective-permute-start(bf16[32,768]{1,0:T(8,128)(2,1)S(1)} %get-tuple-element.87), channel_id=1, source_target_pairs={{0,1},{1,0},{2,3},{3,2},{4,5},{5,4},{6,7},{7,6},{8,9},{9,8},{10,11... | collective-permute-start | bytes 147464 | tf_op jit(solution)/shard_map/ppermute | solution.py:724
  16.9 5.1 %collective-permute-start.7 = (bf16[32,768]{1,0:T(8,128)(2,1)S(1)}, bf16[32,768]{1,0:T(8,128)(2,1)S(1)}, u32[]{:S(2)}, u32[]{:S(2)}) collective-permute-start(bf16[32,768]{1,0:T(8,128)(2,1)S(1)} %add_convert_fusion.2), channel_id=1, source_target_pairs={{0,6},{1,7},{2,4},{3,5},{4,2},{5,3},{6,0},{7,1},{8,14},{9,15},{10,... | collective-permute-start | bytes 147464 | tf_op jit(solution)/shard_map/ppermute | solution.py:724
  18.0 4.6 %collective-permute-start.5 = (bf16[32,768]{1,0:T(8,128)(2,1)S(1)}, bf16[32,768]{1,0:T(8,128)(2,1)S(1)}, u32[]{:S(2)}, u32[]{:S(2)}) collective-permute-start(bf16[32,768]{1,0:T(8,128)(2,1)S(1)} %add_convert_fusion.2), channel_id=1, source_target_pairs={{0,2},{1,3},{2,0},{3,1},{4,6},{5,7},{6,4},{7,5},{8,10},{9,11},{10,... | collective-permute-start | bytes 147464 | tf_op jit(solution)/shard_map/ppermute | solution.py:724
  18.7 4.2 %collective-permute-start.6 = (bf16[32,768]{1,0:T(8,128)(2,1)S(1)}, bf16[32,768]{1,0:T(8,128)(2,1)S(1)}, u32[]{:S(2)}, u32[]{:S(2)}) collective-permute-start(bf16[32,768]{1,0:T(8,128)(2,1)S(1)} %add_convert_fusion.2), channel_id=1, source_target_pairs={{0,4},{1,5},{2,6},{3,7},{4,0},{5,1},{6,2},{7,3},{8,12},{9,13},{10,... | collective-permute-start | bytes 147464 | tf_op jit(solution)/shard_map/ppermute | solution.py:724
  23.0 5.1 %collective-permute-start.8 = (bf16[32,768]{1,0:T(8,128)(2,1)S(1)}, bf16[32,768]{1,0:T(8,128)(2,1)S(1)}, u32[]{:S(2)}, u32[]{:S(2)}) collective-permute-start(bf16[32,768]{1,0:T(8,128)(2,1)S(1)} %add_convert_fusion.1), channel_id=1, source_target_pairs={{0,8},{1,9},{2,10},{3,11},{4,12},{5,13},{6,14},{7,15},{8,0},{9,1},... | collective-permute-start | bytes 147464 | tf_op jit(solution)/shard_map/ppermute | solution.py:724
  28.1 1.3 %collective-permute-start.9 = (bf16[32,768]{1,0:T(8,128)(2,1)S(1)}, bf16[32,768]{1,0:T(8,128)(2,1)S(1)}, u32[]{:S(2)}, u32[]{:S(2)}) collective-permute-start(bf16[32,768]{1,0:T(8,128)(2,1)S(1)} %add_convert_fusion.refs_0_), channel_id=1, source_target_pairs={{0,1},{1,0},{2,3},{3,2},{4,5},{5,4},{6,7},{7,6},{8,9},{9,8},{10,11... | collective-permute-start | bytes 147464 | tf_op jit(solution)/shard_map/ppermute | solution.py:724
